TPU v7x, 256 devices: a whole 4x4x8 slice. The times are simulated.
256 devices in a mesh: fsdp: 16 (over z, core), slab: 8 (over y, x_lo), rep: 2 (over x_hi).
Axes of the slice: x: 4 (x_hi: 2, x_lo: 2; x = x_hi * 2 + x_lo), y: 4, z: 8, core: 2. Of those that a mesh axis runs over, the one named last changes fastest.
Arguments:
- inputs: bfloat16 [32, 32, 8, 8, 256], P(('fsdp', 'rep'), 'slab'), may hold values from -6 to 6
- weights: bfloat16 [256, 27, 256], P('fsdp'), may hold values from -0.078125 to 0.078125
- upstream: bfloat16 [32, 32, 8, 8, 256], P(('fsdp', 'rep'), 'slab'), may hold values from -6 to 6
Outputs:
- activated: bfloat16 [32, 32, 8, 8, 256], P(('fsdp', 'rep'), 'slab')
- input_grad: bfloat16 [32, 32, 8, 8, 256], P(('fsdp', 'rep'), 'slab')
- weight_grad: float32 [256, 27, 256], P('fsdp')
All inputs are finite; a program needn't handle non-finite values.
Results may differ from a plain program's by a relative error of at most 0.0049.
Values may be sent and summed in bfloat16 or wider, within the bound.
No kernel may reach another device: no remote copies, remote signals or barrier semaphores. Data moves between devices by JAX's collectives and lax.ppermute only.
A program may use at most 256 MiB of HBM per device.

v0:
```python
import jax
import jax.numpy as jnp
from jax import lax
from jax.sharding import PartitionSpec as P


def padded_2(cells, sides, width):
    for axis, dim in sides:
        count = lax.axis_size(axis)
        ends = count - 1
        head = lax.slice_in_dim(cells, 0, width, axis=dim)
        tail = lax.slice_in_dim(cells, cells.shape[dim] - width, cells.shape[dim], axis=dim)
        cells = jnp.concatenate(
            [
                lax.ppermute(tail, axis, [(i, (i + 1) % count) for i in range(ends)]),
                cells,
                lax.ppermute(head, axis, [((i + 1) % count, i) for i in range(ends)]),
            ],
            axis=dim,
        )
    return cells


def silu_slope(preact):
    logistic = jax.nn.sigmoid(preact)
    return logistic * (1.0 + preact * (1.0 - logistic))


def pad_cross(field):
    return jnp.pad(field, ((0, 0), (0, 0), (1, 1), (1, 1), (0, 0)))


def grad_rim(field):
    return pad_cross(padded_2(field, (("slab", 1),), 1))


def tap_list():
    return [
        (along_x, along_y, along_z)
        for along_x in range(3)
        for along_y in range(3)
        for along_z in range(3)
    ]


def forward_rows(padded, weight_rows):
    planes = padded.shape[1] - 2
    height = padded.shape[2] - 2
    breadth = padded.shape[3] - 2
    total = None
    for index, (along_x, along_y, along_z) in enumerate(tap_list()):
        window = padded[
            :,
            along_x : along_x + planes,
            along_y : along_y + height,
            along_z : along_z + breadth,
            :,
        ]
        term = jnp.einsum(
            "bxyzi,oi->bxyzo", window, weight_rows[:, index, :], preferred_element_type=jnp.float32
        )
        total = term if total is None else total + term
    return total


def backward_rows(grads_pad, weight_rows):
    planes = grads_pad.shape[1] - 2
    height = grads_pad.shape[2] - 2
    breadth = grads_pad.shape[3] - 2
    total = None
    for index, (along_x, along_y, along_z) in enumerate(tap_list()):
        grad_window = grads_pad[
            :,
            2 - along_x : 2 - along_x + planes,
            2 - along_y : 2 - along_y + height,
            2 - along_z : 2 - along_z + breadth,
            :,
        ]
        term = jnp.einsum(
            "bxyzo,oi->bxyzi",
            grad_window,
            weight_rows[:, index, :],
            preferred_element_type=jnp.float32,
        )
        total = term if total is None else total + term
    return total


def weight_terms(grads, padded, factor):
    planes = grads.shape[1]
    height = grads.shape[2]
    breadth = grads.shape[3]
    stacked = []
    for along_x, along_y, along_z in tap_list():
        window = padded[
            :,
            along_x : along_x + planes,
            along_y : along_y + height,
            along_z : along_z + breadth,
            :,
        ]
        stacked.append(
            jnp.einsum("bxyzo,bxyzi->oi", grads, window, preferred_element_type=jnp.float32)
        )
    return jnp.stack(stacked, axis=1) * factor


def local(inputs, weights, upstream):
    samples = inputs.shape[0]
    planes = inputs.shape[1]
    height = inputs.shape[2]
    breadth = inputs.shape[3]
    total_cells = (
        samples
        * lax.axis_size("fsdp")
        * lax.axis_size("rep")
        * planes
        * lax.axis_size("slab")
        * height
        * breadth
    )
    factor = float(total_cells) ** (-0.5)
    inputs_halo = padded_2(inputs, (("slab", 1),), 1)
    inputs_pad = pad_cross(inputs_halo)
    whole = lax.all_gather(weights, "fsdp", axis=0, tiled=True)
    preact = forward_rows(inputs_pad, whole)
    activated = jax.nn.silu(preact).astype(jnp.bfloat16)
    grad_pre = (upstream.astype(jnp.float32) * silu_slope(preact)).astype(jnp.bfloat16)
    grads_pad = grad_rim(grad_pre)
    input_grad = backward_rows(grads_pad, whole).astype(jnp.bfloat16)
    terms = weight_terms(grad_pre, inputs_pad, factor)
    shard = lax.psum_scatter(terms, "fsdp", scatter_dimension=0, tiled=True)
    weight_grad = lax.psum(shard, ("slab", "rep"))
    return (activated, input_grad, weight_grad)


def solution(mesh):
    placed = (
        P(("fsdp", "rep"), "slab", None, None, None),
        P("fsdp", None, None),
        P(("fsdp", "rep"), "slab", None, None, None),
    )
    return jax.shard_map(
        local,
        mesh=mesh,
        in_specs=placed,
        out_specs=(
            P(("fsdp", "rep"), "slab", None, None, None),
            P(("fsdp", "rep"), "slab", None, None, None),
            P("fsdp", None, None),
        ),
        check_vma=False,
    )
```

profile of v0, /device:TPU:2, one launch (start us, length us, event | category | flops | bytes accessed | tf_op | source)
XLA Modules:
  0.0 247.2 jit_solution(10040391627877063961)
XLA Ops:
  8.7 3.4 %collective-permute-start = (bf16[1,1,8,8,256]{4,3,2,1,0:T(8,128)(2,1)S(1)}, bf16[1,1,8,8,256]{4,3,2,1,0:T(8,128)(2,1)S(1)}, u32[]{:S(2)}, u32[]{:S(2)}) collective-permute-start(bf16[1,1,8,8,256]{4,3,2,1,0:T(8,128)(2,1)S(1)} %get-tuple-element.5), channel_id=1, source_target_pairs={{0,2},{2,4},{4,6},{6,8},{8,10},{10,12},{12,14},{1,3},{3,5},{5,7},{... | collective-permute-start | bytes 98312 | tf_op jit(solution)/shard_map/ppermute | solution.py:15
  12.2 2.4 collective-permute-start.1
  14.6 4.3 %collective-permute-done.1 = bf16[1,1,8,8,256]{4,3,2,1,0:T(8,128)(2,1)S(1)} collective-permute-done((bf16[1,1,8,8,256]{4,3,2,1,0:T(8,128)(2,1)S(1)}, bf16[1,1,8,8,256]{4,3,2,1,0:T(8,128)(2,1)S(1)}, u32[]{:S(2)}, u32[]{:S(2)}) %collective-permute-start.1) | collective-permute-done | bytes 32800 | tf_op jit(solution)/shard_map/ppermute | solution.py:17
  20.0 34.4 %all-gather.2.cloned.1.call-done = bf16[256,27,256]{2,0,1:T(8,128)(2,1)} async-done(((bf16[16,27,256]{2,0,1:T(8,128)(2,1)}), bf16[256,27,256]{2,0,1:T(8,128)(2,1)}) %all-gather.2.cloned.1.call-update) | async-done | bytes 3538960 | tf_op jit(solution)/shard_map/all_gather | solution.py:125
  54.4 1.3 fusion.82
  55.7 1.1 fusion.81
  56.8 1.1 fusion.80
  57.9 1.1 convolution_add_fusion.47
  59.1 1.1 convolution_add_fusion.46
  60.2 1.1 convolution_add_fusion.45
  72.6 3.4 %broadcast_multiply_fusion = f32[256,27,256]{2,0,1:T(8,128)} fusion(f32[256,27,256]{2,0,1:T(8,128)S(1)} %fusion.4), kind=kLoop, calls=%fused_computation | loop fusion | flops 1769472 | bytes 14155776 | tf_op jit(solution)/shard_map/mul | solution.py:105
  76.0 3.6 %collective-permute-start.2 = (bf16[1,1,8,8,256]{4,3,2,1,0:T(8,128)(2,1)S(1)}, bf16[1,1,8,8,256]{4,3,2,1,0:T(8,128)(2,1)S(1)}, u32[]{:S(2)}, u32[]{:S(2)}) collective-permute-start(bf16[1,1,8,8,256]{4,3,2,1,0:T(8,128)(2,1)S(1)} %get-tuple-element.3), channel_id=1, source_target_pairs={{0,2},{2,4},{4,6},{6,8},{8,10},{10,12},{12,14},{1,3},{3,5},{5,7},{... | collective-permute-start | bytes 98312 | tf_op jit(solution)/shard_map/ppermute | solution.py:15
  79.7 2.5 collective-permute-start.3
  82.9 3.5 %collective-permute-done.3 = bf16[1,1,8,8,256]{4,3,2,1,0:T(8,128)(2,1)S(1)} collective-permute-done((bf16[1,1,8,8,256]{4,3,2,1,0:T(8,128)(2,1)S(1)}, bf16[1,1,8,8,256]{4,3,2,1,0:T(8,128)(2,1)S(1)}, u32[]{:S(2)}, u32[]{:S(2)}) %collective-permute-start.3) | collective-permute-done | bytes 32800 | tf_op jit(solution)/shard_map/ppermute | solution.py:17
  86.6 1.1 fusion.38
  87.7 1.1 fusion.42
  88.8 1.1 fusion.46
  89.9 1.1 convolution_add_fusion.23
  95.0 47.7 %reduce-scatter.2.cloned.1.call-done = f32[16,27,256]{2,0,1:T(8,128)} async-done(((f32[256,27,256]{2,0,1:T(8,128)}), f32[16,27,256]{2,0,1:T(8,128)}) %reduce-scatter.2.cloned.1.call-update) | async-done | bytes 442384 | tf_op jit(solution)/shard_map/reduce_scatter | solution.py:132
  142.7 1.1 convolution_add_fusion.2
  143.8 1.1 convolution_add_fusion.1
  144.9 1.8 fusion.32
  146.7 92.2 %all-reduce.4.cloned.1.call-done = f32[16,27,256]{2,0,1:T(8,128)} async-done(((f32[16,27,256]{2,0,1:T(8,128)}), f32[16,27,256]{2,0,1:T(8,128)}) %all-reduce.4.cloned.1.call-update) | async-done | bytes 442384 | tf_op jit(solution)/shard_map/psum | solution.py:133
  238.9 1.8 copy.87
  (89 shorter events, 18.4 us)
Async XLA Ops:
  7.2 54.2 %copy-start.2 = (bf16[1,4,8,8,256]{4,3,2,1,0:T(8,128)(2,1)S(1)}, bf16[1,4,8,8,256]{4,3,2,1,0:T(8,128)(2,1)}, u32[]{:S(2)}) copy-start(bf16[1,4,8,8,256]{4,3,2,1,0:T(8,128)(2,1)} %param.3) | copy-start | bytes 393220
  7.2 47.2 %all-gather.2.cloned.1.call-start = ((), (), s32[]{:S(2)}) async-start(), calls=%async_computation.1 | async-start | bytes 3760128 | tf_op jit(solution)/shard_map/all_gather | solution.py:125
  7.9 134.8 %reduce-scatter.2.cloned.1.call-start = ((), (), s32[]{:S(2)}) async-start(), calls=%async_computation.2 | async-start | bytes 7520256 | tf_op jit(solution)/shard_map/reduce_scatter | solution.py:132
  8.7 5.8 %collective-permute-start = (bf16[1,1,8,8,256]{4,3,2,1,0:T(8,128)(2,1)S(1)}, bf16[1,1,8,8,256]{4,3,2,1,0:T(8,128)(2,1)S(1)}, u32[]{:S(2)}, u32[]{:S(2)}) collective-permute-start(bf16[1,1,8,8,256]{4,3,2,1,0:T(8,128)(2,1)S(1)} %get-tuple-element.5), channel_id=1, source_target_pairs={{0,2},{2,4},{4,6},{6,8},{8,10},{10,12},{12,14},{1,3},{3,5},{5,7},{... | collective-permute-start | bytes 98312 | tf_op jit(solution)/shard_map/ppermute | solution.py:15
  12.2 6.7 %collective-permute-start.1 = (bf16[1,1,8,8,256]{4,3,2,1,0:T(8,128)(2,1)S(1)}, bf16[1,1,8,8,256]{4,3,2,1,0:T(8,128)(2,1)S(1)}, u32[]{:S(2)}, u32[]{:S(2)}) collective-permute-start(bf16[1,1,8,8,256]{4,3,2,1,0:T(8,128)(2,1)S(1)} %get-tuple-element.6), channel_id=1, source_target_pairs={{2,0},{4,2},{6,4},{8,6},{10,8},{12,10},{14,12},{3,1},{5,3},{7,5},{... | collective-permute-start | bytes 98312 | tf_op jit(solution)/shard_map/ppermute | solution.py:17
  54.4 7.0 %copy-start = (bf16[256,27,256]{2,0,1:T(8,128)(2,1)S(1)}, bf16[256,27,256]{2,0,1:T(8,128)(2,1)}, u32[]{:S(2)}) copy-start(bf16[256,27,256]{2,0,1:T(8,128)(2,1)} %all-gather.2.cloned.1.call-done) | copy-start | bytes 10616836
  63.9 2.1 copy-start.3
  76.0 163.0 %all-reduce.4.cloned.1.call-start = ((), (), s32[]{:S(2)}) async-start(), calls=%async_computation.3 | async-start | bytes 884736 | tf_op jit(solution)/shard_map/psum | solution.py:133
  76.0 15.0 %copy-start.1 = (bf16[256,27,256]{2,0,1:T(8,128)(2,1)S(1)}, bf16[256,27,256]{2,0,1:T(8,128)(2,1)}, u32[]{:S(2)}) copy-start(bf16[256,27,256]{2,0,1:T(8,128)(2,1)} %all-gather.2.cloned.1.call-done) | copy-start | bytes 10616836
  76.0 6.9 %collective-permute-start.2 = (bf16[1,1,8,8,256]{4,3,2,1,0:T(8,128)(2,1)S(1)}, bf16[1,1,8,8,256]{4,3,2,1,0:T(8,128)(2,1)S(1)}, u32[]{:S(2)}, u32[]{:S(2)}) collective-permute-start(bf16[1,1,8,8,256]{4,3,2,1,0:T(8,128)(2,1)S(1)} %get-tuple-element.3), channel_id=1, source_target_pairs={{0,2},{2,4},{4,6},{6,8},{8,10},{10,12},{12,14},{1,3},{3,5},{5,7},{... | collective-permute-start | bytes 98312 | tf_op jit(solution)/shard_map/ppermute | solution.py:15
  79.7 6.7 %collective-permute-start.3 = (bf16[1,1,8,8,256]{4,3,2,1,0:T(8,128)(2,1)S(1)}, bf16[1,1,8,8,256]{4,3,2,1,0:T(8,128)(2,1)S(1)}, u32[]{:S(2)}, u32[]{:S(2)}) collective-permute-start(bf16[1,1,8,8,256]{4,3,2,1,0:T(8,128)(2,1)S(1)} %get-tuple-element.4), channel_id=1, source_target_pairs={{2,0},{4,2},{6,4},{8,6},{10,8},{12,10},{14,12},{3,1},{5,3},{7,5},{... | collective-permute-start | bytes 98312 | tf_op jit(solution)/shard_map/ppermute | solution.py:17
Sparse Core Ops, SparseCore 0:
  9.9 44.4 all-gather.1
  76.1 66.5 reduce-scatter.1
  146.3 92.5 all-reduce.3
where the time goes:
time: 248 us; the launch traced here: 247 us
  waiting for transfers between devices  183 us (74%)
  matrix products  29.9 us (12%)
  between operations  14.4 us (6%)
  starting transfers between devices  12 us (5%)
  other arithmetic  5.36 us (2%)
  local copies, waits for them, and re-layouts  2.61 us (1%)
    psum x1, waiting for transfers between devices, local(): weight_grad = lax.psum(shard, ('slab', 'rep'))  92.2 us
    reduce_scatter x1, waiting for transfers between devices, local(): shard = lax.psum_scatter(terms, 'fsdp', scatter_dimension=0, tiled=True)  47.7 us
    all_gather x1, waiting for transfers between devices, local(): whole = lax.all_gather(weights, 'fsdp', axis=0, tiled=True)  34.4 us
    dot_general x27, matrix products, backward_rows(): jnp.einsum('bxyzo,oi->bxyzi', grad_window, weight_rows[:, index, :], pref...  12.1 us
    dot_general x27, matrix products, forward_rows(): jnp.einsum('bxyzi,oi->bxyzo', window, weight_rows[:, index, :], preferred...  11.7 us
    ppermute x2, waiting for transfers between devices, padded_2(): lax.ppermute(head, axis, [((i + 1) % count, i) for i in range(ends)])  7.81 us
    ppermute x2, starting transfers between devices, padded_2(): lax.ppermute(tail, axis, [(i, (i + 1) % count) for i in range(ends)])  7.09 us
    dot_general x27, matrix products, weight_terms(): jnp.einsum('bxyzo,bxyzi->oi', grads, window, preferred_element_type=jnp.f...  6.1 us
  transfers between devices with their start and end apart: 7, of which 5 were waited for; matrix products, arithmetic and copies ran while one was open for 6% of the time, Pallas kernels for 0%

commit v1 on v0

v1 whole, which is shorter than its diff:
```python
import functools

import jax
import jax.numpy as jnp
from jax import lax
from jax.experimental import pallas as pl
from jax.experimental.pallas import tpu as pltpu
from jax.sharding import PartitionSpec as P

F32 = jnp.float32
BF16 = jnp.bfloat16
CELLS = 256
LANES = 128
SLABS = 8
OUTS = 32
TAPS = 27
ROWS = 28 * OUTS
WHOLE = SLABS * CELLS
COLUMNS = WHOLE // LANES


def tap_index(along_x, along_y, along_z):
    return (along_x * 3 + along_y) * 3 + along_z


def pack_kernel(x_ref, u_ref, out_ref):
    turned = jnp.transpose(u_ref[...].astype(F32)).astype(BF16)
    for slab in range(SLABS):
        out_ref[slab, :CELLS, :] = x_ref[...]
        out_ref[slab, CELLS:, :] = turned[slab * OUTS : (slab + 1) * OUTS]


def lane_masks():
    lane = lax.broadcasted_iota(jnp.int32, (16, LANES), 1)
    row = (lane >> 3) & 7
    col = lane & 7
    return lane < 64, row, col


def inside(coordinate, shift):
    moved = coordinate + shift
    return (moved >= 0) & (moved < 8)


def turn(block, shift):
    return pltpu.roll(block, shift % LANES, 1)


def main_kernel(core_ref, r_ref, w_ref, act_ref, own_ref, other_ref, g_ref, w2_ref, z_ref):
    for tap in range(TAPS):
        for core in range(2):
            w2_ref[tap * OUTS + core * 16 : tap * OUTS + core * 16 + 16, :] = w_ref[
                (tap // 4) * 2 + core, (tap % 4) * 16 : (tap % 4) * 16 + 16, :
            ]
    w2_ref[TAPS * OUTS :, :] = jnp.zeros((OUTS, CELLS), BF16)
    g_ref[TAPS * OUTS :, :] = jnp.zeros((OUTS, WHOLE), BF16)
    taps_by_outs = w2_ref[: TAPS * OUTS, :]
    for slab in range(SLABS):
        z_ref[:, slab * CELLS : (slab + 1) * CELLS] = lax.dot_general(
            taps_by_outs,
            r_ref[slab, :CELLS, :],
            (((1,), (1,)), ((), ())),
            preferred_element_type=F32,
        )
    low, row, col = lane_masks()
    zero = jnp.zeros((16, LANES), F32)
    for group in range(2):

        def term(along_x, along_y, along_z, column):
            if column < 0 or column >= COLUMNS:
                return zero
            start = tap_index(along_x, along_y, along_z) * OUTS + group * 16
            return z_ref[start : start + 16, column * LANES : (column + 1) * LANES]

        grads = []
        for column in range(COLUMNS):
            total = None
            for c in range(3):
                over_y = None
                for b in range(3):
                    mixed = jnp.where(
                        low,
                        term(2, b, c, column + 1) + term(0, b, c, column),
                        term(2, b, c, column) + term(0, b, c, column - 1),
                    )
                    over_x = term(1, b, c, column) + turn(mixed, 64)
                    if b != 1:
                        over_x = jnp.where(inside(row, b - 1), turn(over_x, -8 * (b - 1)), 0.0)
                    over_y = over_x if over_y is None else over_y + over_x
                if c != 1:
                    over_y = jnp.where(inside(col, c - 1), turn(over_y, -(c - 1)), 0.0)
                total = over_y if total is None else total + over_y
            slab, part = column // 2, column % 2
            lanes = slice(part * LANES, (part + 1) * LANES)
            outs = slice(group * 16, group * 16 + 16)
            logistic = 1.0 / (1.0 + jnp.exp(-total))
            act_ref[slab, outs, lanes] = (total * logistic).astype(BF16)
            upstream = r_ref[
                slab, CELLS + group * 16 : CELLS + group * 16 + 16, lanes
            ].astype(F32)
            grad = upstream * (logistic * (1.0 + total * (1.0 - logistic)))
            grads.append(grad.astype(BF16).astype(F32))
        for c in range(3):
            if c == 1:
                by_z = grads
            else:
                by_z = [jnp.where(inside(col, 1 - c), turn(g, c - 1), 0.0) for g in grads]
            for b in range(3):
                if b == 1:
                    by_y = by_z
                else:
                    by_y = [
                        jnp.where(inside(row, 1 - b), turn(g, 8 * (b - 1)), 0.0) for g in by_z
                    ]
                swapped = [zero] + [turn(g, 64) for g in by_y] + [zero]
                for column in range(COLUMNS):
                    lanes = slice(column * LANES, (column + 1) * LANES)
                    here = swapped[column + 1]
                    for a, value in (
                        (0, jnp.where(low, here, swapped[column + 2])),
                        (1, by_y[column]),
                        (2, jnp.where(low, swapped[column], here)),
                    ):
                        start = tap_index(a, b, c) * OUTS + group * 16
                        g_ref[start : start + 16, lanes] = value.astype(BF16)
    whole = jnp.dot(
        g_ref[: TAPS * OUTS, :],
        r_ref[:, :CELLS, :].reshape(WHOLE, CELLS),
        preferred_element_type=F32,
    )
    first = core_ref[0] == 0
    for tap in range(TAPS):
        start = tap * OUTS
        left = whole[start : start + 16]
        right = whole[start + 16 : start + 32]
        own_ref[tap * 16 : tap * 16 + 16, :] = jnp.where(first, left, right)
        other_ref[tap * 16 : tap * 16 + 16, :] = jnp.where(first, right, left).astype(
            other_ref.dtype
        )
    own_ref[TAPS * 16 :, :] = jnp.zeros((5 * 16, CELLS), own_ref.dtype)
    other_ref[TAPS * 16 :, :] = jnp.zeros((5 * 16, CELLS), other_ref.dtype)


def input_kernel(g_ref, w2_ref, act_ref, out_ref):
    turned = jnp.transpose(w2_ref[...].astype(F32)).astype(BF16)
    for slab in range(SLABS):
        out_ref[slab, :CELLS, :] = jnp.dot(
            turned, g_ref[:, slab * CELLS : (slab + 1) * CELLS], preferred_element_type=F32
        ).astype(BF16)
        out_ref[slab, CELLS:, :] = act_ref[slab]


def final_kernel(r_ref, act_ref, grad_ref):
    total = r_ref[0, :CELLS, :].astype(F32)
    for slab in range(1, SLABS):
        total = total + r_ref[slab, :CELLS, :].astype(F32)
    grad_ref[...] = jnp.transpose(total).astype(BF16)
    act_ref[...] = jnp.transpose(r_ref[:, CELLS:, :].astype(F32).reshape(CELLS, CELLS)).astype(BF16)


VMEM = pl.BlockSpec(memory_space=pltpu.VMEM)
SMEM = pl.BlockSpec(memory_space=pltpu.SMEM)
PARAMS = pltpu.CompilerParams(vmem_limit_bytes=48 * 1024 * 1024)


def shape(*dims, dtype=BF16):
    return jax.ShapeDtypeStruct(dims, dtype)


def call(kernel, outs, operands, specs=None, scratch=(), flops=0):
    moved = sum(a.size * a.dtype.itemsize for a in list(operands) + list(outs))
    return pl.pallas_call(
        kernel,
        out_shape=tuple(outs),
        in_specs=specs or [VMEM] * len(operands),
        out_specs=tuple(VMEM for _ in outs),
        scratch_shapes=list(scratch),
        compiler_params=PARAMS,
        cost_estimate=pl.CostEstimate(flops=flops, bytes_accessed=moved, transcendentals=0),
    )(*operands)


def repeated(block, count):
    return jnp.broadcast_to(block[None], (count,) + block.shape)


def local(inputs, weights, upstream):
    owner = lax.axis_index("fsdp")
    slab = lax.axis_index("slab")
    chips = lax.axis_size("fsdp") // 2
    reps = lax.axis_size("rep")
    total_cells = 2 * chips * reps * WHOLE
    factor = float(total_cells) ** (-0.5)

    def place(z, core, y, rep):
        return ((z * 2 + core) * SLABS + y) * reps + rep

    everyone = ("fsdp", "slab", "rep")
    crossed = [
        (place(z, core, y, rep), place(y, core, z, rep))
        for z in range(chips)
        for core in range(2)
        for y in range(SLABS)
        for rep in range(reps)
    ]
    cores = [(2 * z + core, 2 * z + 1 - core) for z in range(chips) for core in range(2)]
    columns = [[2 * z + core for z in range(chips)] for core in range(2)]

    by_tap = jnp.pad(jnp.transpose(weights, (1, 0, 2)), ((0, 5), (0, 0), (0, 0)))
    piece = lax.dynamic_slice_in_dim(by_tap, slab * 4, 4, axis=0).reshape(64, CELLS)
    piece = lax.ppermute(piece, everyone, crossed)
    pieces = lax.all_to_all(repeated(piece, 2 * chips), "fsdp", 0, 0)

    cells = inputs.reshape(CELLS, CELLS)
    packed = call(
        pack_kernel,
        [shape(SLABS, CELLS + OUTS, CELLS)],
        (cells, upstream.reshape(CELLS, CELLS)),
    )[0]
    gathered = lax.all_to_all(packed, "slab", 0, 0)

    core = (owner % 2).astype(jnp.int32).reshape(1)
    act, own, other, grads, kernel_rows = call(
        main_kernel,
        [
            shape(SLABS, OUTS, CELLS),
            shape(512, CELLS, dtype=F32),
            shape(512, CELLS, dtype=F32),
            shape(ROWS, WHOLE),
            shape(ROWS, CELLS),
        ],
        (core, gathered, pieces),
        specs=[SMEM, VMEM, VMEM],
        scratch=[pltpu.VMEM((TAPS * OUTS, WHOLE), F32)],
        flops=4 * ROWS * WHOLE * CELLS,
    )
    own = own + lax.ppermute(other, "fsdp", cores)
    sums = lax.all_to_all(
        own.astype(BF16).reshape(chips, 64, CELLS), "fsdp", 0, 0, axis_index_groups=columns
    )
    sums = jnp.sum(sums.astype(F32), axis=0).astype(BF16)

    terms = call(
        input_kernel,
        [shape(SLABS, CELLS + OUTS, CELLS)],
        (grads, kernel_rows, act),
        flops=2 * ROWS * WHOLE * CELLS,
    )[0]
    returned = lax.all_to_all(terms, "slab", 0, 0)
    activated, input_grad = call(
        final_kernel, [shape(CELLS, CELLS), shape(CELLS, CELLS)], (returned,)
    )

    sums = lax.ppermute(sums, everyone, crossed)
    parts = lax.all_to_all(repeated(sums, SLABS * reps), ("slab", "rep"), 0, 0)
    parts = jnp.sum(parts.reshape(SLABS, reps, 64, CELLS).astype(F32), axis=1)
    weight_grad = jnp.transpose(parts.reshape(32, 16, CELLS)[:TAPS], (1, 0, 2)) * factor
    return (
        activated.reshape(inputs.shape),
        input_grad.reshape(inputs.shape),
        weight_grad,
    )


def solution(mesh):
    placed = (
        P(("fsdp", "rep"), "slab", None, None, None),
        P("fsdp", None, None),
        P(("fsdp", "rep"), "slab", None, None, None),
    )
    return jax.shard_map(
        local,
        mesh=mesh,
        in_specs=placed,
        out_specs=(
            P(("fsdp", "rep"), "slab", None, None, None),
            P(("fsdp", "rep"), "slab", None, None, None),
            P("fsdp", None, None),
        ),
        check_vma=False,
    )
```

time: 248 us -> 123 us (0.50)
  waiting for transfers between devices: 183 us -> 66.2 us
  matrix products: 29.9 us -> 0 us
  starting transfers between devices: 12 us -> 38.7 us
  between operations: 14.4 us -> 0.72 us
  Pallas kernels: 0 us -> 10.3 us
  other arithmetic: 5.36 us -> 1.67 us
    psum x1 -> x0, waiting for transfers between devices: 92.2 us -> none  [local(): weight_grad = lax.psum(shard, ('slab', 'rep'))]
    all_to_all x0 -> x5, waiting for transfers between devices: none -> 56.7 us  [the longest x1 16.7 us: local(): gathered = lax.all_to_all(packed, 'slab', 0, 0)]
    reduce_scatter x1 -> x0, waiting for transfers between devices: 47.7 us -> none  [local(): shard = lax.psum_scatter(terms, 'fsdp', scatter_dimension=0, tiled=True)]
    all_gather x1 -> x0, waiting for transfers between devices: 34.4 us -> none  [local(): whole = lax.all_gather(weights, 'fsdp', axis=0, tiled=True)]
    all_to_all x0 -> x5, starting transfers between devices: none -> 32.4 us  [the longest x1 14.1 us: local(): pieces = lax.all_to_all(repeated(piece, 2 * chips), 'fsdp', 0, 0)]
    dot_general x81 -> x0, matrix products: 29.9 us -> none  [the longest x27 12.1 us: backward_rows(): jnp.einsum('bxyzo,oi->bxyzi', grad_window, weight_rows[:, index, :], pref...]
    pallas_call x0 -> x4, Pallas kernels: none -> 10.3 us  [call(): pl.pallas_call(kernel, out_shape=tuple(outs), in_specs=specs or [VMEM] *...]
    ppermute x4 -> x3, starting transfers between devices: 11.9 us -> 6.34 us  [the longest x1 3.79 us: local(): piece = lax.ppermute(piece, everyone, crossed)]
  transfers between devices with their start and end apart: 7 -> 8, of which waited for: 5 -> 8; matrix products, arithmetic and copies ran while one was open for 6% -> 0% of each run, Pallas kernels for 0% -> 4%
where the time goes in v1:
time: 123 us; the launch traced here: 122 us
  waiting for transfers between devices  66.2 us (54%)
  starting transfers between devices  38.7 us (31%)
  Pallas kernels  10.3 us (8%)
  local copies, waits for them, and re-layouts  4.59 us (4%)
  other arithmetic  1.67 us (1%)
    all_to_all x1, waiting for transfers between devices, local(): gathered = lax.all_to_all(packed, 'slab', 0, 0)  16.7 us
    all_to_all x1, waiting for transfers between devices, local(): pieces = lax.all_to_all(repeated(piece, 2 * chips), 'fsdp', 0, 0)  14.9 us
    all_to_all x1, starting transfers between devices, local(): pieces = lax.all_to_all(repeated(piece, 2 * chips), 'fsdp', 0, 0)  14.1 us
    pallas_call x4, Pallas kernels, call(): pl.pallas_call(kernel, out_shape=tuple(outs), in_specs=specs or [VMEM] *...  10.3 us
    all_to_all x1, waiting for transfers between devices, local(): returned = lax.all_to_all(terms, 'slab', 0, 0)  9.19 us
    all_to_all x1, waiting for transfers between devices, local(): parts = lax.all_to_all(repeated(sums, SLABS * reps), ('slab', 'rep'), 0, 0)  8.14 us
    all_to_all x1, waiting for transfers between devices, local(): lax.all_to_all(own.astype(BF16).reshape(chips, 64, CELLS), 'fsdp', 0, 0,...  7.86 us
    all_to_all x1, starting transfers between devices, local(): parts = lax.all_to_all(repeated(sums, SLABS * reps), ('slab', 'rep'), 0, 0)  6.12 us
  transfers between devices with their start and end apart: 8, of which 8 were waited for; matrix products, arithmetic and copies ran while one was open for 0% of the time, Pallas kernels for 4%

profile of v1, /device:TPU:2, one launch (start us, length us, event | category | flops | bytes accessed | tf_op | source)
XLA Modules:
  0.0 122.1 jit_solution(11778142970178882461)
XLA Ops:
  0.7 0.8 pad_dynamic-slice_fusion
  1.5 3.8 %collective-permute-start = (bf16[64,256]{1,0:T(8,128)(2,1)S(1)}, bf16[64,256]{1,0:T(8,128)(2,1)S(1)}, u32[]{:S(2)}, u32[]{:S(2)}) collective-permute-start(bf16[64,256]{1,0:T(8,128)(2,1)S(1)} %bitcast.18), channel_id=1, source_target_pairs={{0,0},{1,1},{2,32},{3,33},{4,64},{5,65},{6,96},{7,97},{8,128},{9,1... | collective-permute-start | bytes 98312 | tf_op jit(solution)/shard_map/ppermute | solution.py:211
  5.3 3.1 %collective-permute-done = bf16[64,256]{1,0:T(8,128)(2,1)S(1)} collective-permute-done((bf16[64,256]{1,0:T(8,128)(2,1)S(1)}, bf16[64,256]{1,0:T(8,128)(2,1)S(1)}, u32[]{:S(2)}, u32[]{:S(2)}) %collective-permute-start) | collective-permute-done | bytes 32800 | tf_op jit(solution)/shard_map/ppermute | solution.py:211
  8.4 0.9 broadcast_in_dim.4
  9.2 14.1 %all-to-all-start.1 = ((bf16[16,64,256]{2,1,0:T(8,128)(2,1)}), bf16[16,64,256]{2,1,0:T(8,128)(2,1)S(1)}, u32[]{:S(2)}, u32[]{:S(2)}) async-start(bf16[16,64,256]{2,1,0:T(8,128)(2,1)} %broadcast_in_dim.4), calls=%async_computation.1 | async-start | bytes 1048576 | tf_op jit(solution)/shard_map/all_to_all | solution.py:212
  23.4 1.1 shard_map.58
  24.5 14.9 %all-to-all-done.1.w_ref = bf16[16,64,256]{2,1,0:T(8,128)(2,1)S(1)} async-done(((bf16[16,64,256]{2,1,0:T(8,128)(2,1)}), bf16[16,64,256]{2,1,0:T(8,128)(2,1)S(1)}, u32[]{:S(2)}, u32[]{:S(2)}) %all-to-all-start.1) | async-done | bytes 524320 | tf_op jit(solution)/shard_map/all_to_all | solution.py:212
  39.4 3.7 %all-to-all-start = ((bf16[8,288,256]{2,1,0:T(8,128)(2,1)}), bf16[8,288,256]{2,1,0:T(8,128)(2,1)S(1)}, u32[]{:S(2)}, u32[]{:S(2)}) async-start(bf16[8,288,256]{2,1,0:T(8,128)(2,1)} %shard_map.58), calls=%async_computation | async-start | bytes 2359296 | tf_op jit(solution)/shard_map/all_to_all | solution.py:220
  43.1 16.7 %all-to-all-done.r_ref = bf16[8,288,256]{2,1,0:T(8,128)(2,1)S(1)} async-done(((bf16[8,288,256]{2,1,0:T(8,128)(2,1)}), bf16[8,288,256]{2,1,0:T(8,128)(2,1)S(1)}, u32[]{:S(2)}, u32[]{:S(2)}) %all-to-all-start) | async-done | bytes 1179680 | tf_op jit(solution)/shard_map/all_to_all | solution.py:220
  59.8 5.9 %shard_map.59 = (bf16[8,32,256]{2,1,0:T(8,128)(2,1)S(1)}, f32[512,256]{1,0:T(8,128)S(1)}, f32[512,256]{1,0:T(8,128)S(1)}, bf16[896,2048]{1,0:T(8,128)(2,1)}, bf16[896,256]{1,0:T(8,128)(2,1)S(1)}) custom-call(s32[1]{0:T(128)} %bitcast.core_ref, bf16[8,288,256]{2,1,0:T(8,128)(2,1)S(1)} %all-to-all-done.r_ref, bf16[16,64,256]{2,1,0:T(8,128)(2,1)S(1)} %all-to-all-done.1.w_ref), custom_call_target="tpu_custom_call" | custom-call | flops 1879048192 | bytes 7012356 | tf_op jit(solution)/shard_map/pallas_call | solution.py:172
  66.2 1.5 %collective-permute-done.1 = f32[512,256]{1,0:T(8,128)S(1)} collective-permute-done((f32[512,256]{1,0:T(8,128)S(1)}, f32[512,256]{1,0:T(8,128)S(1)}, u32[]{:S(2)}, u32[]{:S(2)}) %collective-permute-start.1) | collective-permute-done | bytes 524320 | tf_op jit(solution)/shard_map/ppermute | solution.py:237
  68.5 3.8 %all-to-all-start.3 = ((bf16[8,64,256]{2,1,0:T(8,128)(2,1)}), bf16[8,64,256]{2,1,0:T(8,128)(2,1)S(1)}, u32[]{:S(2)}, u32[]{:S(2)}) async-start(bf16[8,64,256]{2,1,0:T(8,128)(2,1)} %bitcast.7), calls=%async_computation.3 | async-start | bytes 524288 | tf_op jit(solution)/shard_map/all_to_all | solution.py:238
  72.3 2.0 %copy-done = bf16[896,2048]{1,0:T(8,128)(2,1)S(1)} copy-done((bf16[896,2048]{1,0:T(8,128)(2,1)S(1)}, bf16[896,2048]{1,0:T(8,128)(2,1)}, u32[]{:S(2)}) %copy-start) | copy-done | bytes 3670040
  74.3 2.3 %shard_map.60 = bf16[8,288,256]{2,1,0:T(8,128)(2,1)} custom-call(bf16[896,2048]{1,0:T(8,128)(2,1)S(1)} %copy-done, bf16[896,256]{1,0:T(8,128)(2,1)S(1)} %get-tuple-element.11.w2_ref, bf16[8,32,256]{2,1,0:T(8,128)(2,1)S(1)} %get-tuple-element.12.act_ref), custom_call_target="tpu_custom_call" | custom-call | flops 939524096 | bytes 5439488 | tf_op jit(solution)/shard_map/pallas_call | solution.py:172
  76.6 7.9 %all-to-all-done.3 = bf16[8,64,256]{2,1,0:T(8,128)(2,1)S(1)} async-done(((bf16[8,64,256]{2,1,0:T(8,128)(2,1)}), bf16[8,64,256]{2,1,0:T(8,128)(2,1)S(1)}, u32[]{:S(2)}, u32[]{:S(2)}) %all-to-all-start.3) | async-done | bytes 262176 | tf_op jit(solution)/shard_map/all_to_all | solution.py:238
  84.5 4.7 %all-to-all-start.2 = ((bf16[8,288,256]{2,1,0:T(8,128)(2,1)}), bf16[8,288,256]{2,1,0:T(8,128)(2,1)S(1)}, u32[]{:S(2)}, u32[]{:S(2)}) async-start(bf16[8,288,256]{2,1,0:T(8,128)(2,1)} %shard_map.60), calls=%async_computation.2 | async-start | bytes 2359296 | tf_op jit(solution)/shard_map/all_to_all | solution.py:249
  89.2 2.0 %collective-permute-start.2 = (bf16[64,256]{1,0:T(8,128)(2,1)S(1)}, bf16[64,256]{1,0:T(8,128)(2,1)S(1)}, u32[]{:S(2)}, u32[]{:S(2)}) collective-permute-start(bf16[64,256]{1,0:T(8,128)(2,1)S(1)} %reduce_sum.21), channel_id=1, source_target_pairs={{0,0},{1,1},{2,32},{3,33},{4,64},{5,65},{6,96},{7,97},{8,128},{9,1... | collective-permute-start | bytes 98312 | tf_op jit(solution)/shard_map/ppermute | solution.py:254
  91.3 4.8 %collective-permute-done.2 = bf16[64,256]{1,0:T(8,128)(2,1)S(1)} collective-permute-done((bf16[64,256]{1,0:T(8,128)(2,1)S(1)}, bf16[64,256]{1,0:T(8,128)(2,1)S(1)}, u32[]{:S(2)}, u32[]{:S(2)}) %collective-permute-start.2) | collective-permute-done | bytes 32800 | tf_op jit(solution)/shard_map/ppermute | solution.py:254
  96.0 9.2 %all-to-all-done.2.r_ref = bf16[8,288,256]{2,1,0:T(8,128)(2,1)S(1)} async-done(((bf16[8,288,256]{2,1,0:T(8,128)(2,1)}), bf16[8,288,256]{2,1,0:T(8,128)(2,1)S(1)}, u32[]{:S(2)}, u32[]{:S(2)}) %all-to-all-start.2) | async-done | bytes 1179680 | tf_op jit(solution)/shard_map/all_to_all | solution.py:249
  105.2 0.9 broadcast_in_dim.5
  106.1 6.1 %all-to-all-start.4 = ((bf16[16,64,256]{2,1,0:T(8,128)(2,1)}), bf16[16,64,256]{2,1,0:T(8,128)(2,1)S(1)}, u32[]{:S(2)}, u32[]{:S(2)}) async-start(bf16[16,64,256]{2,1,0:T(8,128)(2,1)} %broadcast_in_dim.5), calls=%async_computation.4 | async-start | bytes 1048576 | tf_op jit(solution)/shard_map/all_to_all | solution.py:255
  112.2 0.9 shard_map.61
  113.1 8.1 %all-to-all-done.4 = bf16[16,64,256]{2,1,0:T(8,128)(2,1)S(1)} async-done(((bf16[16,64,256]{2,1,0:T(8,128)(2,1)}), bf16[16,64,256]{2,1,0:T(8,128)(2,1)S(1)}, u32[]{:S(2)}, u32[]{:S(2)}) %all-to-all-start.4) | async-done | bytes 524320 | tf_op jit(solution)/shard_map/all_to_all | solution.py:255
  121.4 0.8 fusion
  (9 shorter events, 1.4 us)
Async XLA Ops:
  0.6 22.7 %copy-start.2 = (bf16[1,4,8,8,256]{4,3,2,1,0:T(8,128)(2,1)S(1)}, bf16[1,4,8,8,256]{4,3,2,1,0:T(8,128)(2,1)}, u32[]{:S(2)}) copy-start(bf16[1,4,8,8,256]{4,3,2,1,0:T(8,128)(2,1)} %param.5) | copy-start | bytes 393220
  0.6 22.7 %copy-start.1 = (bf16[1,4,8,8,256]{4,3,2,1,0:T(8,128)(2,1)S(1)}, bf16[1,4,8,8,256]{4,3,2,1,0:T(8,128)(2,1)}, u32[]{:S(2)}) copy-start(bf16[1,4,8,8,256]{4,3,2,1,0:T(8,128)(2,1)} %param.3) | copy-start | bytes 393220
  1.5 6.9 %collective-permute-start = (bf16[64,256]{1,0:T(8,128)(2,1)S(1)}, bf16[64,256]{1,0:T(8,128)(2,1)S(1)}, u32[]{:S(2)}, u32[]{:S(2)}) collective-permute-start(bf16[64,256]{1,0:T(8,128)(2,1)S(1)} %bitcast.18), channel_id=1, source_target_pairs={{0,0},{1,1},{2,32},{3,33},{4,64},{5,65},{6,96},{7,97},{8,128},{9,1... | collective-permute-start | bytes 98312 | tf_op jit(solution)/shard_map/ppermute | solution.py:211
  9.2 30.1 %all-to-all-start.1 = ((bf16[16,64,256]{2,1,0:T(8,128)(2,1)}), bf16[16,64,256]{2,1,0:T(8,128)(2,1)S(1)}, u32[]{:S(2)}, u32[]{:S(2)}) async-start(bf16[16,64,256]{2,1,0:T(8,128)(2,1)} %broadcast_in_dim.4), calls=%async_computation.1 | async-start | bytes 1048576 | tf_op jit(solution)/shard_map/all_to_all | solution.py:212
  39.4 20.4 %all-to-all-start = ((bf16[8,288,256]{2,1,0:T(8,128)(2,1)}), bf16[8,288,256]{2,1,0:T(8,128)(2,1)S(1)}, u32[]{:S(2)}, u32[]{:S(2)}) async-start(bf16[8,288,256]{2,1,0:T(8,128)(2,1)} %shard_map.58), calls=%async_computation | async-start | bytes 2359296 | tf_op jit(solution)/shard_map/all_to_all | solution.py:220
  65.7 2.1 %collective-permute-start.1 = (f32[512,256]{1,0:T(8,128)S(1)}, f32[512,256]{1,0:T(8,128)S(1)}, u32[]{:S(2)}, u32[]{:S(2)}) collective-permute-start(f32[512,256]{1,0:T(8,128)S(1)} %get-tuple-element.16), channel_id=1, source_target_pairs={{0,16},{16,0},{32,48},{48,32},{64,80},{80,64},{96,112},{112,96},{1... | collective-permute-start | bytes 1572872 | tf_op jit(solution)/shard_map/ppermute | solution.py:237
  68.5 16.0 %all-to-all-start.3 = ((bf16[8,64,256]{2,1,0:T(8,128)(2,1)}), bf16[8,64,256]{2,1,0:T(8,128)(2,1)S(1)}, u32[]{:S(2)}, u32[]{:S(2)}) async-start(bf16[8,64,256]{2,1,0:T(8,128)(2,1)} %bitcast.7), calls=%async_computation.3 | async-start | bytes 524288 | tf_op jit(solution)/shard_map/all_to_all | solution.py:238
  72.3 2.0 %copy-start = (bf16[896,2048]{1,0:T(8,128)(2,1)S(1)}, bf16[896,2048]{1,0:T(8,128)(2,1)}, u32[]{:S(2)}) copy-start(bf16[896,2048]{1,0:T(8,128)(2,1)} %get-tuple-element.10.g_ref) | copy-start | bytes 11010052
  84.5 20.7 %all-to-all-start.2 = ((bf16[8,288,256]{2,1,0:T(8,128)(2,1)}), bf16[8,288,256]{2,1,0:T(8,128)(2,1)S(1)}, u32[]{:S(2)}, u32[]{:S(2)}) async-start(bf16[8,288,256]{2,1,0:T(8,128)(2,1)} %shard_map.60), calls=%async_computation.2 | async-start | bytes 2359296 | tf_op jit(solution)/shard_map/all_to_all | solution.py:249
  89.2 6.8 %collective-permute-start.2 = (bf16[64,256]{1,0:T(8,128)(2,1)S(1)}, bf16[64,256]{1,0:T(8,128)(2,1)S(1)}, u32[]{:S(2)}, u32[]{:S(2)}) collective-permute-start(bf16[64,256]{1,0:T(8,128)(2,1)S(1)} %reduce_sum.21), channel_id=1, source_target_pairs={{0,0},{1,1},{2,32},{3,33},{4,64},{5,65},{6,96},{7,97},{8,128},{9,1... | collective-permute-start | bytes 98312 | tf_op jit(solution)/shard_map/ppermute | solution.py:254
  106.1 15.2 %all-to-all-start.4 = ((bf16[16,64,256]{2,1,0:T(8,128)(2,1)}), bf16[16,64,256]{2,1,0:T(8,128)(2,1)S(1)}, u32[]{:S(2)}, u32[]{:S(2)}) async-start(bf16[16,64,256]{2,1,0:T(8,128)(2,1)} %broadcast_in_dim.5), calls=%async_computation.4 | async-start | bytes 1048576 | tf_op jit(solution)/shard_map/all_to_all | solution.py:255

commit v2 on v1

--- a/solution.py
+++ b/solution.py
@@ -1,5 +1,3 @@
-import functools
-
 import jax
 import jax.numpy as jnp
 from jax import lax
@@ -46,12 +44,15 @@
     return pltpu.roll(block, shift % LANES, 1)
 
 
-def main_kernel(core_ref, r_ref, w_ref, act_ref, own_ref, other_ref, g_ref, w2_ref, z_ref):
+def main_kernel(
+    core_ref, r_ref, same_ref, opposite_ref, out_ref, own_ref, other_ref, g_ref, w2_ref, z_ref
+):
+    first = core_ref[0] == 0
     for tap in range(TAPS):
-        for core in range(2):
-            w2_ref[tap * OUTS + core * 16 : tap * OUTS + core * 16 + 16, :] = w_ref[
-                (tap // 4) * 2 + core, (tap % 4) * 16 : (tap % 4) * 16 + 16, :
-            ]
+        start = tap * OUTS
+        same, opposite = same_ref[tap], opposite_ref[tap]
+        w2_ref[start : start + 16, :] = jnp.where(first, same, opposite)
+        w2_ref[start + 16 : start + 32, :] = jnp.where(first, opposite, same)
     w2_ref[TAPS * OUTS :, :] = jnp.zeros((OUTS, CELLS), BF16)
     g_ref[TAPS * OUTS :, :] = jnp.zeros((OUTS, WHOLE), BF16)
     taps_by_outs = w2_ref[: TAPS * OUTS, :]
@@ -92,9 +93,10 @@
                 total = over_y if total is None else total + over_y
             slab, part = column // 2, column % 2
             lanes = slice(part * LANES, (part + 1) * LANES)
-            outs = slice(group * 16, group * 16 + 16)
             logistic = 1.0 / (1.0 + jnp.exp(-total))
-            act_ref[slab, outs, lanes] = (total * logistic).astype(BF16)
+            out_ref[slab, CELLS + group * 16 : CELLS + group * 16 + 16, lanes] = (
+                total * logistic
+            ).astype(BF16)
             upstream = r_ref[
                 slab, CELLS + group * 16 : CELLS + group * 16 + 16, lanes
             ].astype(F32)
@@ -128,7 +130,6 @@
         r_ref[:, :CELLS, :].reshape(WHOLE, CELLS),
         preferred_element_type=F32,
     )
-    first = core_ref[0] == 0
     for tap in range(TAPS):
         start = tap * OUTS
         left = whole[start : start + 16]
@@ -139,15 +140,25 @@
         )
     own_ref[TAPS * 16 :, :] = jnp.zeros((5 * 16, CELLS), own_ref.dtype)
     other_ref[TAPS * 16 :, :] = jnp.zeros((5 * 16, CELLS), other_ref.dtype)
-
-
-def input_kernel(g_ref, w2_ref, act_ref, out_ref):
     turned = jnp.transpose(w2_ref[...].astype(F32)).astype(BF16)
     for slab in range(SLABS):
         out_ref[slab, :CELLS, :] = jnp.dot(
             turned, g_ref[:, slab * CELLS : (slab + 1) * CELLS], preferred_element_type=F32
         ).astype(BF16)
-        out_ref[slab, CELLS:, :] = act_ref[slab]
+
+
+def halve_kernel(bit_ref, mine_ref, got_ref, kept_ref, sent_ref):
+    half = kept_ref.shape[0]
+    total = mine_ref[...] + got_ref[...].astype(F32)
+    first = bit_ref[0] == 0
+    kept_ref[...] = jnp.where(first, total[:half], total[half:])
+    sent_ref[...] = jnp.where(first, total[half:], total[:half]).astype(BF16)
+
+
+def share_kernel(left_ref, right_ref, after_ref, out_ref):
+    total = (left_ref[...].astype(F32) + right_ref[...].astype(F32)).astype(BF16)
+    for slab in range(SLABS):
+        out_ref[slab] = total
 
 
 def final_kernel(r_ref, act_ref, grad_ref):
@@ -180,8 +191,8 @@
     )(*operands)
 
 
-def repeated(block, count):
-    return jnp.broadcast_to(block[None], (count,) + block.shape)
+def reversed_bits(z):
+    return (z & 1) * 4 + (z & 2) + (z >> 2)
 
 
 def local(inputs, weights, upstream):
@@ -204,12 +215,10 @@
         for rep in range(reps)
     ]
     cores = [(2 * z + core, 2 * z + 1 - core) for z in range(chips) for core in range(2)]
-    columns = [[2 * z + core for z in range(chips)] for core in range(2)]
-
-    by_tap = jnp.pad(jnp.transpose(weights, (1, 0, 2)), ((0, 5), (0, 0), (0, 0)))
-    piece = lax.dynamic_slice_in_dim(by_tap, slab * 4, 4, axis=0).reshape(64, CELLS)
-    piece = lax.ppermute(piece, everyone, crossed)
-    pieces = lax.all_to_all(repeated(piece, 2 * chips), "fsdp", 0, 0)
+
+    by_tap = jnp.transpose(weights, (1, 0, 2))
+    same = lax.ppermute(by_tap, everyone, crossed)
+    opposite = lax.ppermute(same, "fsdp", cores)
 
     cells = inputs.reshape(CELLS, CELLS)
     packed = call(
@@ -220,40 +229,64 @@
     gathered = lax.all_to_all(packed, "slab", 0, 0)
 
     core = (owner % 2).astype(jnp.int32).reshape(1)
-    act, own, other, grads, kernel_rows = call(
+    terms, own, other = call(
         main_kernel,
         [
-            shape(SLABS, OUTS, CELLS),
+            shape(SLABS, CELLS + OUTS, CELLS),
             shape(512, CELLS, dtype=F32),
             shape(512, CELLS, dtype=F32),
-            shape(ROWS, WHOLE),
-            shape(ROWS, CELLS),
         ],
-        (core, gathered, pieces),
-        specs=[SMEM, VMEM, VMEM],
-        scratch=[pltpu.VMEM((TAPS * OUTS, WHOLE), F32)],
-        flops=4 * ROWS * WHOLE * CELLS,
-    )
-    own = own + lax.ppermute(other, "fsdp", cores)
-    sums = lax.all_to_all(
-        own.astype(BF16).reshape(chips, 64, CELLS), "fsdp", 0, 0, axis_index_groups=columns
-    )
-    sums = jnp.sum(sums.astype(F32), axis=0).astype(BF16)
-
-    terms = call(
-        input_kernel,
-        [shape(SLABS, CELLS + OUTS, CELLS)],
-        (grads, kernel_rows, act),
-        flops=2 * ROWS * WHOLE * CELLS,
-    )[0]
+        (core, gathered, same, opposite),
+        specs=[SMEM, VMEM, VMEM, VMEM],
+        scratch=[
+            pltpu.VMEM((ROWS, WHOLE), BF16),
+            pltpu.VMEM((ROWS, CELLS), BF16),
+            pltpu.VMEM((TAPS * OUTS, WHOLE), F32),
+        ],
+        flops=6 * ROWS * WHOLE * CELLS,
+    )
     returned = lax.all_to_all(terms, "slab", 0, 0)
     activated, input_grad = call(
         final_kernel, [shape(CELLS, CELLS), shape(CELLS, CELLS)], (returned,)
     )
 
-    sums = lax.ppermute(sums, everyone, crossed)
-    parts = lax.all_to_all(repeated(sums, SLABS * reps), ("slab", "rep"), 0, 0)
-    parts = jnp.sum(parts.reshape(SLABS, reps, 64, CELLS).astype(F32), axis=1)
+    got = lax.ppermute(other, "fsdp", cores)
+    chip = owner // 2
+    for step in range(3):
+        bit = ((chip >> step) & 1).astype(jnp.int32).reshape(1)
+        half = own.shape[0] // 2
+        own, sent = call(
+            halve_kernel,
+            [shape(half, CELLS, dtype=F32), shape(half, CELLS)],
+            (bit, own, got),
+            specs=[SMEM, VMEM, VMEM],
+        )
+        pairs = [
+            (2 * z + core, 2 * (z ^ (1 << step)) + core) for z in range(chips) for core in range(2)
+        ]
+        got = lax.ppermute(sent, "fsdp", pairs)
+    sums = (own + got.astype(F32)).astype(BF16)
+    shares = [
+        lax.ppermute(
+            sums,
+            everyone,
+            [
+                (place(z, core, y, rep), place(y, core, reversed_bits(z), (rep + turn_by) % reps))
+                for z in range(chips)
+                for core in range(2)
+                for y in range(SLABS)
+                for rep in range(reps)
+            ],
+        )
+        for turn_by in range(reps)
+    ]
+    share = call(
+        share_kernel,
+        [shape(SLABS, 64, CELLS)],
+        (*shares, returned),
+        specs=[VMEM, VMEM, pl.BlockSpec(memory_space=pl.ANY)],
+    )[0]
+    parts = lax.all_to_all(share, "slab", 0, 0).astype(F32)
     weight_grad = jnp.transpose(parts.reshape(32, 16, CELLS)[:TAPS], (1, 0, 2)) * factor
     return (
         activated.reshape(inputs.shape),

time: 123 us -> 110 us (0.89)
  waiting for transfers between devices: 66.2 us -> 47.9 us
  starting transfers between devices: 38.7 us -> 47.8 us
  local copies, waits for them, and re-layouts: 4.59 us -> 1.8 us
  Pallas kernels: 10.3 us -> 8.93 us
    all_to_all x3 -> x1, waiting for transfers between devices: 30.9 us -> 5.21 us  [local(): parts = lax.all_to_all(share, 'slab', 0, 0).astype(F32)]
    ppermute x3 -> x8, waiting for transfers between devices: 9.41 us -> 33 us  [the longest x1 17.8 us: local(): same = lax.ppermute(by_tap, everyone, crossed)]
    ppermute x3 -> x8, starting transfers between devices: 6.34 us -> 26.4 us  [the longest x3 14.6 us: local(): got = lax.ppermute(sent, 'fsdp', pairs)]
    all_to_all x3 -> x1, starting transfers between devices: 24 us -> 11.6 us  [local(): parts = lax.all_to_all(share, 'slab', 0, 0).astype(F32)]
    all_to_all x1, waiting for transfers between devices: 9.19 us -> 0.01 us  [local(): returned = lax.all_to_all(terms, 'slab', 0, 0)]
    all_to_all x1, waiting for transfers between devices: 16.7 us -> 9.7 us  [local(): gathered = lax.all_to_all(packed, 'slab', 0, 0)]
    all_to_all x1, starting transfers between devices: 3.71 us -> 6.06 us  [local(): gathered = lax.all_to_all(packed, 'slab', 0, 0)]
    broadcast_in_dim x2 -> x0, local copies, waits for them, and re-layouts: 1.72 us -> none  [repeated(): return jnp.broadcast_to(block[None], (count,) + block.shape)]
  transfers between devices with their start and end apart: 8 -> 11, of which waited for: 8 -> 10; matrix products, arithmetic and copies ran while one was open for 0% -> 0% of each run, Pallas kernels for 4% -> 1%
where the time goes in v2:
time: 110 us; the launch traced here: 108 us
  waiting for transfers between devices  47.9 us (44%)
  starting transfers between devices  47.8 us (43%)
  Pallas kernels  8.93 us (8%)
  local copies, waits for them, and re-layouts  1.8 us (2%)
    ppermute x1, waiting for transfers between devices, local(): same = lax.ppermute(by_tap, everyone, crossed)  17.8 us
    ppermute x3, starting transfers between devices, local(): got = lax.ppermute(sent, 'fsdp', pairs)  14.6 us
    all_to_all x1, starting transfers between devices, local(): parts = lax.all_to_all(share, 'slab', 0, 0).astype(F32)  11.6 us
    all_to_all x1, waiting for transfers between devices, local(): gathered = lax.all_to_all(packed, 'slab', 0, 0)  9.7 us
    pallas_call x7, Pallas kernels, call(): pl.pallas_call(kernel, out_shape=tuple(outs), in_specs=specs or [VMEM] *...  8.93 us
    ppermute x2, starting transfers between devices, local(): lax.ppermute(sums, everyone, [(place(z, core, y, rep), place(y, core, rev...  8.55 us
    ppermute x3, waiting for transfers between devices, local(): got = lax.ppermute(sent, 'fsdp', pairs)  8.45 us
    all_to_all x1, starting transfers between devices, local(): gathered = lax.all_to_all(packed, 'slab', 0, 0)  6.06 us
  transfers between devices with their start and end apart: 11, of which 10 were waited for; matrix products, arithmetic and copies ran while one was open for 0% of the time, Pallas kernels for 1%

profile of v2, /device:TPU:2, one launch (start us, length us, event | category | flops | bytes accessed | tf_op | source)
XLA Modules:
  0.0 107.9 jit_solution(7623258584001547088)
XLA Ops:
  0.6 0.9 copy-done
  1.5 0.9 copy-done.1
  2.4 1.1 %shard_map.58 = bf16[8,288,256]{2,1,0:T(8,128)(2,1)} custom-call(bf16[256,256]{1,0:T(8,128)(2,1)S(1)} %bitcast.12, bf16[256,256]{1,0:T(8,128)(2,1)S(1)} %bitcast.13), custom_call_target="tpu_custom_call" | custom-call | bytes 1441792 | tf_op jit(solution)/shard_map/pallas_call | solution.py:183
  3.6 6.1 %all-to-all-start = ((bf16[8,288,256]{2,1,0:T(8,128)(2,1)}), bf16[8,288,256]{2,1,0:T(8,128)(2,1)S(1)}, u32[]{:S(2)}, u32[]{:S(2)}) async-start(bf16[8,288,256]{2,1,0:T(8,128)(2,1)} %shard_map.58), calls=%async_computation | async-start | bytes 2359296 | tf_op jit(solution)/shard_map/all_to_all | solution.py:229
  9.7 3.3 %collective-permute-start = (bf16[27,16,256]{2,1,0:T(8,128)(2,1)S(1)}, bf16[27,16,256]{2,1,0:T(8,128)(2,1)S(1)}, u32[]{:S(2)}, u32[]{:S(2)}) collective-permute-start(bf16[27,16,256]{2,1,0:T(8,128)(2,1)S(1)} %bitcast.15), channel_id=1, source_target_pairs={{0,0},{1,1},{2,32},{3,33},{4,64},{5,65},{6,96},{7,97},{8,128},{9,1... | collective-permute-start | bytes 663560 | tf_op jit(solution)/shard_map/ppermute | solution.py:220
  12.9 17.8 %collective-permute-done.same_ref = bf16[27,16,256]{2,1,0:T(8,128)(2,1)S(1)} collective-permute-done((bf16[27,16,256]{2,1,0:T(8,128)(2,1)S(1)}, bf16[27,16,256]{2,1,0:T(8,128)(2,1)S(1)}, u32[]{:S(2)}, u32[]{:S(2)}) %collective-permute-start) | collective-permute-done | bytes 221216 | tf_op jit(solution)/shard_map/ppermute | solution.py:220
  30.7 1.5 %collective-permute-done.1.opposite_ref = bf16[27,16,256]{2,1,0:T(8,128)(2,1)S(1)} collective-permute-done((bf16[27,16,256]{2,1,0:T(8,128)(2,1)S(1)}, bf16[27,16,256]{2,1,0:T(8,128)(2,1)S(1)}, u32[]{:S(2)}, u32[]{:S(2)}) %collective-permute-start.1) | collective-permute-done | bytes 221216 | tf_op jit(solution)/shard_map/ppermute | solution.py:221
  32.2 9.7 %all-to-all-done.r_ref = bf16[8,288,256]{2,1,0:T(8,128)(2,1)S(1)} async-done(((bf16[8,288,256]{2,1,0:T(8,128)(2,1)}), bf16[8,288,256]{2,1,0:T(8,128)(2,1)S(1)}, u32[]{:S(2)}, u32[]{:S(2)}) %all-to-all-start) | async-done | bytes 1179680 | tf_op jit(solution)/shard_map/all_to_all | solution.py:229
  41.9 6.1 %shard_map.59 = (bf16[8,288,256]{2,1,0:T(8,128)(2,1)}, f32[512,256]{1,0:T(8,128)S(1)}, f32[512,256]{1,0:T(8,128)S(1)}) custom-call(s32[1]{0:T(128)} %bitcast.core_ref, bf16[8,288,256]{2,1,0:T(8,128)(2,1)S(1)} %all-to-all-done.r_ref, bf16[27,16,256]{2,1,0:T(8,128)(2,1)S(1)} %collective-permute-done.same_ref, ...), custom_call_target="tpu_custom_call" | custom-call | flops 2818572288 | bytes 3850244 | tf_op jit(solution)/shard_map/pallas_call | solution.py:183
  47.9 3.7 %all-to-all-start.1 = ((bf16[8,288,256]{2,1,0:T(8,128)(2,1)}), bf16[8,288,256]{2,1,0:T(8,128)(2,1)S(1)}, u32[]{:S(2)}, u32[]{:S(2)}) async-start(bf16[8,288,256]{2,1,0:T(8,128)(2,1)} %get-tuple-element.14), calls=%async_computation.1 | async-start | bytes 2359296 | tf_op jit(solution)/shard_map/all_to_all | solution.py:248
  51.6 1.9 %collective-permute-done.2.got_ref = f32[512,256]{1,0:T(8,128)S(1)} collective-permute-done((f32[512,256]{1,0:T(8,128)S(1)}, f32[512,256]{1,0:T(8,128)S(1)}, u32[]{:S(2)}, u32[]{:S(2)}) %collective-permute-start.2) | collective-permute-done | bytes 524320 | tf_op jit(solution)/shard_map/ppermute | solution.py:253
  53.6 2.8 %collective-permute-start.3 = (bf16[256,256]{1,0:T(8,128)(2,1)S(1)}, bf16[256,256]{1,0:T(8,128)(2,1)S(1)}, u32[]{:S(2)}, u32[]{:S(2)}) collective-permute-start(bf16[256,256]{1,0:T(8,128)(2,1)S(1)} %get-tuple-element.20), channel_id=1, source_target_pairs={{0,32},{16,48},{32,0},{48,16},{64,96},{80,112},{96,64},{112,80},{1... | collective-permute-start | bytes 393224 | tf_op jit(solution)/shard_map/ppermute | solution.py:267
  56.4 3.8 %collective-permute-done.3.got_ref = bf16[256,256]{1,0:T(8,128)(2,1)S(1)} collective-permute-done((bf16[256,256]{1,0:T(8,128)(2,1)S(1)}, bf16[256,256]{1,0:T(8,128)(2,1)S(1)}, u32[]{:S(2)}, u32[]{:S(2)}) %collective-permute-start.3) | collective-permute-done | bytes 131104 | tf_op jit(solution)/shard_map/ppermute | solution.py:267
  60.2 4.9 %collective-permute-start.4 = (bf16[128,256]{1,0:T(8,128)(2,1)S(1)}, bf16[128,256]{1,0:T(8,128)(2,1)S(1)}, u32[]{:S(2)}, u32[]{:S(2)}) collective-permute-start(bf16[128,256]{1,0:T(8,128)(2,1)S(1)} %get-tuple-element.22), channel_id=1, source_target_pairs={{0,64},{16,80},{32,96},{48,112},{64,0},{80,16},{96,32},{112,48},{1... | collective-permute-start | bytes 196616 | tf_op jit(solution)/shard_map/ppermute | solution.py:267
  65.1 2.8 %collective-permute-done.4.got_ref = bf16[128,256]{1,0:T(8,128)(2,1)S(1)} collective-permute-done((bf16[128,256]{1,0:T(8,128)(2,1)S(1)}, bf16[128,256]{1,0:T(8,128)(2,1)S(1)}, u32[]{:S(2)}, u32[]{:S(2)}) %collective-permute-start.4) | collective-permute-done | bytes 65568 | tf_op jit(solution)/shard_map/ppermute | solution.py:267
  67.9 7.0 %collective-permute-start.5 = (bf16[64,256]{1,0:T(8,128)(2,1)S(1)}, bf16[64,256]{1,0:T(8,128)(2,1)S(1)}, u32[]{:S(2)}, u32[]{:S(2)}) collective-permute-start(bf16[64,256]{1,0:T(8,128)(2,1)S(1)} %get-tuple-element.24), channel_id=1, source_target_pairs={{0,128},{16,144},{32,160},{48,176},{64,192},{80,208},{96,224},{112... | collective-permute-start | bytes 98312 | tf_op jit(solution)/shard_map/ppermute | solution.py:267
  74.8 1.9 %collective-permute-done.5 = bf16[64,256]{1,0:T(8,128)(2,1)S(1)} collective-permute-done((bf16[64,256]{1,0:T(8,128)(2,1)S(1)}, bf16[64,256]{1,0:T(8,128)(2,1)S(1)}, u32[]{:S(2)}, u32[]{:S(2)}) %collective-permute-start.5) | collective-permute-done | bytes 32800 | tf_op jit(solution)/shard_map/ppermute | solution.py:267
  76.7 0.9 collective-permute-start.7
  77.6 7.6 %collective-permute-start.6 = (bf16[64,256]{1,0:T(8,128)(2,1)S(1)}, bf16[64,256]{1,0:T(8,128)(2,1)S(1)}, u32[]{:S(2)}, u32[]{:S(2)}) collective-permute-start(bf16[64,256]{1,0:T(8,128)(2,1)S(1)} %add_convert_fusion), channel_id=1, source_target_pairs={{0,0},{1,1},{2,32},{3,33},{4,64},{5,65},{6,96},{7,97},{8,128},{9,1... | collective-permute-start | bytes 98312 | tf_op jit(solution)/shard_map/ppermute | solution.py:270
  85.5 3.1 %collective-permute-done.6.left_ref = bf16[64,256]{1,0:T(8,128)(2,1)S(1)} collective-permute-done((bf16[64,256]{1,0:T(8,128)(2,1)S(1)}, bf16[64,256]{1,0:T(8,128)(2,1)S(1)}, u32[]{:S(2)}, u32[]{:S(2)}) %collective-permute-start.6) | collective-permute-done | bytes 32800 | tf_op jit(solution)/shard_map/ppermute | solution.py:270
  89.4 11.6 %all-to-all-start.2 = ((bf16[8,64,256]{2,1,0:T(8,128)(2,1)}), bf16[8,64,256]{2,1,0:T(8,128)(2,1)S(1)}, u32[]{:S(2)}, u32[]{:S(2)}) async-start(bf16[8,64,256]{2,1,0:T(8,128)(2,1)} %shard_map.64), calls=%async_computation.2 | async-start | bytes 524288 | tf_op jit(solution)/shard_map/all_to_all | solution.py:289
  101.0 0.9 shard_map.60
  101.9 5.2 %all-to-all-done.2 = bf16[8,64,256]{2,1,0:T(8,128)(2,1)S(1)} async-done(((bf16[8,64,256]{2,1,0:T(8,128)(2,1)}), bf16[8,64,256]{2,1,0:T(8,128)(2,1)S(1)}, u32[]{:S(2)}, u32[]{:S(2)}) %all-to-all-start.2) | async-done | bytes 262176 | tf_op jit(solution)/shard_map/all_to_all | solution.py:289
  107.1 0.8 multiply_bitcast_fusion
  (13 shorter events, 1.1 us)
Async XLA Ops:
  0.6 0.9 copy-start
  1.5 0.9 copy-start.1
  3.6 6.1 %copy-start.2 = (bf16[16,27,256]{2,0,1:T(8,128)(2,1)S(1)}, bf16[16,27,256]{2,0,1:T(8,128)(2,1)}, u32[]{:S(2)}) copy-start(bf16[16,27,256]{2,0,1:T(8,128)(2,1)} %param.4) | copy-start | bytes 663556
  3.6 38.3 %all-to-all-start = ((bf16[8,288,256]{2,1,0:T(8,128)(2,1)}), bf16[8,288,256]{2,1,0:T(8,128)(2,1)S(1)}, u32[]{:S(2)}, u32[]{:S(2)}) async-start(bf16[8,288,256]{2,1,0:T(8,128)(2,1)} %shard_map.58), calls=%async_computation | async-start | bytes 2359296 | tf_op jit(solution)/shard_map/all_to_all | solution.py:229
  9.7 21.1 %collective-permute-start = (bf16[27,16,256]{2,1,0:T(8,128)(2,1)S(1)}, bf16[27,16,256]{2,1,0:T(8,128)(2,1)S(1)}, u32[]{:S(2)}, u32[]{:S(2)}) collective-permute-start(bf16[27,16,256]{2,1,0:T(8,128)(2,1)S(1)} %bitcast.15), channel_id=1, source_target_pairs={{0,0},{1,1},{2,32},{3,33},{4,64},{5,65},{6,96},{7,97},{8,128},{9,1... | collective-permute-start | bytes 663560 | tf_op jit(solution)/shard_map/ppermute | solution.py:220
  30.7 1.5 %collective-permute-start.1 = (bf16[27,16,256]{2,1,0:T(8,128)(2,1)S(1)}, bf16[27,16,256]{2,1,0:T(8,128)(2,1)S(1)}, u32[]{:S(2)}, u32[]{:S(2)}) collective-permute-start(bf16[27,16,256]{2,1,0:T(8,128)(2,1)S(1)} %collective-permute-done.same_ref), channel_id=1, source_target_pairs={{0,16},{16,0},{32,48},{48,32},{64,80},{80,64},{96,112},{112,96},{1... | collective-permute-start | bytes 663560 | tf_op jit(solution)/shard_map/ppermute | solution.py:221
  47.9 40.7 %all-to-all-start.1 = ((bf16[8,288,256]{2,1,0:T(8,128)(2,1)}), bf16[8,288,256]{2,1,0:T(8,128)(2,1)S(1)}, u32[]{:S(2)}, u32[]{:S(2)}) async-start(bf16[8,288,256]{2,1,0:T(8,128)(2,1)} %get-tuple-element.14), calls=%async_computation.1 | async-start | bytes 2359296 | tf_op jit(solution)/shard_map/all_to_all | solution.py:248
  51.6 1.9 %collective-permute-start.2 = (f32[512,256]{1,0:T(8,128)S(1)}, f32[512,256]{1,0:T(8,128)S(1)}, u32[]{:S(2)}, u32[]{:S(2)}) collective-permute-start(f32[512,256]{1,0:T(8,128)S(1)} %get-tuple-element.18), channel_id=1, source_target_pairs={{0,16},{16,0},{32,48},{48,32},{64,80},{80,64},{96,112},{112,96},{1... | collective-permute-start | bytes 1572872 | tf_op jit(solution)/shard_map/ppermute | solution.py:253
  53.6 6.6 %collective-permute-start.3 = (bf16[256,256]{1,0:T(8,128)(2,1)S(1)}, bf16[256,256]{1,0:T(8,128)(2,1)S(1)}, u32[]{:S(2)}, u32[]{:S(2)}) collective-permute-start(bf16[256,256]{1,0:T(8,128)(2,1)S(1)} %get-tuple-element.20), channel_id=1, source_target_pairs={{0,32},{16,48},{32,0},{48,16},{64,96},{80,112},{96,64},{112,80},{1... | collective-permute-start | bytes 393224 | tf_op jit(solution)/shard_map/ppermute | solution.py:267
  60.2 7.6 %collective-permute-start.4 = (bf16[128,256]{1,0:T(8,128)(2,1)S(1)}, bf16[128,256]{1,0:T(8,128)(2,1)S(1)}, u32[]{:S(2)}, u32[]{:S(2)}) collective-permute-start(bf16[128,256]{1,0:T(8,128)(2,1)S(1)} %get-tuple-element.22), channel_id=1, source_target_pairs={{0,64},{16,80},{32,96},{48,112},{64,0},{80,16},{96,32},{112,48},{1... | collective-permute-start | bytes 196616 | tf_op jit(solution)/shard_map/ppermute | solution.py:267
  67.9 8.9 %collective-permute-start.5 = (bf16[64,256]{1,0:T(8,128)(2,1)S(1)}, bf16[64,256]{1,0:T(8,128)(2,1)S(1)}, u32[]{:S(2)}, u32[]{:S(2)}) collective-permute-start(bf16[64,256]{1,0:T(8,128)(2,1)S(1)} %get-tuple-element.24), channel_id=1, source_target_pairs={{0,128},{16,144},{32,160},{48,176},{64,192},{80,208},{96,224},{112... | collective-permute-start | bytes 98312 | tf_op jit(solution)/shard_map/ppermute | solution.py:267
  76.7 8.8 %collective-permute-start.7 = (bf16[64,256]{1,0:T(8,128)(2,1)S(1)}, bf16[64,256]{1,0:T(8,128)(2,1)S(1)}, u32[]{:S(2)}, u32[]{:S(2)}) collective-permute-start(bf16[64,256]{1,0:T(8,128)(2,1)S(1)} %add_convert_fusion), channel_id=1, source_target_pairs={{0,1},{1,0},{2,33},{3,32},{4,65},{5,64},{6,97},{7,96},{8,129},{9,1... | collective-permute-start | bytes 98312 | tf_op jit(solution)/shard_map/ppermute | solution.py:270
  77.6 11.0 %collective-permute-start.6 = (bf16[64,256]{1,0:T(8,128)(2,1)S(1)}, bf16[64,256]{1,0:T(8,128)(2,1)S(1)}, u32[]{:S(2)}, u32[]{:S(2)}) collective-permute-start(bf16[64,256]{1,0:T(8,128)(2,1)S(1)} %add_convert_fusion), channel_id=1, source_target_pairs={{0,0},{1,1},{2,32},{3,33},{4,64},{5,65},{6,96},{7,97},{8,128},{9,1... | collective-permute-start | bytes 98312 | tf_op jit(solution)/shard_map/ppermute | solution.py:270
  89.4 17.7 %all-to-all-start.2 = ((bf16[8,64,256]{2,1,0:T(8,128)(2,1)}), bf16[8,64,256]{2,1,0:T(8,128)(2,1)S(1)}, u32[]{:S(2)}, u32[]{:S(2)}) async-start(bf16[8,64,256]{2,1,0:T(8,128)(2,1)} %shard_map.64), calls=%async_computation.2 | async-start | bytes 524288 | tf_op jit(solution)/shard_map/all_to_all | solution.py:289

commit v3 on v2

--- a/solution.py
+++ b/solution.py
@@ -21,11 +21,12 @@
     return (along_x * 3 + along_y) * 3 + along_z
 
 
-def pack_kernel(x_ref, u_ref, out_ref):
+def pack_kernel(chip_ref, x_ref, u_ref, out_ref):
     turned = jnp.transpose(u_ref[...].astype(F32)).astype(BF16)
     for slab in range(SLABS):
         out_ref[slab, :CELLS, :] = x_ref[...]
-        out_ref[slab, CELLS:, :] = turned[slab * OUTS : (slab + 1) * OUTS]
+    for pair in range(SLABS):
+        out_ref[(pair + chip_ref[0]) & 7, CELLS:, :] = turned[pair * OUTS : (pair + 1) * OUTS]
 
 
 def lane_masks():
@@ -138,8 +139,6 @@
         other_ref[tap * 16 : tap * 16 + 16, :] = jnp.where(first, right, left).astype(
             other_ref.dtype
         )
-    own_ref[TAPS * 16 :, :] = jnp.zeros((5 * 16, CELLS), own_ref.dtype)
-    other_ref[TAPS * 16 :, :] = jnp.zeros((5 * 16, CELLS), other_ref.dtype)
     turned = jnp.transpose(w2_ref[...].astype(F32)).astype(BF16)
     for slab in range(SLABS):
         out_ref[slab, :CELLS, :] = jnp.dot(
@@ -147,26 +146,35 @@
         ).astype(BF16)
 
 
-def halve_kernel(bit_ref, mine_ref, got_ref, kept_ref, sent_ref):
-    half = kept_ref.shape[0]
-    total = mine_ref[...] + got_ref[...].astype(F32)
-    first = bit_ref[0] == 0
-    kept_ref[...] = jnp.where(first, total[:half], total[half:])
-    sent_ref[...] = jnp.where(first, total[half:], total[:half]).astype(BF16)
-
-
-def share_kernel(left_ref, right_ref, after_ref, out_ref):
-    total = (left_ref[...].astype(F32) + right_ref[...].astype(F32)).astype(BF16)
-    for slab in range(SLABS):
-        out_ref[slab] = total
-
-
-def final_kernel(r_ref, act_ref, grad_ref):
+def lengthen_kernel(rows_ref, after_ref, out_ref):
+    out_ref[: TAPS * 16, :] = rows_ref[...]
+    out_ref[TAPS * 16 :, :] = jnp.zeros((out_ref.shape[0] - TAPS * 16, CELLS), BF16)
+
+
+def share_kernel(parts_ref, out_ref):
+    total = parts_ref[0].astype(F32)
+    for place in range(1, parts_ref.shape[0]):
+        total = total + parts_ref[place].astype(F32)
+    for place in range(out_ref.shape[0]):
+        out_ref[place] = total.astype(BF16)
+
+
+def final_kernel(chip_ref, r_ref, act_ref, grad_ref):
     total = r_ref[0, :CELLS, :].astype(F32)
     for slab in range(1, SLABS):
         total = total + r_ref[slab, :CELLS, :].astype(F32)
     grad_ref[...] = jnp.transpose(total).astype(BF16)
-    act_ref[...] = jnp.transpose(r_ref[:, CELLS:, :].astype(F32).reshape(CELLS, CELLS)).astype(BF16)
+    for half in range(2):
+        turned = jnp.transpose(
+            jnp.concatenate(
+                [
+                    r_ref[(pair + chip_ref[0]) & 7, CELLS:, :].astype(F32)
+                    for pair in range(half * 4, half * 4 + 4)
+                ],
+                axis=0,
+            )
+        )
+        act_ref[:, half * LANES : (half + 1) * LANES] = turned.astype(BF16)
 
 
 VMEM = pl.BlockSpec(memory_space=pltpu.VMEM)
@@ -191,13 +199,10 @@
     )(*operands)
 
 
-def reversed_bits(z):
-    return (z & 1) * 4 + (z & 2) + (z >> 2)
-
-
 def local(inputs, weights, upstream):
     owner = lax.axis_index("fsdp")
-    slab = lax.axis_index("slab")
+    core = (owner % 2).astype(jnp.int32).reshape(1)
+    chip = (owner // 2).astype(jnp.int32).reshape(1)
     chips = lax.axis_size("fsdp") // 2
     reps = lax.axis_size("rep")
     total_cells = 2 * chips * reps * WHOLE
@@ -207,8 +212,8 @@
         return ((z * 2 + core) * SLABS + y) * reps + rep
 
     everyone = ("fsdp", "slab", "rep")
-    crossed = [
-        (place(z, core, y, rep), place(y, core, z, rep))
+    mirrored = [
+        (place(z, core, y, rep), place((y - z) % SLABS, core, y, rep))
         for z in range(chips)
         for core in range(2)
         for y in range(SLABS)
@@ -217,24 +222,24 @@
     cores = [(2 * z + core, 2 * z + 1 - core) for z in range(chips) for core in range(2)]
 
     by_tap = jnp.transpose(weights, (1, 0, 2))
-    same = lax.ppermute(by_tap, everyone, crossed)
+    same = lax.ppermute(by_tap, everyone, mirrored)
     opposite = lax.ppermute(same, "fsdp", cores)
 
     cells = inputs.reshape(CELLS, CELLS)
     packed = call(
         pack_kernel,
         [shape(SLABS, CELLS + OUTS, CELLS)],
-        (cells, upstream.reshape(CELLS, CELLS)),
+        (chip, cells, upstream.reshape(CELLS, CELLS)),
+        specs=[SMEM, VMEM, VMEM],
     )[0]
     gathered = lax.all_to_all(packed, "slab", 0, 0)
 
-    core = (owner % 2).astype(jnp.int32).reshape(1)
     terms, own, other = call(
         main_kernel,
         [
             shape(SLABS, CELLS + OUTS, CELLS),
-            shape(512, CELLS, dtype=F32),
-            shape(512, CELLS, dtype=F32),
+            shape(TAPS * 16, CELLS, dtype=F32),
+            shape(TAPS * 16, CELLS, dtype=F32),
         ],
         (core, gathered, same, opposite),
         specs=[SMEM, VMEM, VMEM, VMEM],
@@ -247,46 +252,26 @@
     )
     returned = lax.all_to_all(terms, "slab", 0, 0)
     activated, input_grad = call(
-        final_kernel, [shape(CELLS, CELLS), shape(CELLS, CELLS)], (returned,)
-    )
-
-    got = lax.ppermute(other, "fsdp", cores)
-    chip = owner // 2
-    for step in range(3):
-        bit = ((chip >> step) & 1).astype(jnp.int32).reshape(1)
-        half = own.shape[0] // 2
-        own, sent = call(
-            halve_kernel,
-            [shape(half, CELLS, dtype=F32), shape(half, CELLS)],
-            (bit, own, got),
-            specs=[SMEM, VMEM, VMEM],
-        )
-        pairs = [
-            (2 * z + core, 2 * (z ^ (1 << step)) + core) for z in range(chips) for core in range(2)
-        ]
-        got = lax.ppermute(sent, "fsdp", pairs)
-    sums = (own + got.astype(F32)).astype(BF16)
-    shares = [
-        lax.ppermute(
-            sums,
-            everyone,
-            [
-                (place(z, core, y, rep), place(y, core, reversed_bits(z), (rep + turn_by) % reps))
-                for z in range(chips)
-                for core in range(2)
-                for y in range(SLABS)
-                for rep in range(reps)
-            ],
-        )
-        for turn_by in range(reps)
-    ]
-    share = call(
-        share_kernel,
-        [shape(SLABS, 64, CELLS)],
-        (*shares, returned),
-        specs=[VMEM, VMEM, pl.BlockSpec(memory_space=pl.ANY)],
+        final_kernel,
+        [shape(CELLS, CELLS), shape(CELLS, CELLS)],
+        (chip, returned),
+        specs=[SMEM, VMEM],
+    )
+
+    sums = (own + lax.ppermute(other, "fsdp", cores)).astype(BF16)
+    sums = lax.ppermute(sums, everyone, mirrored)
+    plane = SLABS * reps
+    sums = call(
+        lengthen_kernel,
+        [shape(512, CELLS)],
+        (sums, returned),
+        specs=[VMEM, pl.BlockSpec(memory_space=pl.ANY)],
     )[0]
-    parts = lax.all_to_all(share, "slab", 0, 0).astype(F32)
+    scattered = lax.all_to_all(
+        sums.reshape(plane, 512 // plane, CELLS), ("slab", "rep"), 0, 0
+    )
+    share = call(share_kernel, [shape(plane, 512 // plane, CELLS)], (scattered,))[0]
+    parts = lax.all_to_all(share, ("slab", "rep"), 0, 0).astype(F32)
     weight_grad = jnp.transpose(parts.reshape(32, 16, CELLS)[:TAPS], (1, 0, 2)) * factor
     return (
         activated.reshape(inputs.shape),

time: 110 us -> 84.7 us (0.77); the launches traced: 108 us -> 84.3 us
  starting transfers between devices: 47.8 us -> 25 us
  waiting for transfers between devices: 47.9 us -> 32.6 us
  blocking collectives: 0 us -> 14.5 us
    ppermute x7 -> x3, starting transfers between devices: 26.4 us -> 5.74 us  [the longest x1 3.81 us: local(): same = lax.ppermute(by_tap, everyone, mirrored)]
    all_to_all x0 -> x1, blocking collectives: none -> 14.5 us  [local(): lax.all_to_all(sums.reshape(plane, 512 // plane, CELLS), ('slab', 'rep'),...]
    ppermute x7 -> x3, waiting for transfers between devices: 31.5 us -> 22.8 us  [the longest x1 12.2 us: local(): sums = lax.ppermute(sums, everyone, mirrored)]
    all_to_all x1, waiting for transfers between devices: 9.7 us -> 1.79 us  [local(): gathered = lax.all_to_all(packed, 'slab', 0, 0)]
    all_to_all x1, starting transfers between devices: 11.6 us -> 4.88 us  [local(): parts = lax.all_to_all(share, ('slab', 'rep'), 0, 0).astype(F32)]
    all_to_all x1, starting transfers between devices: 3.7 us -> 8.3 us  [local(): returned = lax.all_to_all(terms, 'slab', 0, 0)]
    pallas_call x7 -> x5, Pallas kernels: 8.93 us -> 8.88 us  [call(): pl.pallas_call(kernel, out_shape=tuple(outs), in_specs=specs or [VMEM] *...]
  transfers between devices with their start and end apart: 11 -> 7, of which waited for: 10 -> 7; matrix products, arithmetic and copies ran while one was open for 0% -> 0% of each run, Pallas kernels for 1% -> 1%
where the time goes in v3:
time: 84.7 us; the launch traced here: 84.3 us
  waiting for transfers between devices  32.6 us (38%)
  starting transfers between devices  25 us (30%)
  blocking collectives  14.5 us (17%)
  Pallas kernels  8.88 us (10%)
  local copies, waits for them, and re-layouts  1.8 us (2%)
  other arithmetic  0.87 us (1%)
    all_to_all x1, blocking collectives, local(): lax.all_to_all(sums.reshape(plane, 512 // plane, CELLS), ('slab', 'rep'),...  14.5 us
    ppermute x1, waiting for transfers between devices, local(): sums = lax.ppermute(sums, everyone, mirrored)  12.2 us
    pallas_call x5, Pallas kernels, call(): pl.pallas_call(kernel, out_shape=tuple(outs), in_specs=specs or [VMEM] *...  8.88 us
    ppermute x1, waiting for transfers between devices, local(): same = lax.ppermute(by_tap, everyone, mirrored)  8.84 us
    all_to_all x1, starting transfers between devices, local(): returned = lax.all_to_all(terms, 'slab', 0, 0)  8.3 us
    all_to_all x1, waiting for transfers between devices, local(): parts = lax.all_to_all(share, ('slab', 'rep'), 0, 0).astype(F32)  6.19 us
    all_to_all x1, starting transfers between devices, local(): gathered = lax.all_to_all(packed, 'slab', 0, 0)  6.06 us
    all_to_all x1, starting transfers between devices, local(): parts = lax.all_to_all(share, ('slab', 'rep'), 0, 0).astype(F32)  4.88 us
  transfers between devices with their start and end apart: 7, of which 7 were waited for; matrix products, arithmetic and copies ran while one was open for 0% of the time, Pallas kernels for 1%

profile of v3, /device:TPU:2, one launch (start us, length us, event | category | flops | bytes accessed | tf_op | source)
XLA Modules:
  0.0 84.3 jit_solution(8266388725050569061)
XLA Ops:
  0.6 0.0 copy-start
  0.7 0.9 %copy-done = bf16[1,4,8,8,256]{4,3,2,1,0:T(8,128)(2,1)S(1)} copy-done((bf16[1,4,8,8,256]{4,3,2,1,0:T(8,128)(2,1)S(1)}, bf16[1,4,8,8,256]{4,3,2,1,0:T(8,128)(2,1)}, u32[]{:S(2)}) %copy-start) | copy-done | bytes 131096
  1.6 0.9 %copy-done.1 = bf16[1,4,8,8,256]{4,3,2,1,0:T(8,128)(2,1)S(1)} copy-done((bf16[1,4,8,8,256]{4,3,2,1,0:T(8,128)(2,1)S(1)}, bf16[1,4,8,8,256]{4,3,2,1,0:T(8,128)(2,1)}, u32[]{:S(2)}) %copy-start.1) | copy-done | bytes 131096
  2.5 1.1 %shard_map.58 = bf16[8,288,256]{2,1,0:T(8,128)(2,1)} custom-call(s32[1]{0:T(128)} %bitcast.chip_ref, bf16[256,256]{1,0:T(8,128)(2,1)S(1)} %bitcast.12, bf16[256,256]{1,0:T(8,128)(2,1)S(1)} %bitcast.13), custom_call_target="tpu_custom_call" | custom-call | bytes 1441796 | tf_op jit(solution)/shard_map/pallas_call | solution.py:191
  3.6 6.1 %all-to-all-start = ((bf16[8,288,256]{2,1,0:T(8,128)(2,1)}), bf16[8,288,256]{2,1,0:T(8,128)(2,1)S(1)}, u32[]{:S(2)}, u32[]{:S(2)}) async-start(bf16[8,288,256]{2,1,0:T(8,128)(2,1)} %shard_map.58), calls=%async_computation | async-start | bytes 2359296 | tf_op jit(solution)/shard_map/all_to_all | solution.py:235
  9.7 3.8 %collective-permute-start = (bf16[27,16,256]{2,1,0:T(8,128)(2,1)S(1)}, bf16[27,16,256]{2,1,0:T(8,128)(2,1)S(1)}, u32[]{:S(2)}, u32[]{:S(2)}) collective-permute-start(bf16[27,16,256]{2,1,0:T(8,128)(2,1)S(1)} %bitcast.15), channel_id=1, source_target_pairs={{0,0},{1,1},{2,34},{3,35},{4,68},{5,69},{6,102},{7,103},{8,136},{9... | collective-permute-start | bytes 663560 | tf_op jit(solution)/shard_map/ppermute | solution.py:225
  13.5 8.8 %collective-permute-done.same_ref = bf16[27,16,256]{2,1,0:T(8,128)(2,1)S(1)} collective-permute-done((bf16[27,16,256]{2,1,0:T(8,128)(2,1)S(1)}, bf16[27,16,256]{2,1,0:T(8,128)(2,1)S(1)}, u32[]{:S(2)}, u32[]{:S(2)}) %collective-permute-start) | collective-permute-done | bytes 221216 | tf_op jit(solution)/shard_map/ppermute | solution.py:225
  22.3 0.0 collective-permute-start.1
  22.3 1.5 %collective-permute-done.1.opposite_ref = bf16[27,16,256]{2,1,0:T(8,128)(2,1)S(1)} collective-permute-done((bf16[27,16,256]{2,1,0:T(8,128)(2,1)S(1)}, bf16[27,16,256]{2,1,0:T(8,128)(2,1)S(1)}, u32[]{:S(2)}, u32[]{:S(2)}) %collective-permute-start.1) | collective-permute-done | bytes 221216 | tf_op jit(solution)/shard_map/ppermute | solution.py:226
  23.8 1.8 %all-to-all-done.r_ref = bf16[8,288,256]{2,1,0:T(8,128)(2,1)S(1)} async-done(((bf16[8,288,256]{2,1,0:T(8,128)(2,1)}), bf16[8,288,256]{2,1,0:T(8,128)(2,1)S(1)}, u32[]{:S(2)}, u32[]{:S(2)}) %all-to-all-start) | async-done | bytes 1179680 | tf_op jit(solution)/shard_map/all_to_all | solution.py:235
  25.6 6.0 %shard_map.59 = (bf16[8,288,256]{2,1,0:T(8,128)(2,1)}, f32[432,256]{1,0:T(8,128)S(1)}, f32[432,256]{1,0:T(8,128)S(1)}) custom-call(s32[1]{0:T(128)} %bitcast.1.core_ref, bf16[8,288,256]{2,1,0:T(8,128)(2,1)S(1)} %all-to-all-done.r_ref, bf16[27,16,256]{2,1,0:T(8,128)(2,1)S(1)} %collective-permute-done.same_ref, ...), custom_call_target="tpu_custom_call" | custom-call | flops 2818572288 | bytes 3686404 | tf_op jit(solution)/shard_map/pallas_call | solution.py:191
  31.7 8.3 %all-to-all-start.1 = ((bf16[8,288,256]{2,1,0:T(8,128)(2,1)}), bf16[8,288,256]{2,1,0:T(8,128)(2,1)S(1)}, u32[]{:S(2)}, u32[]{:S(2)}) async-start(bf16[8,288,256]{2,1,0:T(8,128)(2,1)} %get-tuple-element.8), calls=%async_computation.1 | async-start | bytes 2359296 | tf_op jit(solution)/shard_map/all_to_all | solution.py:253
  40.0 0.0 collective-permute-start.2
  40.0 1.8 %collective-permute-done.2 = f32[432,256]{1,0:T(8,128)S(1)} collective-permute-done((f32[432,256]{1,0:T(8,128)S(1)}, f32[432,256]{1,0:T(8,128)S(1)}, u32[]{:S(2)}, u32[]{:S(2)}) %collective-permute-start.2) | collective-permute-done | bytes 442400 | tf_op jit(solution)/shard_map/ppermute | solution.py:261
  41.7 0.1 add_convert_fusion
  41.8 1.9 %collective-permute-start.3 = (bf16[432,256]{1,0:T(8,128)(2,1)S(1)}, bf16[432,256]{1,0:T(8,128)(2,1)S(1)}, u32[]{:S(2)}, u32[]{:S(2)}) collective-permute-start(bf16[432,256]{1,0:T(8,128)(2,1)S(1)} %add_convert_fusion), channel_id=1, source_target_pairs={{0,0},{1,1},{2,34},{3,35},{4,68},{5,69},{6,102},{7,103},{8,136},{9... | collective-permute-start | bytes 663560 | tf_op jit(solution)/shard_map/ppermute | solution.py:262
  43.7 12.2 %collective-permute-done.3.rows_ref = bf16[432,256]{1,0:T(8,128)(2,1)S(1)} collective-permute-done((bf16[432,256]{1,0:T(8,128)(2,1)S(1)}, bf16[432,256]{1,0:T(8,128)(2,1)S(1)}, u32[]{:S(2)}, u32[]{:S(2)}) %collective-permute-start.3) | collective-permute-done | bytes 221216 | tf_op jit(solution)/shard_map/ppermute | solution.py:262
  55.9 0.3 all-to-all-done.1.r_ref.after_ref
  56.2 14.5 %all_to_all.20.parts_ref = bf16[16,32,256]{2,1,0:T(8,128)(2,1)S(1)} all-to-all(bf16[16,32,256]{2,1,0:T(8,128)(2,1)S(1)} %bitcast.11), channel_id=1, replica_groups=mesh['fsdp'=16,'slab'=8,'rep'=2] {'slab','rep'}, dimensions={0} | all-to-all | bytes 524288 | tf_op jit(solution)/shard_map/all_to_all | solution.py:270
  70.7 0.8 shard_map.62
  71.5 4.9 %all-to-all-start.3 = ((bf16[16,32,256]{2,1,0:T(8,128)(2,1)}), bf16[16,32,256]{2,1,0:T(8,128)(2,1)S(1)}, u32[]{:S(2)}, u32[]{:S(2)}) async-start(bf16[16,32,256]{2,1,0:T(8,128)(2,1)} %shard_map.62), calls=%async_computation.3 | async-start | bytes 524288 | tf_op jit(solution)/shard_map/all_to_all | solution.py:274
  76.4 0.9 %shard_map.60 = (bf16[256,256]{1,0:T(8,128)(2,1)}, bf16[256,256]{1,0:T(8,128)(2,1)}) custom-call(s32[1]{0:T(128)} %bitcast.chip_ref, bf16[8,288,256]{2,1,0:T(8,128)(2,1)S(1)} %all-to-all-done.1.r_ref.after_ref), custom_call_target="tpu_custom_call" | custom-call | bytes 1441796 | tf_op jit(solution)/shard_map/pallas_call | solution.py:191
  77.3 6.2 %all-to-all-done.3 = bf16[16,32,256]{2,1,0:T(8,128)(2,1)S(1)} async-done(((bf16[16,32,256]{2,1,0:T(8,128)(2,1)}), bf16[16,32,256]{2,1,0:T(8,128)(2,1)S(1)}, u32[]{:S(2)}, u32[]{:S(2)}) %all-to-all-start.3) | async-done | bytes 262176 | tf_op jit(solution)/shard_map/all_to_all | solution.py:274
  83.5 0.8 multiply_bitcast_fusion
  (4 shorter events, 0.0 us)
Async XLA Ops:
  0.6 0.9 %copy-start = (bf16[1,4,8,8,256]{4,3,2,1,0:T(8,128)(2,1)S(1)}, bf16[1,4,8,8,256]{4,3,2,1,0:T(8,128)(2,1)}, u32[]{:S(2)}) copy-start(bf16[1,4,8,8,256]{4,3,2,1,0:T(8,128)(2,1)} %param.3) | copy-start | bytes 393220
  1.5 0.9 %copy-start.1 = (bf16[1,4,8,8,256]{4,3,2,1,0:T(8,128)(2,1)S(1)}, bf16[1,4,8,8,256]{4,3,2,1,0:T(8,128)(2,1)}, u32[]{:S(2)}) copy-start(bf16[1,4,8,8,256]{4,3,2,1,0:T(8,128)(2,1)} %param.5) | copy-start | bytes 393220
  3.6 6.1 %copy-start.2 = (bf16[16,27,256]{2,0,1:T(8,128)(2,1)S(1)}, bf16[16,27,256]{2,0,1:T(8,128)(2,1)}, u32[]{:S(2)}) copy-start(bf16[16,27,256]{2,0,1:T(8,128)(2,1)} %param.4) | copy-start | bytes 663556
  3.6 22.0 %all-to-all-start = ((bf16[8,288,256]{2,1,0:T(8,128)(2,1)}), bf16[8,288,256]{2,1,0:T(8,128)(2,1)S(1)}, u32[]{:S(2)}, u32[]{:S(2)}) async-start(bf16[8,288,256]{2,1,0:T(8,128)(2,1)} %shard_map.58), calls=%async_computation | async-start | bytes 2359296 | tf_op jit(solution)/shard_map/all_to_all | solution.py:235
  9.7 12.7 %collective-permute-start = (bf16[27,16,256]{2,1,0:T(8,128)(2,1)S(1)}, bf16[27,16,256]{2,1,0:T(8,128)(2,1)S(1)}, u32[]{:S(2)}, u32[]{:S(2)}) collective-permute-start(bf16[27,16,256]{2,1,0:T(8,128)(2,1)S(1)} %bitcast.15), channel_id=1, source_target_pairs={{0,0},{1,1},{2,34},{3,35},{4,68},{5,69},{6,102},{7,103},{8,136},{9... | collective-permute-start | bytes 663560 | tf_op jit(solution)/shard_map/ppermute | solution.py:225
  22.3 1.5 %collective-permute-start.1 = (bf16[27,16,256]{2,1,0:T(8,128)(2,1)S(1)}, bf16[27,16,256]{2,1,0:T(8,128)(2,1)S(1)}, u32[]{:S(2)}, u32[]{:S(2)}) collective-permute-start(bf16[27,16,256]{2,1,0:T(8,128)(2,1)S(1)} %collective-permute-done.same_ref), channel_id=1, source_target_pairs={{0,16},{16,0},{32,48},{48,32},{64,80},{80,64},{96,112},{112,96},{1... | collective-permute-start | bytes 663560 | tf_op jit(solution)/shard_map/ppermute | solution.py:226
  31.7 24.6 %all-to-all-start.1 = ((bf16[8,288,256]{2,1,0:T(8,128)(2,1)}), bf16[8,288,256]{2,1,0:T(8,128)(2,1)S(1)}, u32[]{:S(2)}, u32[]{:S(2)}) async-start(bf16[8,288,256]{2,1,0:T(8,128)(2,1)} %get-tuple-element.8), calls=%async_computation.1 | async-start | bytes 2359296 | tf_op jit(solution)/shard_map/all_to_all | solution.py:253
  40.0 1.8 %collective-permute-start.2 = (f32[432,256]{1,0:T(8,128)S(1)}, f32[432,256]{1,0:T(8,128)S(1)}, u32[]{:S(2)}, u32[]{:S(2)}) collective-permute-start(f32[432,256]{1,0:T(8,128)S(1)} %get-tuple-element.12), channel_id=1, source_target_pairs={{0,16},{16,0},{32,48},{48,32},{64,80},{80,64},{96,112},{112,96},{1... | collective-permute-start | bytes 1327112 | tf_op jit(solution)/shard_map/ppermute | solution.py:261
  41.8 14.1 %collective-permute-start.3 = (bf16[432,256]{1,0:T(8,128)(2,1)S(1)}, bf16[432,256]{1,0:T(8,128)(2,1)S(1)}, u32[]{:S(2)}, u32[]{:S(2)}) collective-permute-start(bf16[432,256]{1,0:T(8,128)(2,1)S(1)} %add_convert_fusion), channel_id=1, source_target_pairs={{0,0},{1,1},{2,34},{3,35},{4,68},{5,69},{6,102},{7,103},{8,136},{9... | collective-permute-start | bytes 663560 | tf_op jit(solution)/shard_map/ppermute | solution.py:262
  71.5 12.0 %all-to-all-start.3 = ((bf16[16,32,256]{2,1,0:T(8,128)(2,1)}), bf16[16,32,256]{2,1,0:T(8,128)(2,1)S(1)}, u32[]{:S(2)}, u32[]{:S(2)}) async-start(bf16[16,32,256]{2,1,0:T(8,128)(2,1)} %shard_map.62), calls=%async_computation.3 | async-start | bytes 524288 | tf_op jit(solution)/shard_map/all_to_all | solution.py:274

commit v4 on v3

--- a/solution.py
+++ b/solution.py
@@ -21,12 +21,37 @@
     return (along_x * 3 + along_y) * 3 + along_z
 
 
-def pack_kernel(chip_ref, x_ref, u_ref, out_ref):
-    turned = jnp.transpose(u_ref[...].astype(F32)).astype(BF16)
-    for slab in range(SLABS):
-        out_ref[slab, :CELLS, :] = x_ref[...]
+def home(pair, core, chip):
+    return (pair + 4 * core + chip) & 7
+
+
+def pack_kernel(chip_ref, x_ref, u_ref, out_ref, x_own, u_own, turned, sems):
+    take_u = pltpu.make_async_copy(u_ref, u_own, sems.at[0])
+    take_x = pltpu.make_async_copy(x_ref, x_own, sems.at[1])
+    take_u.start()
+    take_x.start()
+    take_x.wait()
+    copies = [
+        pltpu.make_async_copy(x_own, out_ref.at[slab, pl.ds(0, CELLS), :], sems.at[2 + slab])
+        for slab in range(SLABS)
+    ]
+    for copy in copies:
+        copy.start()
+    take_u.wait()
+    by_out = jnp.transpose(u_own[...].astype(F32)).astype(BF16)
     for pair in range(SLABS):
-        out_ref[(pair + chip_ref[0]) & 7, CELLS:, :] = turned[pair * OUTS : (pair + 1) * OUTS]
+        for core in range(2):
+            start = pair * OUTS + core * 16
+            turned[home(pair, core, chip_ref[0]), core * 16 : core * 16 + 16, :] = by_out[
+                start : start + 16
+            ]
+    last = pltpu.make_async_copy(
+        turned, out_ref.at[:, pl.ds(CELLS, OUTS), :], sems.at[2 + SLABS]
+    )
+    last.start()
+    for copy in copies:
+        copy.wait()
+    last.wait()
 
 
 def lane_masks():
@@ -168,8 +193,13 @@
         turned = jnp.transpose(
             jnp.concatenate(
                 [
-                    r_ref[(pair + chip_ref[0]) & 7, CELLS:, :].astype(F32)
+                    r_ref[
+                        home(pair, core, chip_ref[0]),
+                        CELLS + core * 16 : CELLS + core * 16 + 16,
+                        :,
+                    ].astype(F32)
                     for pair in range(half * 4, half * 4 + 4)
+                    for core in range(2)
                 ],
                 axis=0,
             )
@@ -179,22 +209,23 @@
 
 VMEM = pl.BlockSpec(memory_space=pltpu.VMEM)
 SMEM = pl.BlockSpec(memory_space=pltpu.SMEM)
-PARAMS = pltpu.CompilerParams(vmem_limit_bytes=48 * 1024 * 1024)
+ANY = pl.BlockSpec(memory_space=pl.ANY)
+HBM = pl.BlockSpec(memory_space=pltpu.HBM)
 
 
 def shape(*dims, dtype=BF16):
     return jax.ShapeDtypeStruct(dims, dtype)
 
 
-def call(kernel, outs, operands, specs=None, scratch=(), flops=0):
+def call(kernel, outs, operands, specs=None, scratch=(), flops=0, out_spec=VMEM, vmem=48):
     moved = sum(a.size * a.dtype.itemsize for a in list(operands) + list(outs))
     return pl.pallas_call(
         kernel,
         out_shape=tuple(outs),
         in_specs=specs or [VMEM] * len(operands),
-        out_specs=tuple(VMEM for _ in outs),
+        out_specs=tuple(out_spec for _ in outs),
         scratch_shapes=list(scratch),
-        compiler_params=PARAMS,
+        compiler_params=pltpu.CompilerParams(vmem_limit_bytes=vmem * 1024 * 1024),
         cost_estimate=pl.CostEstimate(flops=flops, bytes_accessed=moved, transcendentals=0),
     )(*operands)
 
@@ -213,7 +244,7 @@
 
     everyone = ("fsdp", "slab", "rep")
     mirrored = [
-        (place(z, core, y, rep), place((y - z) % SLABS, core, y, rep))
+        (place(z, core, y, rep), place((y + 4 * core - z) % SLABS, core, y, rep))
         for z in range(chips)
         for core in range(2)
         for y in range(SLABS)
@@ -230,7 +261,15 @@
         pack_kernel,
         [shape(SLABS, CELLS + OUTS, CELLS)],
         (chip, cells, upstream.reshape(CELLS, CELLS)),
-        specs=[SMEM, VMEM, VMEM],
+        specs=[SMEM, HBM, HBM],
+        scratch=[
+            pltpu.VMEM((CELLS, CELLS), BF16),
+            pltpu.VMEM((CELLS, CELLS), BF16),
+            pltpu.VMEM((SLABS, OUTS, CELLS), BF16),
+            pltpu.SemaphoreType.DMA((3 + SLABS,)),
+        ],
+        out_spec=HBM,
+        vmem=56,
     )[0]
     gathered = lax.all_to_all(packed, "slab", 0, 0)
 
@@ -265,7 +304,7 @@
         lengthen_kernel,
         [shape(512, CELLS)],
         (sums, returned),
-        specs=[VMEM, pl.BlockSpec(memory_space=pl.ANY)],
+        specs=[VMEM, ANY],
     )[0]
     scattered = lax.all_to_all(
         sums.reshape(plane, 512 // plane, CELLS), ("slab", "rep"), 0, 0

time: 84.7 us -> 84.3 us (level)
  waiting for transfers between devices: 32.6 us -> 27.6 us
  starting transfers between devices: 25 us -> 28.9 us
  local copies, waits for them, and re-layouts: 1.8 us -> 0.01 us
  blocking collectives: 14.5 us -> 16 us
  Pallas kernels: 8.88 us -> 9.82 us
    ppermute x1, waiting for transfers between devices: 12.2 us -> 4.41 us  [local(): sums = lax.ppermute(sums, everyone, mirrored)]
    all_to_all x1, waiting for transfers between devices: 0.29 us -> 6.54 us  [local(): returned = lax.all_to_all(terms, 'slab', 0, 0)]
    ppermute x1, waiting for transfers between devices: 8.84 us -> 3.99 us  [local(): same = lax.ppermute(by_tap, everyone, mirrored)]
    ppermute x1, starting transfers between devices: 0.01 us -> 3.47 us  [local(): opposite = lax.ppermute(same, 'fsdp', cores)]
    unnamed x6 -> x2, local copies, waits for them, and re-layouts: 1.8 us -> 0.01 us
    all_to_all x1, waiting for transfers between devices: 1.79 us -> 3.54 us  [local(): gathered = lax.all_to_all(packed, 'slab', 0, 0)]
    ppermute x1, starting transfers between devices: 1.92 us -> 3.41 us  [local(): sums = lax.ppermute(sums, everyone, mirrored)]
    all_to_all x1, blocking collectives: 14.5 us -> 16 us  [local(): lax.all_to_all(sums.reshape(plane, 512 // plane, CELLS), ('slab', 'rep'),...]
where the time goes in v4:
time: 84.3 us; the launch traced here: 83.9 us
  starting transfers between devices  28.9 us (34%)
  waiting for transfers between devices  27.6 us (33%)
  blocking collectives  16 us (19%)
  Pallas kernels  9.82 us (12%)
  other arithmetic  0.87 us (1%)
    all_to_all x1, blocking collectives, local(): lax.all_to_all(sums.reshape(plane, 512 // plane, CELLS), ('slab', 'rep'),...  16 us
    pallas_call x5, Pallas kernels, call(): pl.pallas_call(kernel, out_shape=tuple(outs), in_specs=specs or [VMEM] *...  9.82 us
    all_to_all x1, starting transfers between devices, local(): returned = lax.all_to_all(terms, 'slab', 0, 0)  7.29 us
    all_to_all x1, waiting for transfers between devices, local(): returned = lax.all_to_all(terms, 'slab', 0, 0)  6.54 us
    all_to_all x1, waiting for transfers between devices, local(): parts = lax.all_to_all(share, ('slab', 'rep'), 0, 0).astype(F32)  6.19 us
    all_to_all x1, starting transfers between devices, local(): gathered = lax.all_to_all(packed, 'slab', 0, 0)  6.07 us
    all_to_all x1, starting transfers between devices, local(): parts = lax.all_to_all(share, ('slab', 'rep'), 0, 0).astype(F32)  4.88 us
    ppermute x1, waiting for transfers between devices, local(): sums = lax.ppermute(sums, everyone, mirrored)  4.41 us
  transfers between devices with their start and end apart: 7, of which 7 were waited for; matrix products, arithmetic and copies ran while one was open for 0% of the time, Pallas kernels for 1%

profile of v4, /device:TPU:2, one launch (start us, length us, event | category | flops | bytes accessed | tf_op | source)
XLA Modules:
  0.0 83.9 jit_solution(2730594707962175739)
XLA Ops:
  0.6 2.1 %shard_map.58 = bf16[8,288,256]{2,1,0:T(8,128)(2,1)} custom-call(s32[1]{0:T(128)} %bitcast.chip_ref, bf16[256,256]{1,0:T(8,128)(2,1)} %bitcast.13, bf16[256,256]{1,0:T(8,128)(2,1)} %bitcast.14), custom_call_target="tpu_custom_call" | custom-call | bytes 1441796 | tf_op jit(solution)/shard_map/pallas_call | solution.py:222
  2.7 0.0 copy-start
  2.8 6.1 %all-to-all-start = ((bf16[8,288,256]{2,1,0:T(8,128)(2,1)}), bf16[8,288,256]{2,1,0:T(8,128)(2,1)S(1)}, u32[]{:S(2)}, u32[]{:S(2)}) async-start(bf16[8,288,256]{2,1,0:T(8,128)(2,1)} %shard_map.58), calls=%async_computation | async-start | bytes 2359296 | tf_op jit(solution)/shard_map/all_to_all | solution.py:274
  8.8 0.0 copy-done
  8.8 3.8 %collective-permute-start = (bf16[27,16,256]{2,1,0:T(8,128)(2,1)S(1)}, bf16[27,16,256]{2,1,0:T(8,128)(2,1)S(1)}, u32[]{:S(2)}, u32[]{:S(2)}) collective-permute-start(bf16[27,16,256]{2,1,0:T(8,128)(2,1)S(1)} %bitcast.15), channel_id=1, source_target_pairs={{0,0},{1,1},{2,34},{3,35},{4,68},{5,69},{6,102},{7,103},{8,136},{9... | collective-permute-start | bytes 663560 | tf_op jit(solution)/shard_map/ppermute | solution.py:256
  12.7 4.0 %collective-permute-done.same_ref = bf16[27,16,256]{2,1,0:T(8,128)(2,1)S(1)} collective-permute-done((bf16[27,16,256]{2,1,0:T(8,128)(2,1)S(1)}, bf16[27,16,256]{2,1,0:T(8,128)(2,1)S(1)}, u32[]{:S(2)}, u32[]{:S(2)}) %collective-permute-start) | collective-permute-done | bytes 221216 | tf_op jit(solution)/shard_map/ppermute | solution.py:256
  16.6 3.5 %collective-permute-start.1 = (bf16[27,16,256]{2,1,0:T(8,128)(2,1)S(1)}, bf16[27,16,256]{2,1,0:T(8,128)(2,1)S(1)}, u32[]{:S(2)}, u32[]{:S(2)}) collective-permute-start(bf16[27,16,256]{2,1,0:T(8,128)(2,1)S(1)} %collective-permute-done.same_ref), channel_id=1, source_target_pairs={{0,16},{16,0},{32,48},{48,32},{64,80},{80,64},{96,112},{112,96},{1... | collective-permute-start | bytes 663560 | tf_op jit(solution)/shard_map/ppermute | solution.py:257
  20.1 1.1 %collective-permute-done.1.opposite_ref = bf16[27,16,256]{2,1,0:T(8,128)(2,1)S(1)} collective-permute-done((bf16[27,16,256]{2,1,0:T(8,128)(2,1)S(1)}, bf16[27,16,256]{2,1,0:T(8,128)(2,1)S(1)}, u32[]{:S(2)}, u32[]{:S(2)}) %collective-permute-start.1) | collective-permute-done | bytes 221216 | tf_op jit(solution)/shard_map/ppermute | solution.py:257
  21.2 3.5 %all-to-all-done.r_ref = bf16[8,288,256]{2,1,0:T(8,128)(2,1)S(1)} async-done(((bf16[8,288,256]{2,1,0:T(8,128)(2,1)}), bf16[8,288,256]{2,1,0:T(8,128)(2,1)S(1)}, u32[]{:S(2)}, u32[]{:S(2)}) %all-to-all-start) | async-done | bytes 1179680 | tf_op jit(solution)/shard_map/all_to_all | solution.py:274
  24.8 6.0 %shard_map.59 = (bf16[8,288,256]{2,1,0:T(8,128)(2,1)}, f32[432,256]{1,0:T(8,128)S(1)}, f32[432,256]{1,0:T(8,128)S(1)}) custom-call(s32[1]{0:T(128)} %bitcast.1.core_ref, bf16[8,288,256]{2,1,0:T(8,128)(2,1)S(1)} %all-to-all-done.r_ref, bf16[27,16,256]{2,1,0:T(8,128)(2,1)S(1)} %collective-permute-done.same_ref, ...), custom_call_target="tpu_custom_call" | custom-call | flops 2818572288 | bytes 3686404 | tf_op jit(solution)/shard_map/pallas_call | solution.py:222
  30.8 7.3 %all-to-all-start.1 = ((bf16[8,288,256]{2,1,0:T(8,128)(2,1)}), bf16[8,288,256]{2,1,0:T(8,128)(2,1)S(1)}, u32[]{:S(2)}, u32[]{:S(2)}) async-start(bf16[8,288,256]{2,1,0:T(8,128)(2,1)} %get-tuple-element.8), calls=%async_computation.1 | async-start | bytes 2359296 | tf_op jit(solution)/shard_map/all_to_all | solution.py:292
  38.1 0.0 collective-permute-start.2
  38.1 1.8 %collective-permute-done.2 = f32[432,256]{1,0:T(8,128)S(1)} collective-permute-done((f32[432,256]{1,0:T(8,128)S(1)}, f32[432,256]{1,0:T(8,128)S(1)}, u32[]{:S(2)}, u32[]{:S(2)}) %collective-permute-start.2) | collective-permute-done | bytes 442400 | tf_op jit(solution)/shard_map/ppermute | solution.py:300
  39.9 0.1 add_convert_fusion
  40.0 3.4 %collective-permute-start.3 = (bf16[432,256]{1,0:T(8,128)(2,1)S(1)}, bf16[432,256]{1,0:T(8,128)(2,1)S(1)}, u32[]{:S(2)}, u32[]{:S(2)}) collective-permute-start(bf16[432,256]{1,0:T(8,128)(2,1)S(1)} %add_convert_fusion), channel_id=1, source_target_pairs={{0,0},{1,1},{2,34},{3,35},{4,68},{5,69},{6,102},{7,103},{8,136},{9... | collective-permute-start | bytes 663560 | tf_op jit(solution)/shard_map/ppermute | solution.py:301
  43.4 4.4 %collective-permute-done.3.rows_ref = bf16[432,256]{1,0:T(8,128)(2,1)S(1)} collective-permute-done((bf16[432,256]{1,0:T(8,128)(2,1)S(1)}, bf16[432,256]{1,0:T(8,128)(2,1)S(1)}, u32[]{:S(2)}, u32[]{:S(2)}) %collective-permute-start.3) | collective-permute-done | bytes 221216 | tf_op jit(solution)/shard_map/ppermute | solution.py:301
  47.8 6.5 %all-to-all-done.1.r_ref.after_ref = bf16[8,288,256]{2,1,0:T(8,128)(2,1)S(1)} async-done(((bf16[8,288,256]{2,1,0:T(8,128)(2,1)}), bf16[8,288,256]{2,1,0:T(8,128)(2,1)S(1)}, u32[]{:S(2)}, u32[]{:S(2)}) %all-to-all-start.1) | async-done | bytes 1179680 | tf_op jit(solution)/shard_map/all_to_all | solution.py:292
  54.4 16.0 %all_to_all.20.parts_ref = bf16[16,32,256]{2,1,0:T(8,128)(2,1)S(1)} all-to-all(bf16[16,32,256]{2,1,0:T(8,128)(2,1)S(1)} %bitcast.11), channel_id=1, replica_groups=mesh['fsdp'=16,'slab'=8,'rep'=2] {'slab','rep'}, dimensions={0} | all-to-all | bytes 524288 | tf_op jit(solution)/shard_map/all_to_all | solution.py:309
  70.3 0.8 shard_map.62
  71.1 4.9 %all-to-all-start.3 = ((bf16[16,32,256]{2,1,0:T(8,128)(2,1)}), bf16[16,32,256]{2,1,0:T(8,128)(2,1)S(1)}, u32[]{:S(2)}, u32[]{:S(2)}) async-start(bf16[16,32,256]{2,1,0:T(8,128)(2,1)} %shard_map.62), calls=%async_computation.3 | async-start | bytes 524288 | tf_op jit(solution)/shard_map/all_to_all | solution.py:313
  76.0 0.9 %shard_map.60 = (bf16[256,256]{1,0:T(8,128)(2,1)}, bf16[256,256]{1,0:T(8,128)(2,1)}) custom-call(s32[1]{0:T(128)} %bitcast.chip_ref, bf16[8,288,256]{2,1,0:T(8,128)(2,1)S(1)} %all-to-all-done.1.r_ref.after_ref), custom_call_target="tpu_custom_call" | custom-call | bytes 1441796 | tf_op jit(solution)/shard_map/pallas_call | solution.py:222
  76.9 6.2 %all-to-all-done.3 = bf16[16,32,256]{2,1,0:T(8,128)(2,1)S(1)} async-done(((bf16[16,32,256]{2,1,0:T(8,128)(2,1)}), bf16[16,32,256]{2,1,0:T(8,128)(2,1)S(1)}, u32[]{:S(2)}, u32[]{:S(2)}) %all-to-all-start.3) | async-done | bytes 262176 | tf_op jit(solution)/shard_map/all_to_all | solution.py:313
  83.1 0.8 multiply_bitcast_fusion
  (1 shorter events, 0.0 us)
Async XLA Ops:
  2.7 6.1 %copy-start = (bf16[16,27,256]{2,0,1:T(8,128)(2,1)S(1)}, bf16[16,27,256]{2,0,1:T(8,128)(2,1)}, u32[]{:S(2)}) copy-start(bf16[16,27,256]{2,0,1:T(8,128)(2,1)} %param.4) | copy-start | bytes 663556
  2.8 22.0 %all-to-all-start = ((bf16[8,288,256]{2,1,0:T(8,128)(2,1)}), bf16[8,288,256]{2,1,0:T(8,128)(2,1)S(1)}, u32[]{:S(2)}, u32[]{:S(2)}) async-start(bf16[8,288,256]{2,1,0:T(8,128)(2,1)} %shard_map.58), calls=%async_computation | async-start | bytes 2359296 | tf_op jit(solution)/shard_map/all_to_all | solution.py:274
  8.8 7.8 %collective-permute-start = (bf16[27,16,256]{2,1,0:T(8,128)(2,1)S(1)}, bf16[27,16,256]{2,1,0:T(8,128)(2,1)S(1)}, u32[]{:S(2)}, u32[]{:S(2)}) collective-permute-start(bf16[27,16,256]{2,1,0:T(8,128)(2,1)S(1)} %bitcast.15), channel_id=1, source_target_pairs={{0,0},{1,1},{2,34},{3,35},{4,68},{5,69},{6,102},{7,103},{8,136},{9... | collective-permute-start | bytes 663560 | tf_op jit(solution)/shard_map/ppermute | solution.py:256
  16.6 4.6 %collective-permute-start.1 = (bf16[27,16,256]{2,1,0:T(8,128)(2,1)S(1)}, bf16[27,16,256]{2,1,0:T(8,128)(2,1)S(1)}, u32[]{:S(2)}, u32[]{:S(2)}) collective-permute-start(bf16[27,16,256]{2,1,0:T(8,128)(2,1)S(1)} %collective-permute-done.same_ref), channel_id=1, source_target_pairs={{0,16},{16,0},{32,48},{48,32},{64,80},{80,64},{96,112},{112,96},{1... | collective-permute-start | bytes 663560 | tf_op jit(solution)/shard_map/ppermute | solution.py:257
  30.8 23.5 %all-to-all-start.1 = ((bf16[8,288,256]{2,1,0:T(8,128)(2,1)}), bf16[8,288,256]{2,1,0:T(8,128)(2,1)S(1)}, u32[]{:S(2)}, u32[]{:S(2)}) async-start(bf16[8,288,256]{2,1,0:T(8,128)(2,1)} %get-tuple-element.8), calls=%async_computation.1 | async-start | bytes 2359296 | tf_op jit(solution)/shard_map/all_to_all | solution.py:292
  38.1 1.8 %collective-permute-start.2 = (f32[432,256]{1,0:T(8,128)S(1)}, f32[432,256]{1,0:T(8,128)S(1)}, u32[]{:S(2)}, u32[]{:S(2)}) collective-permute-start(f32[432,256]{1,0:T(8,128)S(1)} %get-tuple-element.12), channel_id=1, source_target_pairs={{0,16},{16,0},{32,48},{48,32},{64,80},{80,64},{96,112},{112,96},{1... | collective-permute-start | bytes 1327112 | tf_op jit(solution)/shard_map/ppermute | solution.py:300
  40.0 7.8 %collective-permute-start.3 = (bf16[432,256]{1,0:T(8,128)(2,1)S(1)}, bf16[432,256]{1,0:T(8,128)(2,1)S(1)}, u32[]{:S(2)}, u32[]{:S(2)}) collective-permute-start(bf16[432,256]{1,0:T(8,128)(2,1)S(1)} %add_convert_fusion), channel_id=1, source_target_pairs={{0,0},{1,1},{2,34},{3,35},{4,68},{5,69},{6,102},{7,103},{8,136},{9... | collective-permute-start | bytes 663560 | tf_op jit(solution)/shard_map/ppermute | solution.py:301
  71.1 12.0 %all-to-all-start.3 = ((bf16[16,32,256]{2,1,0:T(8,128)(2,1)}), bf16[16,32,256]{2,1,0:T(8,128)(2,1)S(1)}, u32[]{:S(2)}, u32[]{:S(2)}) async-start(bf16[16,32,256]{2,1,0:T(8,128)(2,1)} %shard_map.62), calls=%async_computation.3 | async-start | bytes 524288 | tf_op jit(solution)/shard_map/all_to_all | solution.py:313

commit v5 on v4

--- a/solution.py
+++ b/solution.py
@@ -15,6 +15,7 @@
 ROWS = 28 * OUTS
 WHOLE = SLABS * CELLS
 COLUMNS = WHOLE // LANES
+AHEAD = 2 * 10**10
 
 
 def tap_index(along_x, along_y, along_z):
@@ -171,6 +172,14 @@
         ).astype(BF16)
 
 
+def copy_kernel(rows_ref, out_ref):
+    out_ref[...] = rows_ref[...]
+
+
+def add_kernel(own_ref, got_ref, out_ref):
+    out_ref[...] = (own_ref[...] + got_ref[...]).astype(BF16)
+
+
 def lengthen_kernel(rows_ref, after_ref, out_ref):
     out_ref[: TAPS * 16, :] = rows_ref[...]
     out_ref[TAPS * 16 :, :] = jnp.zeros((out_ref.shape[0] - TAPS * 16, CELLS), BF16)
@@ -254,7 +263,8 @@
 
     by_tap = jnp.transpose(weights, (1, 0, 2))
     same = lax.ppermute(by_tap, everyone, mirrored)
-    opposite = lax.ppermute(same, "fsdp", cores)
+    onward = call(copy_kernel, [shape(TAPS, 16, CELLS)], (same,), flops=AHEAD)[0]
+    opposite = lax.ppermute(onward, "fsdp", cores)
 
     cells = inputs.reshape(CELLS, CELLS)
     packed = call(
@@ -297,7 +307,12 @@
         specs=[SMEM, VMEM],
     )
 
-    sums = (own + lax.ppermute(other, "fsdp", cores)).astype(BF16)
+    sums = call(
+        add_kernel,
+        [shape(TAPS * 16, CELLS)],
+        (own, lax.ppermute(other, "fsdp", cores)),
+        flops=AHEAD,
+    )[0]
     sums = lax.ppermute(sums, everyone, mirrored)
     plane = SLABS * reps
     sums = call(

time: 84.3 us -> 86.8 us (1.030)
  waiting for transfers between devices: 27.6 us -> 34.7 us
  blocking collectives: 16 us -> 13.3 us
  starting transfers between devices: 28.9 us -> 27 us
    all_to_all x1, waiting for transfers between devices: 3.54 us -> 12.9 us  [local(): gathered = lax.all_to_all(packed, 'slab', 0, 0)]
    all_to_all x1, starting transfers between devices: 6.07 us -> 10.8 us  [local(): gathered = lax.all_to_all(packed, 'slab', 0, 0)]
    ppermute x1, waiting for transfers between devices: 3.99 us -> 0.01 us  [local(): same = lax.ppermute(by_tap, everyone, mirrored)]
    ppermute x2, starting transfers between devices: 3.48 us -> 0.1 us  [the longest x1 0.09 us: local(): opposite = lax.ppermute(onward, 'fsdp', cores)]
    all_to_all x1, blocking collectives: 16 us -> 13.3 us  [local(): lax.all_to_all(sums.reshape(plane, 512 // plane, CELLS), ('slab', 'rep'),...]
    all_to_all x1, starting transfers between devices: 7.29 us -> 4.7 us  [local(): returned = lax.all_to_all(terms, 'slab', 0, 0)]
    all_to_all x1, waiting for transfers between devices: 6.54 us -> 9 us  [local(): returned = lax.all_to_all(terms, 'slab', 0, 0)]
    ppermute x2, waiting for transfers between devices: 2.89 us -> 1.46 us  [the longest x1 1.45 us: local(): opposite = lax.ppermute(onward, 'fsdp', cores)]
  transfers between devices with their start and end apart: 7 -> 7, of which waited for: 7 -> 5; matrix products, arithmetic and copies ran while one was open for 0% -> 0% of each run, Pallas kernels for 1% -> 4%
where the time goes in v5:
time: 86.8 us; the launch traced here: 86.4 us
  waiting for transfers between devices  34.7 us (40%)
  starting transfers between devices  27 us (31%)
  blocking collectives  13.3 us (15%)
  Pallas kernels  9.94 us (11%)
    all_to_all x1, blocking collectives, local(): lax.all_to_all(sums.reshape(plane, 512 // plane, CELLS), ('slab', 'rep'),...  13.3 us
    all_to_all x1, waiting for transfers between devices, local(): gathered = lax.all_to_all(packed, 'slab', 0, 0)  12.9 us
    all_to_all x1, starting transfers between devices, local(): gathered = lax.all_to_all(packed, 'slab', 0, 0)  10.8 us
    pallas_call x7, Pallas kernels, call(): pl.pallas_call(kernel, out_shape=tuple(outs), in_specs=specs or [VMEM] *...  9.94 us
    all_to_all x1, waiting for transfers between devices, local(): returned = lax.all_to_all(terms, 'slab', 0, 0)  9 us
    all_to_all x1, waiting for transfers between devices, local(): parts = lax.all_to_all(share, ('slab', 'rep'), 0, 0).astype(F32)  6.19 us
    ppermute x1, waiting for transfers between devices, local(): sums = lax.ppermute(sums, everyone, mirrored)  5.12 us
    all_to_all x1, starting transfers between devices, local(): parts = lax.all_to_all(share, ('slab', 'rep'), 0, 0).astype(F32)  4.88 us
  transfers between devices with their start and end apart: 7, of which 5 were waited for; matrix products, arithmetic and copies ran while one was open for 0% of the time, Pallas kernels for 4%

profile of v5, /device:TPU:2, one launch (start us, length us, event | category | flops | bytes accessed | tf_op | source)
XLA Modules:
  0.0 86.4 jit_solution(17407401206613154648)
XLA Ops:
  0.6 3.8 %collective-permute-start = (bf16[27,16,256]{2,1,0:T(8,128)(2,1)}, bf16[27,16,256]{2,1,0:T(8,128)(2,1)S(1)}, u32[]{:S(2)}, u32[]{:S(2)}) collective-permute-start(bf16[27,16,256]{2,1,0:T(8,128)(2,1)} %bitcast.15), channel_id=1, source_target_pairs={{0,0},{1,1},{2,34},{3,35},{4,68},{5,69},{6,102},{7,103},{8,136},{9... | collective-permute-start | bytes 663560 | tf_op jit(solution)/shard_map/ppermute | solution.py:265
  4.5 2.1 %shard_map.58 = bf16[8,288,256]{2,1,0:T(8,128)(2,1)} custom-call(s32[1]{0:T(128)} %bitcast.chip_ref, bf16[256,256]{1,0:T(8,128)(2,1)} %bitcast.13, bf16[256,256]{1,0:T(8,128)(2,1)} %bitcast.14), custom_call_target="tpu_custom_call" | custom-call | bytes 1441796 | tf_op jit(solution)/shard_map/pallas_call | solution.py:231
  6.6 10.8 %all-to-all-start = ((bf16[8,288,256]{2,1,0:T(8,128)(2,1)}), bf16[8,288,256]{2,1,0:T(8,128)(2,1)S(1)}, u32[]{:S(2)}, u32[]{:S(2)}) async-start(bf16[8,288,256]{2,1,0:T(8,128)(2,1)} %shard_map.58), calls=%async_computation | async-start | bytes 2359296 | tf_op jit(solution)/shard_map/all_to_all | solution.py:284
  17.3 0.0 collective-permute-done.rows_ref.same_ref
  17.4 0.1 collective-permute-start.1
  17.5 1.5 %collective-permute-done.1.opposite_ref = bf16[27,16,256]{2,1,0:T(8,128)(2,1)S(1)} collective-permute-done((bf16[27,16,256]{2,1,0:T(8,128)(2,1)S(1)}, bf16[27,16,256]{2,1,0:T(8,128)(2,1)S(1)}, u32[]{:S(2)}, u32[]{:S(2)}) %collective-permute-start.1) | collective-permute-done | bytes 221216 | tf_op jit(solution)/shard_map/ppermute | solution.py:267
  18.9 12.9 %all-to-all-done.r_ref = bf16[8,288,256]{2,1,0:T(8,128)(2,1)S(1)} async-done(((bf16[8,288,256]{2,1,0:T(8,128)(2,1)}), bf16[8,288,256]{2,1,0:T(8,128)(2,1)S(1)}, u32[]{:S(2)}, u32[]{:S(2)}) %all-to-all-start) | async-done | bytes 1179680 | tf_op jit(solution)/shard_map/all_to_all | solution.py:284
  31.8 6.1 %shard_map.60 = (bf16[8,288,256]{2,1,0:T(8,128)(2,1)}, f32[432,256]{1,0:T(8,128)S(1)}, f32[432,256]{1,0:T(8,128)S(1)}) custom-call(s32[1]{0:T(128)} %bitcast.1.core_ref, bf16[8,288,256]{2,1,0:T(8,128)(2,1)S(1)} %all-to-all-done.r_ref, bf16[27,16,256]{2,1,0:T(8,128)(2,1)S(1)} %collective-permute-done.rows_ref.same_ref, ...), custom_call_target="tpu_custom_call" | custom-call | flops 2818572288 | bytes 3686404 | tf_op jit(solution)/shard_map/pallas_call | solution.py:231
  37.9 0.0 collective-permute-start.2
  37.9 4.7 %all-to-all-start.1 = ((bf16[8,288,256]{2,1,0:T(8,128)(2,1)}), bf16[8,288,256]{2,1,0:T(8,128)(2,1)S(1)}, u32[]{:S(2)}, u32[]{:S(2)}) async-start(bf16[8,288,256]{2,1,0:T(8,128)(2,1)} %get-tuple-element.8), calls=%async_computation.1 | async-start | bytes 2359296 | tf_op jit(solution)/shard_map/all_to_all | solution.py:302
  42.6 0.0 collective-permute-done.2.got_ref
  42.6 0.1 shard_map.62
  42.7 2.7 %collective-permute-start.3 = (bf16[432,256]{1,0:T(8,128)(2,1)S(1)}, bf16[432,256]{1,0:T(8,128)(2,1)S(1)}, u32[]{:S(2)}, u32[]{:S(2)}) collective-permute-start(bf16[432,256]{1,0:T(8,128)(2,1)S(1)} %shard_map.62), channel_id=1, source_target_pairs={{0,0},{1,1},{2,34},{3,35},{4,68},{5,69},{6,102},{7,103},{8,136},{9... | collective-permute-start | bytes 663560 | tf_op jit(solution)/shard_map/ppermute | solution.py:316
  45.4 5.1 %collective-permute-done.3.rows_ref = bf16[432,256]{1,0:T(8,128)(2,1)S(1)} collective-permute-done((bf16[432,256]{1,0:T(8,128)(2,1)S(1)}, bf16[432,256]{1,0:T(8,128)(2,1)S(1)}, u32[]{:S(2)}, u32[]{:S(2)}) %collective-permute-start.3) | collective-permute-done | bytes 221216 | tf_op jit(solution)/shard_map/ppermute | solution.py:316
  50.5 9.0 %all-to-all-done.1.r_ref.after_ref = bf16[8,288,256]{2,1,0:T(8,128)(2,1)S(1)} async-done(((bf16[8,288,256]{2,1,0:T(8,128)(2,1)}), bf16[8,288,256]{2,1,0:T(8,128)(2,1)S(1)}, u32[]{:S(2)}, u32[]{:S(2)}) %all-to-all-start.1) | async-done | bytes 1179680 | tf_op jit(solution)/shard_map/all_to_all | solution.py:302
  59.5 13.3 %all_to_all.20.parts_ref = bf16[16,32,256]{2,1,0:T(8,128)(2,1)S(1)} all-to-all(bf16[16,32,256]{2,1,0:T(8,128)(2,1)S(1)} %bitcast.11), channel_id=1, replica_groups=mesh['fsdp'=16,'slab'=8,'rep'=2] {'slab','rep'}, dimensions={0} | all-to-all | bytes 524288 | tf_op jit(solution)/shard_map/all_to_all | solution.py:324
  72.9 0.8 shard_map.64
  73.6 4.9 %all-to-all-start.3 = ((bf16[16,32,256]{2,1,0:T(8,128)(2,1)}), bf16[16,32,256]{2,1,0:T(8,128)(2,1)S(1)}, u32[]{:S(2)}, u32[]{:S(2)}) async-start(bf16[16,32,256]{2,1,0:T(8,128)(2,1)} %shard_map.64), calls=%async_computation.3 | async-start | bytes 524288 | tf_op jit(solution)/shard_map/all_to_all | solution.py:328
  78.5 0.9 %shard_map.61 = (bf16[256,256]{1,0:T(8,128)(2,1)}, bf16[256,256]{1,0:T(8,128)(2,1)}) custom-call(s32[1]{0:T(128)} %bitcast.chip_ref, bf16[8,288,256]{2,1,0:T(8,128)(2,1)S(1)} %all-to-all-done.1.r_ref.after_ref), custom_call_target="tpu_custom_call" | custom-call | bytes 1441796 | tf_op jit(solution)/shard_map/pallas_call | solution.py:231
  79.4 6.2 %all-to-all-done.3 = bf16[16,32,256]{2,1,0:T(8,128)(2,1)S(1)} async-done(((bf16[16,32,256]{2,1,0:T(8,128)(2,1)}), bf16[16,32,256]{2,1,0:T(8,128)(2,1)S(1)}, u32[]{:S(2)}, u32[]{:S(2)}) %all-to-all-start.3) | async-done | bytes 262176 | tf_op jit(solution)/shard_map/all_to_all | solution.py:328
  85.6 0.8 multiply_bitcast_fusion
  (2 shorter events, 0.0 us)
Async XLA Ops:
  0.6 16.7 %collective-permute-start = (bf16[27,16,256]{2,1,0:T(8,128)(2,1)}, bf16[27,16,256]{2,1,0:T(8,128)(2,1)S(1)}, u32[]{:S(2)}, u32[]{:S(2)}) collective-permute-start(bf16[27,16,256]{2,1,0:T(8,128)(2,1)} %bitcast.15), channel_id=1, source_target_pairs={{0,0},{1,1},{2,34},{3,35},{4,68},{5,69},{6,102},{7,103},{8,136},{9... | collective-permute-start | bytes 663560 | tf_op jit(solution)/shard_map/ppermute | solution.py:265
  6.6 25.2 %all-to-all-start = ((bf16[8,288,256]{2,1,0:T(8,128)(2,1)}), bf16[8,288,256]{2,1,0:T(8,128)(2,1)S(1)}, u32[]{:S(2)}, u32[]{:S(2)}) async-start(bf16[8,288,256]{2,1,0:T(8,128)(2,1)} %shard_map.58), calls=%async_computation | async-start | bytes 2359296 | tf_op jit(solution)/shard_map/all_to_all | solution.py:284
  17.4 1.6 %collective-permute-start.1 = (bf16[27,16,256]{2,1,0:T(8,128)(2,1)S(1)}, bf16[27,16,256]{2,1,0:T(8,128)(2,1)S(1)}, u32[]{:S(2)}, u32[]{:S(2)}) collective-permute-start(bf16[27,16,256]{2,1,0:T(8,128)(2,1)S(1)} %shard_map.59), channel_id=1, source_target_pairs={{0,16},{16,0},{32,48},{48,32},{64,80},{80,64},{96,112},{112,96},{1... | collective-permute-start | bytes 663560 | tf_op jit(solution)/shard_map/ppermute | solution.py:267
  37.9 4.7 %collective-permute-start.2 = (f32[432,256]{1,0:T(8,128)S(1)}, f32[432,256]{1,0:T(8,128)S(1)}, u32[]{:S(2)}, u32[]{:S(2)}) collective-permute-start(f32[432,256]{1,0:T(8,128)S(1)} %get-tuple-element.12), channel_id=1, source_target_pairs={{0,16},{16,0},{32,48},{48,32},{64,80},{80,64},{96,112},{112,96},{1... | collective-permute-start | bytes 1327112 | tf_op jit(solution)/shard_map/ppermute | solution.py:313
  37.9 21.6 %all-to-all-start.1 = ((bf16[8,288,256]{2,1,0:T(8,128)(2,1)}), bf16[8,288,256]{2,1,0:T(8,128)(2,1)S(1)}, u32[]{:S(2)}, u32[]{:S(2)}) async-start(bf16[8,288,256]{2,1,0:T(8,128)(2,1)} %get-tuple-element.8), calls=%async_computation.1 | async-start | bytes 2359296 | tf_op jit(solution)/shard_map/all_to_all | solution.py:302
  42.7 7.8 %collective-permute-start.3 = (bf16[432,256]{1,0:T(8,128)(2,1)S(1)}, bf16[432,256]{1,0:T(8,128)(2,1)S(1)}, u32[]{:S(2)}, u32[]{:S(2)}) collective-permute-start(bf16[432,256]{1,0:T(8,128)(2,1)S(1)} %shard_map.62), channel_id=1, source_target_pairs={{0,0},{1,1},{2,34},{3,35},{4,68},{5,69},{6,102},{7,103},{8,136},{9... | collective-permute-start | bytes 663560 | tf_op jit(solution)/shard_map/ppermute | solution.py:316
  73.6 12.0 %all-to-all-start.3 = ((bf16[16,32,256]{2,1,0:T(8,128)(2,1)}), bf16[16,32,256]{2,1,0:T(8,128)(2,1)S(1)}, u32[]{:S(2)}, u32[]{:S(2)}) async-start(bf16[16,32,256]{2,1,0:T(8,128)(2,1)} %shard_map.64), calls=%async_computation.3 | async-start | bytes 524288 | tf_op jit(solution)/shard_map/all_to_all | solution.py:328

commit v6 on v4

--- a/solution.py
+++ b/solution.py
@@ -1,3 +1,5 @@
+import functools
+
 import jax
 import jax.numpy as jnp
 from jax import lax
@@ -12,6 +14,7 @@
 SLABS = 8
 OUTS = 32
 TAPS = 27
+HALF = 14 * 16
 ROWS = 28 * OUTS
 WHOLE = SLABS * CELLS
 COLUMNS = WHOLE // LANES
@@ -156,6 +159,8 @@
         r_ref[:, :CELLS, :].reshape(WHOLE, CELLS),
         preferred_element_type=F32,
     )
+    own_ref[TAPS * 16 :, :] = jnp.zeros((16, CELLS), F32)
+    other_ref[TAPS * 16 :, :] = jnp.zeros((16, CELLS), F32)
     for tap in range(TAPS):
         start = tap * OUTS
         left = whole[start : start + 16]
@@ -171,9 +176,21 @@
         ).astype(BF16)
 
 
+def halve_kernel(rep_ref, own_ref, got_ref, kept_ref, sent_ref):
+    first = rep_ref[0] == 0
+    low = own_ref[:HALF, :] + got_ref[:HALF, :]
+    high = own_ref[HALF:, :] + got_ref[HALF:, :]
+    kept_ref[...] = jnp.where(first, low, high)
+    sent_ref[...] = jnp.where(first, high, low).astype(BF16)
+
+
+def add_kernel(kept_ref, got_ref, out_ref):
+    out_ref[...] = (kept_ref[...] + got_ref[...].astype(F32)).astype(BF16)
+
+
 def lengthen_kernel(rows_ref, after_ref, out_ref):
-    out_ref[: TAPS * 16, :] = rows_ref[...]
-    out_ref[TAPS * 16 :, :] = jnp.zeros((out_ref.shape[0] - TAPS * 16, CELLS), BF16)
+    out_ref[:HALF, :] = rows_ref[...]
+    out_ref[HALF:, :] = jnp.zeros((out_ref.shape[0] - HALF, CELLS), BF16)
 
 
 def share_kernel(parts_ref, out_ref):
@@ -182,6 +199,13 @@
         total = total + parts_ref[place].astype(F32)
     for place in range(out_ref.shape[0]):
         out_ref[place] = total.astype(BF16)
+
+
+def settle_kernel(factor, parts_ref, out_ref):
+    for tap in range(TAPS):
+        rep, place = tap // 14, tap % 14
+        rows = slice(place % 2 * 16, place % 2 * 16 + 16)
+        out_ref[tap] = parts_ref[place // 2 * 2 + rep, rows, :].astype(F32) * factor
 
 
 def final_kernel(chip_ref, r_ref, act_ref, grad_ref):
@@ -234,6 +258,7 @@
     owner = lax.axis_index("fsdp")
     core = (owner % 2).astype(jnp.int32).reshape(1)
     chip = (owner // 2).astype(jnp.int32).reshape(1)
+    rep = lax.axis_index("rep").astype(jnp.int32).reshape(1)
     chips = lax.axis_size("fsdp") // 2
     reps = lax.axis_size("rep")
     total_cells = 2 * chips * reps * WHOLE
@@ -277,8 +302,8 @@
         main_kernel,
         [
             shape(SLABS, CELLS + OUTS, CELLS),
-            shape(TAPS * 16, CELLS, dtype=F32),
-            shape(TAPS * 16, CELLS, dtype=F32),
+            shape(2 * HALF, CELLS, dtype=F32),
+            shape(2 * HALF, CELLS, dtype=F32),
         ],
         (core, gathered, same, opposite),
         specs=[SMEM, VMEM, VMEM, VMEM],
@@ -297,21 +322,25 @@
         specs=[SMEM, VMEM],
     )
 
-    sums = (own + lax.ppermute(other, "fsdp", cores)).astype(BF16)
+    kept, sent = call(
+        halve_kernel,
+        [shape(HALF, CELLS, dtype=F32), shape(HALF, CELLS)],
+        (rep, own, lax.ppermute(other, "fsdp", cores)),
+        specs=[SMEM, VMEM, VMEM],
+    )
+    got = lax.ppermute(sent, "rep", [(0, 1), (1, 0)])
+    sums = call(add_kernel, [shape(HALF, CELLS)], (kept, got))[0]
     sums = lax.ppermute(sums, everyone, mirrored)
-    plane = SLABS * reps
-    sums = call(
-        lengthen_kernel,
-        [shape(512, CELLS)],
-        (sums, returned),
-        specs=[VMEM, ANY],
+    sums = call(lengthen_kernel, [shape(256, CELLS)], (sums, returned), specs=[VMEM, ANY])[0]
+    scattered = lax.all_to_all(sums.reshape(SLABS, 32, CELLS), "slab", 0, 0)
+    share = call(share_kernel, [shape(SLABS * reps, 32, CELLS)], (scattered,))[0]
+    parts = lax.all_to_all(share, ("slab", "rep"), 0, 0)
+    weight_grad = call(
+        functools.partial(settle_kernel, factor),
+        [shape(TAPS, 16, CELLS, dtype=F32)],
+        (parts,),
     )[0]
-    scattered = lax.all_to_all(
-        sums.reshape(plane, 512 // plane, CELLS), ("slab", "rep"), 0, 0
-    )
-    share = call(share_kernel, [shape(plane, 512 // plane, CELLS)], (scattered,))[0]
-    parts = lax.all_to_all(share, ("slab", "rep"), 0, 0).astype(F32)
-    weight_grad = jnp.transpose(parts.reshape(32, 16, CELLS)[:TAPS], (1, 0, 2)) * factor
+    weight_grad = jnp.transpose(weight_grad, (1, 0, 2))
     return (
         activated.reshape(inputs.shape),
         input_grad.reshape(inputs.shape),

time: 84.3 us -> 92 us (1.091)
  waiting for transfers between devices: 27.6 us -> 33.9 us
  starting transfers between devices: 28.9 us -> 31.2 us
  blocking collectives: 16 us -> 14.3 us
    ppermute x1 -> x2, waiting for transfers between devices: 1.79 us -> 15.9 us  [the longest x1 14.1 us: local(): got = lax.ppermute(sent, 'rep', [(0, 1), (1, 0)])]
    all_to_all x1, waiting for transfers between devices: 6.54 us -> 0.01 us  [local(): returned = lax.all_to_all(terms, 'slab', 0, 0)]
    ppermute x1 -> x2, starting transfers between devices: 0.01 us -> 2.21 us  [the longest x1 2.21 us: local(): got = lax.ppermute(sent, 'rep', [(0, 1), (1, 0)])]
    all_to_all x1, blocking collectives: 16 us -> 14.3 us  [local(): scattered = lax.all_to_all(sums.reshape(SLABS, 32, CELLS), 'slab', 0, 0)]
    ppermute x1, waiting for transfers between devices: 4.41 us -> 3.16 us  [local(): sums = lax.ppermute(sums, everyone, mirrored)]
    pallas_call x5 -> x8, Pallas kernels: 9.82 us -> 10.7 us  [call(): pl.pallas_call(kernel, out_shape=tuple(outs), in_specs=specs or [VMEM] *...]
  transfers between devices with their start and end apart: 7 -> 8, of which waited for: 7 -> 7; matrix products, arithmetic and copies ran while one was open for 0% -> 0% of each run, Pallas kernels for 1% -> 1%
where the time goes in v6:
time: 92 us; the launch traced here: 90.7 us
  waiting for transfers between devices  33.9 us (37%)
  starting transfers between devices  31.2 us (34%)
  blocking collectives  14.3 us (16%)
  Pallas kernels  10.7 us (12%)
    all_to_all x1, blocking collectives, local(): scattered = lax.all_to_all(sums.reshape(SLABS, 32, CELLS), 'slab', 0, 0)  14.3 us
    ppermute x1, waiting for transfers between devices, local(): got = lax.ppermute(sent, 'rep', [(0, 1), (1, 0)])  14.1 us
    pallas_call x8, Pallas kernels, call(): pl.pallas_call(kernel, out_shape=tuple(outs), in_specs=specs or [VMEM] *...  10.7 us
    all_to_all x1, starting transfers between devices, local(): returned = lax.all_to_all(terms, 'slab', 0, 0)  7.3 us
    all_to_all x1, waiting for transfers between devices, local(): parts = lax.all_to_all(share, ('slab', 'rep'), 0, 0)  6.19 us
    all_to_all x1, starting transfers between devices, local(): gathered = lax.all_to_all(packed, 'slab', 0, 0)  6.07 us
    all_to_all x1, starting transfers between devices, local(): parts = lax.all_to_all(share, ('slab', 'rep'), 0, 0)  4.76 us
    ppermute x1, waiting for transfers between devices, local(): same = lax.ppermute(by_tap, everyone, mirrored)  3.99 us
  transfers between devices with their start and end apart: 8, of which 7 were waited for; matrix products, arithmetic and copies ran while one was open for 0% of the time, Pallas kernels for 1%

profile of v6, /device:TPU:2, one launch (start us, length us, event | category | flops | bytes accessed | tf_op | source)
XLA Modules:
  0.0 90.7 jit_solution(4316916940914528369)
XLA Ops:
  0.6 2.1 %shard_map.58 = bf16[8,288,256]{2,1,0:T(8,128)(2,1)} custom-call(s32[1]{0:T(128)} %bitcast.chip_ref, bf16[256,256]{1,0:T(8,128)(2,1)} %bitcast.12, bf16[256,256]{1,0:T(8,128)(2,1)} %bitcast.13), custom_call_target="tpu_custom_call" | custom-call | bytes 1441796 | tf_op jit(solution)/shard_map/pallas_call | solution.py:246
  2.8 0.0 copy-start
  2.8 6.1 %all-to-all-start = ((bf16[8,288,256]{2,1,0:T(8,128)(2,1)}), bf16[8,288,256]{2,1,0:T(8,128)(2,1)S(1)}, u32[]{:S(2)}, u32[]{:S(2)}) async-start(bf16[8,288,256]{2,1,0:T(8,128)(2,1)} %shard_map.58), calls=%async_computation | async-start | bytes 2359296 | tf_op jit(solution)/shard_map/all_to_all | solution.py:299
  8.8 3.8 %collective-permute-start = (bf16[27,16,256]{2,1,0:T(8,128)(2,1)S(1)}, bf16[27,16,256]{2,1,0:T(8,128)(2,1)S(1)}, u32[]{:S(2)}, u32[]{:S(2)}) collective-permute-start(bf16[27,16,256]{2,1,0:T(8,128)(2,1)S(1)} %bitcast.14), channel_id=1, source_target_pairs={{0,0},{1,1},{2,34},{3,35},{4,68},{5,69},{6,102},{7,103},{8,136},{9... | collective-permute-start | bytes 663560 | tf_op jit(solution)/shard_map/ppermute | solution.py:281
  12.7 4.0 %collective-permute-done.same_ref = bf16[27,16,256]{2,1,0:T(8,128)(2,1)S(1)} collective-permute-done((bf16[27,16,256]{2,1,0:T(8,128)(2,1)S(1)}, bf16[27,16,256]{2,1,0:T(8,128)(2,1)S(1)}, u32[]{:S(2)}, u32[]{:S(2)}) %collective-permute-start) | collective-permute-done | bytes 221216 | tf_op jit(solution)/shard_map/ppermute | solution.py:281
  16.7 3.5 %collective-permute-start.1 = (bf16[27,16,256]{2,1,0:T(8,128)(2,1)S(1)}, bf16[27,16,256]{2,1,0:T(8,128)(2,1)S(1)}, u32[]{:S(2)}, u32[]{:S(2)}) collective-permute-start(bf16[27,16,256]{2,1,0:T(8,128)(2,1)S(1)} %collective-permute-done.same_ref), channel_id=1, source_target_pairs={{0,16},{16,0},{32,48},{48,32},{64,80},{80,64},{96,112},{112,96},{1... | collective-permute-start | bytes 663560 | tf_op jit(solution)/shard_map/ppermute | solution.py:282
  20.1 1.1 %collective-permute-done.1.opposite_ref = bf16[27,16,256]{2,1,0:T(8,128)(2,1)S(1)} collective-permute-done((bf16[27,16,256]{2,1,0:T(8,128)(2,1)S(1)}, bf16[27,16,256]{2,1,0:T(8,128)(2,1)S(1)}, u32[]{:S(2)}, u32[]{:S(2)}) %collective-permute-start.1) | collective-permute-done | bytes 221216 | tf_op jit(solution)/shard_map/ppermute | solution.py:282
  21.2 3.5 %all-to-all-done.r_ref = bf16[8,288,256]{2,1,0:T(8,128)(2,1)S(1)} async-done(((bf16[8,288,256]{2,1,0:T(8,128)(2,1)}), bf16[8,288,256]{2,1,0:T(8,128)(2,1)S(1)}, u32[]{:S(2)}, u32[]{:S(2)}) %all-to-all-start) | async-done | bytes 1179680 | tf_op jit(solution)/shard_map/all_to_all | solution.py:299
  24.8 6.0 %shard_map.59 = (bf16[8,288,256]{2,1,0:T(8,128)(2,1)}, f32[448,256]{1,0:T(8,128)S(1)}, f32[448,256]{1,0:T(8,128)S(1)}) custom-call(s32[1]{0:T(128)} %bitcast.1.core_ref, bf16[8,288,256]{2,1,0:T(8,128)(2,1)S(1)} %all-to-all-done.r_ref, bf16[27,16,256]{2,1,0:T(8,128)(2,1)S(1)} %collective-permute-done.same_ref, ...), custom_call_target="tpu_custom_call" | custom-call | flops 2818572288 | bytes 3719172 | tf_op jit(solution)/shard_map/pallas_call | solution.py:246
  30.8 7.3 %all-to-all-start.1 = ((bf16[8,288,256]{2,1,0:T(8,128)(2,1)}), bf16[8,288,256]{2,1,0:T(8,128)(2,1)S(1)}, u32[]{:S(2)}, u32[]{:S(2)}) async-start(bf16[8,288,256]{2,1,0:T(8,128)(2,1)} %get-tuple-element.10), calls=%async_computation.1 | async-start | bytes 2359296 | tf_op jit(solution)/shard_map/all_to_all | solution.py:317
  38.1 0.0 collective-permute-start.2
  38.1 1.8 %collective-permute-done.2.got_ref = f32[448,256]{1,0:T(8,128)S(1)} collective-permute-done((f32[448,256]{1,0:T(8,128)S(1)}, f32[448,256]{1,0:T(8,128)S(1)}, u32[]{:S(2)}, u32[]{:S(2)}) %collective-permute-start.2) | collective-permute-done | bytes 458784 | tf_op jit(solution)/shard_map/ppermute | solution.py:328
  39.9 0.1 shard_map.61
  40.0 2.2 %collective-permute-start.3 = (bf16[224,256]{1,0:T(8,128)(2,1)S(1)}, bf16[224,256]{1,0:T(8,128)(2,1)S(1)}, u32[]{:S(2)}, u32[]{:S(2)}) collective-permute-start(bf16[224,256]{1,0:T(8,128)(2,1)S(1)} %get-tuple-element.16), channel_id=1, source_target_pairs={{0,1},{1,0},{2,3},{3,2},{4,5},{5,4},{6,7},{7,6},{8,9},{9,8},{10,11... | collective-permute-start | bytes 344072 | tf_op jit(solution)/shard_map/ppermute | solution.py:331
  42.2 14.1 %collective-permute-done.3.got_ref = bf16[224,256]{1,0:T(8,128)(2,1)S(1)} collective-permute-done((bf16[224,256]{1,0:T(8,128)(2,1)S(1)}, bf16[224,256]{1,0:T(8,128)(2,1)S(1)}, u32[]{:S(2)}, u32[]{:S(2)}) %collective-permute-start.3) | collective-permute-done | bytes 114720 | tf_op jit(solution)/shard_map/ppermute | solution.py:331
  56.3 3.5 %collective-permute-start.4 = (bf16[224,256]{1,0:T(8,128)(2,1)S(1)}, bf16[224,256]{1,0:T(8,128)(2,1)S(1)}, u32[]{:S(2)}, u32[]{:S(2)}) collective-permute-start(bf16[224,256]{1,0:T(8,128)(2,1)S(1)} %shard_map.62), channel_id=1, source_target_pairs={{0,0},{1,1},{2,34},{3,35},{4,68},{5,69},{6,102},{7,103},{8,136},{9... | collective-permute-start | bytes 344072 | tf_op jit(solution)/shard_map/ppermute | solution.py:333
  59.9 3.2 %collective-permute-done.4.rows_ref = bf16[224,256]{1,0:T(8,128)(2,1)S(1)} collective-permute-done((bf16[224,256]{1,0:T(8,128)(2,1)S(1)}, bf16[224,256]{1,0:T(8,128)(2,1)S(1)}, u32[]{:S(2)}, u32[]{:S(2)}) %collective-permute-start.4) | collective-permute-done | bytes 114720 | tf_op jit(solution)/shard_map/ppermute | solution.py:333
  63.0 0.0 all-to-all-done.1.r_ref.after_ref
  63.0 14.3 %all_to_all.20.parts_ref = bf16[8,32,256]{2,1,0:T(8,128)(2,1)S(1)} all-to-all(bf16[8,32,256]{2,1,0:T(8,128)(2,1)S(1)} %bitcast.10), channel_id=1, replica_groups=mesh['fsdp'=16,'slab'=8,'rep'=2] {'slab'}, dimensions={0} | all-to-all | bytes 262144 | tf_op jit(solution)/shard_map/all_to_all | solution.py:335
  77.3 0.7 shard_map.64
  78.1 4.8 %all-to-all-start.3 = ((bf16[16,32,256]{2,1,0:T(8,128)(2,1)}), bf16[16,32,256]{2,1,0:T(8,128)(2,1)S(1)}, u32[]{:S(2)}, u32[]{:S(2)}) async-start(bf16[16,32,256]{2,1,0:T(8,128)(2,1)} %shard_map.64), calls=%async_computation.3 | async-start | bytes 524288 | tf_op jit(solution)/shard_map/all_to_all | solution.py:337
  82.8 0.9 shard_map.60
  83.7 6.2 %all-to-all-done.3.parts_ref = bf16[16,32,256]{2,1,0:T(8,128)(2,1)S(1)} async-done(((bf16[16,32,256]{2,1,0:T(8,128)(2,1)}), bf16[16,32,256]{2,1,0:T(8,128)(2,1)S(1)}, u32[]{:S(2)}, u32[]{:S(2)}) %all-to-all-start.3) | async-done | bytes 262176 | tf_op jit(solution)/shard_map/all_to_all | solution.py:337
  89.9 0.8 shard_map.65
  (3 shorter events, 0.0 us)
Async XLA Ops:
  2.8 6.1 %copy-start = (bf16[16,27,256]{2,0,1:T(8,128)(2,1)S(1)}, bf16[16,27,256]{2,0,1:T(8,128)(2,1)}, u32[]{:S(2)}) copy-start(bf16[16,27,256]{2,0,1:T(8,128)(2,1)} %param.4) | copy-start | bytes 663556
  2.8 22.0 %all-to-all-start = ((bf16[8,288,256]{2,1,0:T(8,128)(2,1)}), bf16[8,288,256]{2,1,0:T(8,128)(2,1)S(1)}, u32[]{:S(2)}, u32[]{:S(2)}) async-start(bf16[8,288,256]{2,1,0:T(8,128)(2,1)} %shard_map.58), calls=%async_computation | async-start | bytes 2359296 | tf_op jit(solution)/shard_map/all_to_all | solution.py:299
  8.8 7.8 %collective-permute-start = (bf16[27,16,256]{2,1,0:T(8,128)(2,1)S(1)}, bf16[27,16,256]{2,1,0:T(8,128)(2,1)S(1)}, u32[]{:S(2)}, u32[]{:S(2)}) collective-permute-start(bf16[27,16,256]{2,1,0:T(8,128)(2,1)S(1)} %bitcast.14), channel_id=1, source_target_pairs={{0,0},{1,1},{2,34},{3,35},{4,68},{5,69},{6,102},{7,103},{8,136},{9... | collective-permute-start | bytes 663560 | tf_op jit(solution)/shard_map/ppermute | solution.py:281
  16.7 4.6 %collective-permute-start.1 = (bf16[27,16,256]{2,1,0:T(8,128)(2,1)S(1)}, bf16[27,16,256]{2,1,0:T(8,128)(2,1)S(1)}, u32[]{:S(2)}, u32[]{:S(2)}) collective-permute-start(bf16[27,16,256]{2,1,0:T(8,128)(2,1)S(1)} %collective-permute-done.same_ref), channel_id=1, source_target_pairs={{0,16},{16,0},{32,48},{48,32},{64,80},{80,64},{96,112},{112,96},{1... | collective-permute-start | bytes 663560 | tf_op jit(solution)/shard_map/ppermute | solution.py:282
  30.8 32.2 %all-to-all-start.1 = ((bf16[8,288,256]{2,1,0:T(8,128)(2,1)}), bf16[8,288,256]{2,1,0:T(8,128)(2,1)S(1)}, u32[]{:S(2)}, u32[]{:S(2)}) async-start(bf16[8,288,256]{2,1,0:T(8,128)(2,1)} %get-tuple-element.10), calls=%async_computation.1 | async-start | bytes 2359296 | tf_op jit(solution)/shard_map/all_to_all | solution.py:317
  38.1 1.8 %collective-permute-start.2 = (f32[448,256]{1,0:T(8,128)S(1)}, f32[448,256]{1,0:T(8,128)S(1)}, u32[]{:S(2)}, u32[]{:S(2)}) collective-permute-start(f32[448,256]{1,0:T(8,128)S(1)} %get-tuple-element.14), channel_id=1, source_target_pairs={{0,16},{16,0},{32,48},{48,32},{64,80},{80,64},{96,112},{112,96},{1... | collective-permute-start | bytes 1376264 | tf_op jit(solution)/shard_map/ppermute | solution.py:328
  40.0 16.3 %collective-permute-start.3 = (bf16[224,256]{1,0:T(8,128)(2,1)S(1)}, bf16[224,256]{1,0:T(8,128)(2,1)S(1)}, u32[]{:S(2)}, u32[]{:S(2)}) collective-permute-start(bf16[224,256]{1,0:T(8,128)(2,1)S(1)} %get-tuple-element.16), channel_id=1, source_target_pairs={{0,1},{1,0},{2,3},{3,2},{4,5},{5,4},{6,7},{7,6},{8,9},{9,8},{10,11... | collective-permute-start | bytes 344072 | tf_op jit(solution)/shard_map/ppermute | solution.py:331
  56.3 6.7 %collective-permute-start.4 = (bf16[224,256]{1,0:T(8,128)(2,1)S(1)}, bf16[224,256]{1,0:T(8,128)(2,1)S(1)}, u32[]{:S(2)}, u32[]{:S(2)}) collective-permute-start(bf16[224,256]{1,0:T(8,128)(2,1)S(1)} %shard_map.62), channel_id=1, source_target_pairs={{0,0},{1,1},{2,34},{3,35},{4,68},{5,69},{6,102},{7,103},{8,136},{9... | collective-permute-start | bytes 344072 | tf_op jit(solution)/shard_map/ppermute | solution.py:333
  78.1 11.9 %all-to-all-start.3 = ((bf16[16,32,256]{2,1,0:T(8,128)(2,1)}), bf16[16,32,256]{2,1,0:T(8,128)(2,1)S(1)}, u32[]{:S(2)}, u32[]{:S(2)}) async-start(bf16[16,32,256]{2,1,0:T(8,128)(2,1)} %shard_map.64), calls=%async_computation.3 | async-start | bytes 524288 | tf_op jit(solution)/shard_map/all_to_all | solution.py:337

commit v7 on v4

--- a/solution.py
+++ b/solution.py
@@ -27,16 +27,24 @@
 
 def pack_kernel(chip_ref, x_ref, u_ref, out_ref, x_own, u_own, turned, sems):
     take_u = pltpu.make_async_copy(u_ref, u_own, sems.at[0])
-    take_x = pltpu.make_async_copy(x_ref, x_own, sems.at[1])
-    take_u.start()
-    take_x.start()
-    take_x.wait()
-    copies = [
-        pltpu.make_async_copy(x_own, out_ref.at[slab, pl.ds(0, CELLS), :], sems.at[2 + slab])
-        for slab in range(SLABS)
+    takes_x = [
+        pltpu.make_async_copy(x_ref.at[rows, :], x_own.at[rows, :], sems.at[1 + part])
+        for part, rows in enumerate((pl.ds(0, 128), pl.ds(128, 128)))
     ]
-    for copy in copies:
-        copy.start()
+    for take in (takes_x[0], take_u, takes_x[1]):
+        take.start()
+    copies = []
+    for part, rows in enumerate((pl.ds(0, 128), pl.ds(128, 128))):
+        takes_x[part].wait()
+        for slab in range(SLABS):
+            copies.append(
+                pltpu.make_async_copy(
+                    x_own.at[rows, :],
+                    out_ref.at[slab, rows, :],
+                    sems.at[4 + part * SLABS + slab],
+                )
+            )
+            copies[-1].start()
     take_u.wait()
     by_out = jnp.transpose(u_own[...].astype(F32)).astype(BF16)
     for pair in range(SLABS):
@@ -46,7 +54,7 @@
                 start : start + 16
             ]
     last = pltpu.make_async_copy(
-        turned, out_ref.at[:, pl.ds(CELLS, OUTS), :], sems.at[2 + SLABS]
+        turned, out_ref.at[:, pl.ds(CELLS, OUTS), :], sems.at[3]
     )
     last.start()
     for copy in copies:
@@ -161,14 +169,16 @@
         left = whole[start : start + 16]
         right = whole[start + 16 : start + 32]
         own_ref[tap * 16 : tap * 16 + 16, :] = jnp.where(first, left, right)
-        other_ref[tap * 16 : tap * 16 + 16, :] = jnp.where(first, right, left).astype(
-            other_ref.dtype
-        )
+        other_ref[tap * 16 : tap * 16 + 16, :] = jnp.where(first, right, left).astype(BF16)
     turned = jnp.transpose(w2_ref[...].astype(F32)).astype(BF16)
     for slab in range(SLABS):
         out_ref[slab, :CELLS, :] = jnp.dot(
             turned, g_ref[:, slab * CELLS : (slab + 1) * CELLS], preferred_element_type=F32
         ).astype(BF16)
+
+
+def add_kernel(own_ref, got_ref, out_ref):
+    out_ref[...] = (own_ref[...] + got_ref[...].astype(F32)).astype(BF16)
 
 
 def lengthen_kernel(rows_ref, after_ref, out_ref):
@@ -266,7 +276,7 @@
             pltpu.VMEM((CELLS, CELLS), BF16),
             pltpu.VMEM((CELLS, CELLS), BF16),
             pltpu.VMEM((SLABS, OUTS, CELLS), BF16),
-            pltpu.SemaphoreType.DMA((3 + SLABS,)),
+            pltpu.SemaphoreType.DMA((4 + 2 * SLABS,)),
         ],
         out_spec=HBM,
         vmem=56,
@@ -278,7 +288,7 @@
         [
             shape(SLABS, CELLS + OUTS, CELLS),
             shape(TAPS * 16, CELLS, dtype=F32),
-            shape(TAPS * 16, CELLS, dtype=F32),
+            shape(TAPS * 16, CELLS),
         ],
         (core, gathered, same, opposite),
         specs=[SMEM, VMEM, VMEM, VMEM],
@@ -297,7 +307,9 @@
         specs=[SMEM, VMEM],
     )
 
-    sums = (own + lax.ppermute(other, "fsdp", cores)).astype(BF16)
+    sums = call(
+        add_kernel, [shape(TAPS * 16, CELLS)], (own, lax.ppermute(other, "fsdp", cores))
+    )[0]
     sums = lax.ppermute(sums, everyone, mirrored)
     plane = SLABS * reps
     sums = call(

time: 84.3 us -> 83.9 us (level)
    pallas_call x5 -> x6, Pallas kernels: 9.82 us -> 9.81 us  [call(): pl.pallas_call(kernel, out_shape=tuple(outs), in_specs=specs or [VMEM] *...]
where the time goes in v7:
time: 83.9 us; the launch traced here: 83.5 us
  starting transfers between devices  29 us (35%)
  waiting for transfers between devices  27.6 us (33%)
  blocking collectives  15.7 us (19%)
  Pallas kernels  9.81 us (12%)
    all_to_all x1, blocking collectives, local(): lax.all_to_all(sums.reshape(plane, 512 // plane, CELLS), ('slab', 'rep'),...  15.7 us
    pallas_call x6, Pallas kernels, call(): pl.pallas_call(kernel, out_shape=tuple(outs), in_specs=specs or [VMEM] *...  9.81 us
    all_to_all x1, starting transfers between devices, local(): returned = lax.all_to_all(terms, 'slab', 0, 0)  7.3 us
    all_to_all x1, waiting for transfers between devices, local(): returned = lax.all_to_all(terms, 'slab', 0, 0)  6.87 us
    all_to_all x1, waiting for transfers between devices, local(): parts = lax.all_to_all(share, ('slab', 'rep'), 0, 0).astype(F32)  6.19 us
    all_to_all x1, starting transfers between devices, local(): gathered = lax.all_to_all(packed, 'slab', 0, 0)  6.07 us
    all_to_all x1, starting transfers between devices, local(): parts = lax.all_to_all(share, ('slab', 'rep'), 0, 0).astype(F32)  4.88 us
    ppermute x1, waiting for transfers between devices, local(): sums = lax.ppermute(sums, everyone, mirrored)  4.39 us
  transfers between devices with their start and end apart: 7, of which 7 were waited for; matrix products, arithmetic and copies ran while one was open for 0% of the time, Pallas kernels for 1%

profile of v7, /device:TPU:2, one launch (start us, length us, event | category | flops | bytes accessed | tf_op | source)
XLA Modules:
  0.0 83.5 jit_solution(9094267351102342703)
XLA Ops:
  0.6 2.0 %shard_map.58 = bf16[8,288,256]{2,1,0:T(8,128)(2,1)} custom-call(s32[1]{0:T(128)} %bitcast.chip_ref, bf16[256,256]{1,0:T(8,128)(2,1)} %bitcast.13, bf16[256,256]{1,0:T(8,128)(2,1)} %bitcast.14), custom_call_target="tpu_custom_call" | custom-call | bytes 1441796 | tf_op jit(solution)/shard_map/pallas_call | solution.py:232
  2.7 0.0 copy-start
  2.7 6.1 %all-to-all-start = ((bf16[8,288,256]{2,1,0:T(8,128)(2,1)}), bf16[8,288,256]{2,1,0:T(8,128)(2,1)S(1)}, u32[]{:S(2)}, u32[]{:S(2)}) async-start(bf16[8,288,256]{2,1,0:T(8,128)(2,1)} %shard_map.58), calls=%async_computation | async-start | bytes 2359296 | tf_op jit(solution)/shard_map/all_to_all | solution.py:284
  8.8 0.0 copy-done
  8.8 3.8 %collective-permute-start = (bf16[27,16,256]{2,1,0:T(8,128)(2,1)S(1)}, bf16[27,16,256]{2,1,0:T(8,128)(2,1)S(1)}, u32[]{:S(2)}, u32[]{:S(2)}) collective-permute-start(bf16[27,16,256]{2,1,0:T(8,128)(2,1)S(1)} %bitcast.15), channel_id=1, source_target_pairs={{0,0},{1,1},{2,34},{3,35},{4,68},{5,69},{6,102},{7,103},{8,136},{9... | collective-permute-start | bytes 663560 | tf_op jit(solution)/shard_map/ppermute | solution.py:266
  12.6 4.0 %collective-permute-done.same_ref = bf16[27,16,256]{2,1,0:T(8,128)(2,1)S(1)} collective-permute-done((bf16[27,16,256]{2,1,0:T(8,128)(2,1)S(1)}, bf16[27,16,256]{2,1,0:T(8,128)(2,1)S(1)}, u32[]{:S(2)}, u32[]{:S(2)}) %collective-permute-start) | collective-permute-done | bytes 221216 | tf_op jit(solution)/shard_map/ppermute | solution.py:266
  16.6 3.5 %collective-permute-start.1 = (bf16[27,16,256]{2,1,0:T(8,128)(2,1)S(1)}, bf16[27,16,256]{2,1,0:T(8,128)(2,1)S(1)}, u32[]{:S(2)}, u32[]{:S(2)}) collective-permute-start(bf16[27,16,256]{2,1,0:T(8,128)(2,1)S(1)} %collective-permute-done.same_ref), channel_id=1, source_target_pairs={{0,16},{16,0},{32,48},{48,32},{64,80},{80,64},{96,112},{112,96},{1... | collective-permute-start | bytes 663560 | tf_op jit(solution)/shard_map/ppermute | solution.py:267
  20.1 1.1 %collective-permute-done.1.opposite_ref = bf16[27,16,256]{2,1,0:T(8,128)(2,1)S(1)} collective-permute-done((bf16[27,16,256]{2,1,0:T(8,128)(2,1)S(1)}, bf16[27,16,256]{2,1,0:T(8,128)(2,1)S(1)}, u32[]{:S(2)}, u32[]{:S(2)}) %collective-permute-start.1) | collective-permute-done | bytes 221216 | tf_op jit(solution)/shard_map/ppermute | solution.py:267
  21.2 3.5 %all-to-all-done.r_ref = bf16[8,288,256]{2,1,0:T(8,128)(2,1)S(1)} async-done(((bf16[8,288,256]{2,1,0:T(8,128)(2,1)}), bf16[8,288,256]{2,1,0:T(8,128)(2,1)S(1)}, u32[]{:S(2)}, u32[]{:S(2)}) %all-to-all-start) | async-done | bytes 1179680 | tf_op jit(solution)/shard_map/all_to_all | solution.py:284
  24.7 6.0 %shard_map.59 = (bf16[8,288,256]{2,1,0:T(8,128)(2,1)}, f32[432,256]{1,0:T(8,128)S(1)}, bf16[432,256]{1,0:T(8,128)(2,1)S(1)}) custom-call(s32[1]{0:T(128)} %bitcast.1.core_ref, bf16[8,288,256]{2,1,0:T(8,128)(2,1)S(1)} %all-to-all-done.r_ref, bf16[27,16,256]{2,1,0:T(8,128)(2,1)S(1)} %collective-permute-done.same_ref, ...), custom_call_target="tpu_custom_call" | custom-call | flops 2818572288 | bytes 3465220 | tf_op jit(solution)/shard_map/pallas_call | solution.py:232
  30.8 7.3 %all-to-all-start.1 = ((bf16[8,288,256]{2,1,0:T(8,128)(2,1)}), bf16[8,288,256]{2,1,0:T(8,128)(2,1)S(1)}, u32[]{:S(2)}, u32[]{:S(2)}) async-start(bf16[8,288,256]{2,1,0:T(8,128)(2,1)} %get-tuple-element.8), calls=%async_computation.1 | async-start | bytes 2359296 | tf_op jit(solution)/shard_map/all_to_all | solution.py:302
  38.0 0.0 collective-permute-start.2
  38.0 1.5 %collective-permute-done.2.got_ref = bf16[432,256]{1,0:T(8,128)(2,1)S(1)} collective-permute-done((bf16[432,256]{1,0:T(8,128)(2,1)S(1)}, bf16[432,256]{1,0:T(8,128)(2,1)S(1)}, u32[]{:S(2)}, u32[]{:S(2)}) %collective-permute-start.2) | collective-permute-done | bytes 221216 | tf_op jit(solution)/shard_map/ppermute | solution.py:311
  39.5 0.1 shard_map.61
  39.6 3.4 %collective-permute-start.3 = (bf16[432,256]{1,0:T(8,128)(2,1)S(1)}, bf16[432,256]{1,0:T(8,128)(2,1)S(1)}, u32[]{:S(2)}, u32[]{:S(2)}) collective-permute-start(bf16[432,256]{1,0:T(8,128)(2,1)S(1)} %shard_map.61), channel_id=1, source_target_pairs={{0,0},{1,1},{2,34},{3,35},{4,68},{5,69},{6,102},{7,103},{8,136},{9... | collective-permute-start | bytes 663560 | tf_op jit(solution)/shard_map/ppermute | solution.py:313
  43.0 4.4 %collective-permute-done.3.rows_ref = bf16[432,256]{1,0:T(8,128)(2,1)S(1)} collective-permute-done((bf16[432,256]{1,0:T(8,128)(2,1)S(1)}, bf16[432,256]{1,0:T(8,128)(2,1)S(1)}, u32[]{:S(2)}, u32[]{:S(2)}) %collective-permute-start.3) | collective-permute-done | bytes 221216 | tf_op jit(solution)/shard_map/ppermute | solution.py:313
  47.4 6.9 %all-to-all-done.1.r_ref.after_ref = bf16[8,288,256]{2,1,0:T(8,128)(2,1)S(1)} async-done(((bf16[8,288,256]{2,1,0:T(8,128)(2,1)}), bf16[8,288,256]{2,1,0:T(8,128)(2,1)S(1)}, u32[]{:S(2)}, u32[]{:S(2)}) %all-to-all-start.1) | async-done | bytes 1179680 | tf_op jit(solution)/shard_map/all_to_all | solution.py:302
  54.3 15.7 %all_to_all.20.parts_ref = bf16[16,32,256]{2,1,0:T(8,128)(2,1)S(1)} all-to-all(bf16[16,32,256]{2,1,0:T(8,128)(2,1)S(1)} %bitcast.11), channel_id=1, replica_groups=mesh['fsdp'=16,'slab'=8,'rep'=2] {'slab','rep'}, dimensions={0} | all-to-all | bytes 524288 | tf_op jit(solution)/shard_map/all_to_all | solution.py:321
  70.0 0.8 shard_map.63
  70.7 4.9 %all-to-all-start.3 = ((bf16[16,32,256]{2,1,0:T(8,128)(2,1)}), bf16[16,32,256]{2,1,0:T(8,128)(2,1)S(1)}, u32[]{:S(2)}, u32[]{:S(2)}) async-start(bf16[16,32,256]{2,1,0:T(8,128)(2,1)} %shard_map.63), calls=%async_computation.3 | async-start | bytes 524288 | tf_op jit(solution)/shard_map/all_to_all | solution.py:325
  75.6 0.9 %shard_map.60 = (bf16[256,256]{1,0:T(8,128)(2,1)}, bf16[256,256]{1,0:T(8,128)(2,1)}) custom-call(s32[1]{0:T(128)} %bitcast.chip_ref, bf16[8,288,256]{2,1,0:T(8,128)(2,1)S(1)} %all-to-all-done.1.r_ref.after_ref), custom_call_target="tpu_custom_call" | custom-call | bytes 1441796 | tf_op jit(solution)/shard_map/pallas_call | solution.py:232
  76.5 6.2 %all-to-all-done.3 = bf16[16,32,256]{2,1,0:T(8,128)(2,1)S(1)} async-done(((bf16[16,32,256]{2,1,0:T(8,128)(2,1)}), bf16[16,32,256]{2,1,0:T(8,128)(2,1)S(1)}, u32[]{:S(2)}, u32[]{:S(2)}) %all-to-all-start.3) | async-done | bytes 262176 | tf_op jit(solution)/shard_map/all_to_all | solution.py:325
  82.7 0.8 multiply_bitcast_fusion
  (1 shorter events, 0.0 us)
Async XLA Ops:
  2.7 6.1 %copy-start = (bf16[16,27,256]{2,0,1:T(8,128)(2,1)S(1)}, bf16[16,27,256]{2,0,1:T(8,128)(2,1)}, u32[]{:S(2)}) copy-start(bf16[16,27,256]{2,0,1:T(8,128)(2,1)} %param.4) | copy-start | bytes 663556
  2.7 22.0 %all-to-all-start = ((bf16[8,288,256]{2,1,0:T(8,128)(2,1)}), bf16[8,288,256]{2,1,0:T(8,128)(2,1)S(1)}, u32[]{:S(2)}, u32[]{:S(2)}) async-start(bf16[8,288,256]{2,1,0:T(8,128)(2,1)} %shard_map.58), calls=%async_computation | async-start | bytes 2359296 | tf_op jit(solution)/shard_map/all_to_all | solution.py:284
  8.8 7.8 %collective-permute-start = (bf16[27,16,256]{2,1,0:T(8,128)(2,1)S(1)}, bf16[27,16,256]{2,1,0:T(8,128)(2,1)S(1)}, u32[]{:S(2)}, u32[]{:S(2)}) collective-permute-start(bf16[27,16,256]{2,1,0:T(8,128)(2,1)S(1)} %bitcast.15), channel_id=1, source_target_pairs={{0,0},{1,1},{2,34},{3,35},{4,68},{5,69},{6,102},{7,103},{8,136},{9... | collective-permute-start | bytes 663560 | tf_op jit(solution)/shard_map/ppermute | solution.py:266
  16.6 4.6 %collective-permute-start.1 = (bf16[27,16,256]{2,1,0:T(8,128)(2,1)S(1)}, bf16[27,16,256]{2,1,0:T(8,128)(2,1)S(1)}, u32[]{:S(2)}, u32[]{:S(2)}) collective-permute-start(bf16[27,16,256]{2,1,0:T(8,128)(2,1)S(1)} %collective-permute-done.same_ref), channel_id=1, source_target_pairs={{0,16},{16,0},{32,48},{48,32},{64,80},{80,64},{96,112},{112,96},{1... | collective-permute-start | bytes 663560 | tf_op jit(solution)/shard_map/ppermute | solution.py:267
  30.8 23.5 %all-to-all-start.1 = ((bf16[8,288,256]{2,1,0:T(8,128)(2,1)}), bf16[8,288,256]{2,1,0:T(8,128)(2,1)S(1)}, u32[]{:S(2)}, u32[]{:S(2)}) async-start(bf16[8,288,256]{2,1,0:T(8,128)(2,1)} %get-tuple-element.8), calls=%async_computation.1 | async-start | bytes 2359296 | tf_op jit(solution)/shard_map/all_to_all | solution.py:302
  38.0 1.5 %collective-permute-start.2 = (bf16[432,256]{1,0:T(8,128)(2,1)S(1)}, bf16[432,256]{1,0:T(8,128)(2,1)S(1)}, u32[]{:S(2)}, u32[]{:S(2)}) collective-permute-start(bf16[432,256]{1,0:T(8,128)(2,1)S(1)} %get-tuple-element.12), channel_id=1, source_target_pairs={{0,16},{16,0},{32,48},{48,32},{64,80},{80,64},{96,112},{112,96},{1... | collective-permute-start | bytes 663560 | tf_op jit(solution)/shard_map/ppermute | solution.py:311
  39.6 7.8 %collective-permute-start.3 = (bf16[432,256]{1,0:T(8,128)(2,1)S(1)}, bf16[432,256]{1,0:T(8,128)(2,1)S(1)}, u32[]{:S(2)}, u32[]{:S(2)}) collective-permute-start(bf16[432,256]{1,0:T(8,128)(2,1)S(1)} %shard_map.61), channel_id=1, source_target_pairs={{0,0},{1,1},{2,34},{3,35},{4,68},{5,69},{6,102},{7,103},{8,136},{9... | collective-permute-start | bytes 663560 | tf_op jit(solution)/shard_map/ppermute | solution.py:313
  70.7 12.0 %all-to-all-start.3 = ((bf16[16,32,256]{2,1,0:T(8,128)(2,1)}), bf16[16,32,256]{2,1,0:T(8,128)(2,1)S(1)}, u32[]{:S(2)}, u32[]{:S(2)}) async-start(bf16[16,32,256]{2,1,0:T(8,128)(2,1)} %shard_map.63), calls=%async_computation.3 | async-start | bytes 524288 | tf_op jit(solution)/shard_map/all_to_all | solution.py:325

commit v8 on v6

--- a/solution.py
+++ b/solution.py
@@ -24,32 +24,40 @@
     return (along_x * 3 + along_y) * 3 + along_z
 
 
-def home(pair, core, chip):
-    return (pair + 4 * core + chip) & 7
-
-
-def pack_kernel(chip_ref, x_ref, u_ref, out_ref, x_own, u_own, turned, sems):
+def home(pair, core, spot_ref):
+    return ((pair + 4 * core + spot_ref[0]) & 7) ^ (spot_ref[0] >> 3)
+
+
+def pack_kernel(spot_ref, x_ref, u_ref, out_ref, x_own, u_own, turned, sems):
     take_u = pltpu.make_async_copy(u_ref, u_own, sems.at[0])
-    take_x = pltpu.make_async_copy(x_ref, x_own, sems.at[1])
-    take_u.start()
-    take_x.start()
-    take_x.wait()
-    copies = [
-        pltpu.make_async_copy(x_own, out_ref.at[slab, pl.ds(0, CELLS), :], sems.at[2 + slab])
-        for slab in range(SLABS)
+    takes_x = [
+        pltpu.make_async_copy(x_ref.at[rows, :], x_own.at[rows, :], sems.at[1 + part])
+        for part, rows in enumerate((pl.ds(0, 128), pl.ds(128, 128)))
     ]
-    for copy in copies:
-        copy.start()
+    for take in (takes_x[0], take_u, takes_x[1]):
+        take.start()
+    copies = []
+    for part, rows in enumerate((pl.ds(0, 128), pl.ds(128, 128))):
+        takes_x[part].wait()
+        for slab in range(SLABS):
+            copies.append(
+                pltpu.make_async_copy(
+                    x_own.at[rows, :],
+                    out_ref.at[slab, rows, :],
+                    sems.at[4 + part * SLABS + slab],
+                )
+            )
+            copies[-1].start()
     take_u.wait()
     by_out = jnp.transpose(u_own[...].astype(F32)).astype(BF16)
     for pair in range(SLABS):
         for core in range(2):
             start = pair * OUTS + core * 16
-            turned[home(pair, core, chip_ref[0]), core * 16 : core * 16 + 16, :] = by_out[
+            turned[home(pair, core, spot_ref), core * 16 : core * 16 + 16, :] = by_out[
                 start : start + 16
             ]
     last = pltpu.make_async_copy(
-        turned, out_ref.at[:, pl.ds(CELLS, OUTS), :], sems.at[2 + SLABS]
+        turned, out_ref.at[:, pl.ds(CELLS, OUTS), :], sems.at[3]
     )
     last.start()
     for copy in copies:
@@ -160,7 +168,7 @@
         preferred_element_type=F32,
     )
     own_ref[TAPS * 16 :, :] = jnp.zeros((16, CELLS), F32)
-    other_ref[TAPS * 16 :, :] = jnp.zeros((16, CELLS), F32)
+    other_ref[TAPS * 16 :, :] = jnp.zeros((16, CELLS), BF16)
     for tap in range(TAPS):
         start = tap * OUTS
         left = whole[start : start + 16]
@@ -178,8 +186,8 @@
 
 def halve_kernel(rep_ref, own_ref, got_ref, kept_ref, sent_ref):
     first = rep_ref[0] == 0
-    low = own_ref[:HALF, :] + got_ref[:HALF, :]
-    high = own_ref[HALF:, :] + got_ref[HALF:, :]
+    low = own_ref[:HALF, :] + got_ref[:HALF, :].astype(F32)
+    high = own_ref[HALF:, :] + got_ref[HALF:, :].astype(F32)
     kept_ref[...] = jnp.where(first, low, high)
     sent_ref[...] = jnp.where(first, high, low).astype(BF16)
 
@@ -208,7 +216,7 @@
         out_ref[tap] = parts_ref[place // 2 * 2 + rep, rows, :].astype(F32) * factor
 
 
-def final_kernel(chip_ref, r_ref, act_ref, grad_ref):
+def final_kernel(spot_ref, r_ref, act_ref, grad_ref):
     total = r_ref[0, :CELLS, :].astype(F32)
     for slab in range(1, SLABS):
         total = total + r_ref[slab, :CELLS, :].astype(F32)
@@ -218,7 +226,7 @@
             jnp.concatenate(
                 [
                     r_ref[
-                        home(pair, core, chip_ref[0]),
+                        home(pair, core, spot_ref),
                         CELLS + core * 16 : CELLS + core * 16 + 16,
                         :,
                     ].astype(F32)
@@ -257,8 +265,8 @@
 def local(inputs, weights, upstream):
     owner = lax.axis_index("fsdp")
     core = (owner % 2).astype(jnp.int32).reshape(1)
-    chip = (owner // 2).astype(jnp.int32).reshape(1)
     rep = lax.axis_index("rep").astype(jnp.int32).reshape(1)
+    spot = (owner // 2 + 8 * lax.axis_index("rep")).astype(jnp.int32).reshape(1)
     chips = lax.axis_size("fsdp") // 2
     reps = lax.axis_size("rep")
     total_cells = 2 * chips * reps * WHOLE
@@ -269,7 +277,7 @@
 
     everyone = ("fsdp", "slab", "rep")
     mirrored = [
-        (place(z, core, y, rep), place((y + 4 * core - z) % SLABS, core, y, rep))
+        (place(z, core, y, rep), place(((y ^ rep) + 4 * core - z) % SLABS, core, y, rep))
         for z in range(chips)
         for core in range(2)
         for y in range(SLABS)
@@ -285,13 +293,13 @@
     packed = call(
         pack_kernel,
         [shape(SLABS, CELLS + OUTS, CELLS)],
-        (chip, cells, upstream.reshape(CELLS, CELLS)),
+        (spot, cells, upstream.reshape(CELLS, CELLS)),
         specs=[SMEM, HBM, HBM],
         scratch=[
             pltpu.VMEM((CELLS, CELLS), BF16),
             pltpu.VMEM((CELLS, CELLS), BF16),
             pltpu.VMEM((SLABS, OUTS, CELLS), BF16),
-            pltpu.SemaphoreType.DMA((3 + SLABS,)),
+            pltpu.SemaphoreType.DMA((4 + 2 * SLABS,)),
         ],
         out_spec=HBM,
         vmem=56,
@@ -303,7 +311,7 @@
         [
             shape(SLABS, CELLS + OUTS, CELLS),
             shape(2 * HALF, CELLS, dtype=F32),
-            shape(2 * HALF, CELLS, dtype=F32),
+            shape(2 * HALF, CELLS),
         ],
         (core, gathered, same, opposite),
         specs=[SMEM, VMEM, VMEM, VMEM],
@@ -318,7 +326,7 @@
     activated, input_grad = call(
         final_kernel,
         [shape(CELLS, CELLS), shape(CELLS, CELLS)],
-        (chip, returned),
+        (spot, returned),
         specs=[SMEM, VMEM],
     )
 
@@ -328,7 +336,14 @@
         (rep, own, lax.ppermute(other, "fsdp", cores)),
         specs=[SMEM, VMEM, VMEM],
     )
-    got = lax.ppermute(sent, "rep", [(0, 1), (1, 0)])
+    beside = [
+        (place(z, core, y, rep), place(z, core, y ^ 1, 1 - rep))
+        for z in range(chips)
+        for core in range(2)
+        for y in range(SLABS)
+        for rep in range(reps)
+    ]
+    got = lax.ppermute(sent, everyone, beside)
     sums = call(add_kernel, [shape(HALF, CELLS)], (kept, got))[0]
     sums = lax.ppermute(sums, everyone, mirrored)
     sums = call(lengthen_kernel, [shape(256, CELLS)], (sums, returned), specs=[VMEM, ANY])[0]

time: 92 us -> 85.5 us (0.929)
  waiting for transfers between devices: 33.9 us -> 25.9 us
  starting transfers between devices: 31.2 us -> 32.6 us
  blocking collectives: 14.3 us -> 15.3 us
    ppermute x1, waiting for transfers between devices: 14.1 us -> 3.62 us  [local(): got = lax.ppermute(sent, everyone, beside)]
    all_to_all x1, waiting for transfers between devices: 0.01 us -> 2.7 us  [local(): returned = lax.all_to_all(terms, 'slab', 0, 0)]
    all_to_all x1, starting transfers between devices: 4.76 us -> 6.85 us  [local(): parts = lax.all_to_all(share, ('slab', 'rep'), 0, 0)]
    all_to_all x1, blocking collectives: 14.3 us -> 15.3 us  [local(): scattered = lax.all_to_all(sums.reshape(SLABS, 32, CELLS), 'slab', 0, 0)]
  transfers between devices with their start and end apart: 8 -> 8, of which waited for: 7 -> 8; matrix products, arithmetic and copies ran while one was open for 0% -> 0% of each run, Pallas kernels for 1% -> 1%
where the time goes in v8:
time: 85.5 us; the launch traced here: 85.1 us
  starting transfers between devices  32.6 us (38%)
  waiting for transfers between devices  25.9 us (30%)
  blocking collectives  15.3 us (18%)
  Pallas kernels  10.6 us (12%)
    all_to_all x1, blocking collectives, local(): scattered = lax.all_to_all(sums.reshape(SLABS, 32, CELLS), 'slab', 0, 0)  15.3 us
    pallas_call x8, Pallas kernels, call(): pl.pallas_call(kernel, out_shape=tuple(outs), in_specs=specs or [VMEM] *...  10.6 us
    all_to_all x1, starting transfers between devices, local(): returned = lax.all_to_all(terms, 'slab', 0, 0)  7.28 us
    all_to_all x1, starting transfers between devices, local(): parts = lax.all_to_all(share, ('slab', 'rep'), 0, 0)  6.85 us
    all_to_all x1, waiting for transfers between devices, local(): parts = lax.all_to_all(share, ('slab', 'rep'), 0, 0)  6.19 us
    all_to_all x1, starting transfers between devices, local(): gathered = lax.all_to_all(packed, 'slab', 0, 0)  6.07 us
    ppermute x1, waiting for transfers between devices, local(): same = lax.ppermute(by_tap, everyone, mirrored)  3.99 us
    ppermute x1, starting transfers between devices, local(): same = lax.ppermute(by_tap, everyone, mirrored)  3.81 us
  transfers between devices with their start and end apart: 8, of which 8 were waited for; matrix products, arithmetic and copies ran while one was open for 0% of the time, Pallas kernels for 1%

profile of v8, /device:TPU:2, one launch (start us, length us, event | category | flops | bytes accessed | tf_op | source)
XLA Modules:
  0.0 85.1 jit_solution(8727686817849498055)
XLA Ops:
  0.6 2.0 %shard_map.58 = bf16[8,288,256]{2,1,0:T(8,128)(2,1)} custom-call(s32[1]{0:T(128)} %bitcast.spot_ref, bf16[256,256]{1,0:T(8,128)(2,1)} %bitcast.12, bf16[256,256]{1,0:T(8,128)(2,1)} %bitcast.13), custom_call_target="tpu_custom_call" | custom-call | bytes 1441796 | tf_op jit(solution)/shard_map/pallas_call | solution.py:254
  2.7 0.0 copy-start
  2.7 6.1 %all-to-all-start = ((bf16[8,288,256]{2,1,0:T(8,128)(2,1)}), bf16[8,288,256]{2,1,0:T(8,128)(2,1)S(1)}, u32[]{:S(2)}, u32[]{:S(2)}) async-start(bf16[8,288,256]{2,1,0:T(8,128)(2,1)} %shard_map.58), calls=%async_computation | async-start | bytes 2359296 | tf_op jit(solution)/shard_map/all_to_all | solution.py:307
  8.8 3.8 %collective-permute-start = (bf16[27,16,256]{2,1,0:T(8,128)(2,1)S(1)}, bf16[27,16,256]{2,1,0:T(8,128)(2,1)S(1)}, u32[]{:S(2)}, u32[]{:S(2)}) collective-permute-start(bf16[27,16,256]{2,1,0:T(8,128)(2,1)S(1)} %bitcast.14), channel_id=1, source_target_pairs={{0,0},{1,33},{2,34},{3,3},{4,68},{5,101},{6,102},{7,71},{8,136},{9... | collective-permute-start | bytes 663560 | tf_op jit(solution)/shard_map/ppermute | solution.py:289
  12.6 4.0 %collective-permute-done.same_ref = bf16[27,16,256]{2,1,0:T(8,128)(2,1)S(1)} collective-permute-done((bf16[27,16,256]{2,1,0:T(8,128)(2,1)S(1)}, bf16[27,16,256]{2,1,0:T(8,128)(2,1)S(1)}, u32[]{:S(2)}, u32[]{:S(2)}) %collective-permute-start) | collective-permute-done | bytes 221216 | tf_op jit(solution)/shard_map/ppermute | solution.py:289
  16.6 3.5 %collective-permute-start.1 = (bf16[27,16,256]{2,1,0:T(8,128)(2,1)S(1)}, bf16[27,16,256]{2,1,0:T(8,128)(2,1)S(1)}, u32[]{:S(2)}, u32[]{:S(2)}) collective-permute-start(bf16[27,16,256]{2,1,0:T(8,128)(2,1)S(1)} %collective-permute-done.same_ref), channel_id=1, source_target_pairs={{0,16},{16,0},{32,48},{48,32},{64,80},{80,64},{96,112},{112,96},{1... | collective-permute-start | bytes 663560 | tf_op jit(solution)/shard_map/ppermute | solution.py:290
  20.1 1.1 %collective-permute-done.1.opposite_ref = bf16[27,16,256]{2,1,0:T(8,128)(2,1)S(1)} collective-permute-done((bf16[27,16,256]{2,1,0:T(8,128)(2,1)S(1)}, bf16[27,16,256]{2,1,0:T(8,128)(2,1)S(1)}, u32[]{:S(2)}, u32[]{:S(2)}) %collective-permute-start.1) | collective-permute-done | bytes 221216 | tf_op jit(solution)/shard_map/ppermute | solution.py:290
  21.2 3.5 %all-to-all-done.r_ref = bf16[8,288,256]{2,1,0:T(8,128)(2,1)S(1)} async-done(((bf16[8,288,256]{2,1,0:T(8,128)(2,1)}), bf16[8,288,256]{2,1,0:T(8,128)(2,1)S(1)}, u32[]{:S(2)}, u32[]{:S(2)}) %all-to-all-start) | async-done | bytes 1179680 | tf_op jit(solution)/shard_map/all_to_all | solution.py:307
  24.7 6.0 %shard_map.59 = (bf16[8,288,256]{2,1,0:T(8,128)(2,1)}, f32[448,256]{1,0:T(8,128)S(1)}, bf16[448,256]{1,0:T(8,128)(2,1)S(1)}) custom-call(s32[1]{0:T(128)} %bitcast.1.core_ref, bf16[8,288,256]{2,1,0:T(8,128)(2,1)S(1)} %all-to-all-done.r_ref, bf16[27,16,256]{2,1,0:T(8,128)(2,1)S(1)} %collective-permute-done.same_ref, ...), custom_call_target="tpu_custom_call" | custom-call | flops 2818572288 | bytes 3489796 | tf_op jit(solution)/shard_map/pallas_call | solution.py:254
  30.8 7.3 %all-to-all-start.1 = ((bf16[8,288,256]{2,1,0:T(8,128)(2,1)}), bf16[8,288,256]{2,1,0:T(8,128)(2,1)S(1)}, u32[]{:S(2)}, u32[]{:S(2)}) async-start(bf16[8,288,256]{2,1,0:T(8,128)(2,1)} %get-tuple-element.10), calls=%async_computation.1 | async-start | bytes 2359296 | tf_op jit(solution)/shard_map/all_to_all | solution.py:325
  38.0 0.0 collective-permute-start.2
  38.0 1.5 %collective-permute-done.2.got_ref = bf16[448,256]{1,0:T(8,128)(2,1)S(1)} collective-permute-done((bf16[448,256]{1,0:T(8,128)(2,1)S(1)}, bf16[448,256]{1,0:T(8,128)(2,1)S(1)}, u32[]{:S(2)}, u32[]{:S(2)}) %collective-permute-start.2) | collective-permute-done | bytes 229408 | tf_op jit(solution)/shard_map/ppermute | solution.py:336
  39.5 0.1 shard_map.61
  39.6 1.6 %collective-permute-start.3 = (bf16[224,256]{1,0:T(8,128)(2,1)S(1)}, bf16[224,256]{1,0:T(8,128)(2,1)S(1)}, u32[]{:S(2)}, u32[]{:S(2)}) collective-permute-start(bf16[224,256]{1,0:T(8,128)(2,1)S(1)} %get-tuple-element.16), channel_id=1, source_target_pairs={{0,3},{1,2},{2,1},{3,0},{4,7},{5,6},{6,5},{7,4},{8,11},{9,10},{10,... | collective-permute-start | bytes 344072 | tf_op jit(solution)/shard_map/ppermute | solution.py:346
  41.2 3.6 %collective-permute-done.3.got_ref = bf16[224,256]{1,0:T(8,128)(2,1)S(1)} collective-permute-done((bf16[224,256]{1,0:T(8,128)(2,1)S(1)}, bf16[224,256]{1,0:T(8,128)(2,1)S(1)}, u32[]{:S(2)}, u32[]{:S(2)}) %collective-permute-start.3) | collective-permute-done | bytes 114720 | tf_op jit(solution)/shard_map/ppermute | solution.py:346
  44.9 3.4 %collective-permute-start.4 = (bf16[224,256]{1,0:T(8,128)(2,1)S(1)}, bf16[224,256]{1,0:T(8,128)(2,1)S(1)}, u32[]{:S(2)}, u32[]{:S(2)}) collective-permute-start(bf16[224,256]{1,0:T(8,128)(2,1)S(1)} %shard_map.62), channel_id=1, source_target_pairs={{0,0},{1,33},{2,34},{3,3},{4,68},{5,101},{6,102},{7,71},{8,136},{9... | collective-permute-start | bytes 344072 | tf_op jit(solution)/shard_map/ppermute | solution.py:348
  48.3 3.3 %collective-permute-done.4.rows_ref = bf16[224,256]{1,0:T(8,128)(2,1)S(1)} collective-permute-done((bf16[224,256]{1,0:T(8,128)(2,1)S(1)}, bf16[224,256]{1,0:T(8,128)(2,1)S(1)}, u32[]{:S(2)}, u32[]{:S(2)}) %collective-permute-start.4) | collective-permute-done | bytes 114720 | tf_op jit(solution)/shard_map/ppermute | solution.py:348
  51.6 2.7 %all-to-all-done.1.r_ref.after_ref = bf16[8,288,256]{2,1,0:T(8,128)(2,1)S(1)} async-done(((bf16[8,288,256]{2,1,0:T(8,128)(2,1)}), bf16[8,288,256]{2,1,0:T(8,128)(2,1)S(1)}, u32[]{:S(2)}, u32[]{:S(2)}) %all-to-all-start.1) | async-done | bytes 1179680 | tf_op jit(solution)/shard_map/all_to_all | solution.py:325
  54.3 15.3 %all_to_all.20.parts_ref = bf16[8,32,256]{2,1,0:T(8,128)(2,1)S(1)} all-to-all(bf16[8,32,256]{2,1,0:T(8,128)(2,1)S(1)} %bitcast.10), channel_id=1, replica_groups=mesh['fsdp'=16,'slab'=8,'rep'=2] {'slab'}, dimensions={0} | all-to-all | bytes 262144 | tf_op jit(solution)/shard_map/all_to_all | solution.py:350
  69.6 0.7 shard_map.64
  70.3 6.9 %all-to-all-start.3 = ((bf16[16,32,256]{2,1,0:T(8,128)(2,1)}), bf16[16,32,256]{2,1,0:T(8,128)(2,1)S(1)}, u32[]{:S(2)}, u32[]{:S(2)}) async-start(bf16[16,32,256]{2,1,0:T(8,128)(2,1)} %shard_map.64), calls=%async_computation.3 | async-start | bytes 524288 | tf_op jit(solution)/shard_map/all_to_all | solution.py:352
  77.2 0.9 %shard_map.60 = (bf16[256,256]{1,0:T(8,128)(2,1)}, bf16[256,256]{1,0:T(8,128)(2,1)}) custom-call(s32[1]{0:T(128)} %bitcast.spot_ref, bf16[8,288,256]{2,1,0:T(8,128)(2,1)S(1)} %all-to-all-done.1.r_ref.after_ref), custom_call_target="tpu_custom_call" | custom-call | bytes 1441796 | tf_op jit(solution)/shard_map/pallas_call | solution.py:254
  78.1 6.2 %all-to-all-done.3.parts_ref = bf16[16,32,256]{2,1,0:T(8,128)(2,1)S(1)} async-done(((bf16[16,32,256]{2,1,0:T(8,128)(2,1)}), bf16[16,32,256]{2,1,0:T(8,128)(2,1)S(1)}, u32[]{:S(2)}, u32[]{:S(2)}) %all-to-all-start.3) | async-done | bytes 262176 | tf_op jit(solution)/shard_map/all_to_all | solution.py:352
  84.3 0.8 shard_map.65
  (3 shorter events, 0.0 us)
Async XLA Ops:
  2.7 6.1 %copy-start = (bf16[16,27,256]{2,0,1:T(8,128)(2,1)S(1)}, bf16[16,27,256]{2,0,1:T(8,128)(2,1)}, u32[]{:S(2)}) copy-start(bf16[16,27,256]{2,0,1:T(8,128)(2,1)} %param.4) | copy-start | bytes 663556
  2.7 22.0 %all-to-all-start = ((bf16[8,288,256]{2,1,0:T(8,128)(2,1)}), bf16[8,288,256]{2,1,0:T(8,128)(2,1)S(1)}, u32[]{:S(2)}, u32[]{:S(2)}) async-start(bf16[8,288,256]{2,1,0:T(8,128)(2,1)} %shard_map.58), calls=%async_computation | async-start | bytes 2359296 | tf_op jit(solution)/shard_map/all_to_all | solution.py:307
  8.8 7.8 %collective-permute-start = (bf16[27,16,256]{2,1,0:T(8,128)(2,1)S(1)}, bf16[27,16,256]{2,1,0:T(8,128)(2,1)S(1)}, u32[]{:S(2)}, u32[]{:S(2)}) collective-permute-start(bf16[27,16,256]{2,1,0:T(8,128)(2,1)S(1)} %bitcast.14), channel_id=1, source_target_pairs={{0,0},{1,33},{2,34},{3,3},{4,68},{5,101},{6,102},{7,71},{8,136},{9... | collective-permute-start | bytes 663560 | tf_op jit(solution)/shard_map/ppermute | solution.py:289
  16.6 4.6 %collective-permute-start.1 = (bf16[27,16,256]{2,1,0:T(8,128)(2,1)S(1)}, bf16[27,16,256]{2,1,0:T(8,128)(2,1)S(1)}, u32[]{:S(2)}, u32[]{:S(2)}) collective-permute-start(bf16[27,16,256]{2,1,0:T(8,128)(2,1)S(1)} %collective-permute-done.same_ref), channel_id=1, source_target_pairs={{0,16},{16,0},{32,48},{48,32},{64,80},{80,64},{96,112},{112,96},{1... | collective-permute-start | bytes 663560 | tf_op jit(solution)/shard_map/ppermute | solution.py:290
  30.8 23.5 %all-to-all-start.1 = ((bf16[8,288,256]{2,1,0:T(8,128)(2,1)}), bf16[8,288,256]{2,1,0:T(8,128)(2,1)S(1)}, u32[]{:S(2)}, u32[]{:S(2)}) async-start(bf16[8,288,256]{2,1,0:T(8,128)(2,1)} %get-tuple-element.10), calls=%async_computation.1 | async-start | bytes 2359296 | tf_op jit(solution)/shard_map/all_to_all | solution.py:325
  38.0 1.5 %collective-permute-start.2 = (bf16[448,256]{1,0:T(8,128)(2,1)S(1)}, bf16[448,256]{1,0:T(8,128)(2,1)S(1)}, u32[]{:S(2)}, u32[]{:S(2)}) collective-permute-start(bf16[448,256]{1,0:T(8,128)(2,1)S(1)} %get-tuple-element.14), channel_id=1, source_target_pairs={{0,16},{16,0},{32,48},{48,32},{64,80},{80,64},{96,112},{112,96},{1... | collective-permute-start | bytes 688136 | tf_op jit(solution)/shard_map/ppermute | solution.py:336
  39.6 5.3 %collective-permute-start.3 = (bf16[224,256]{1,0:T(8,128)(2,1)S(1)}, bf16[224,256]{1,0:T(8,128)(2,1)S(1)}, u32[]{:S(2)}, u32[]{:S(2)}) collective-permute-start(bf16[224,256]{1,0:T(8,128)(2,1)S(1)} %get-tuple-element.16), channel_id=1, source_target_pairs={{0,3},{1,2},{2,1},{3,0},{4,7},{5,6},{6,5},{7,4},{8,11},{9,10},{10,... | collective-permute-start | bytes 344072 | tf_op jit(solution)/shard_map/ppermute | solution.py:346
  44.9 6.7 %collective-permute-start.4 = (bf16[224,256]{1,0:T(8,128)(2,1)S(1)}, bf16[224,256]{1,0:T(8,128)(2,1)S(1)}, u32[]{:S(2)}, u32[]{:S(2)}) collective-permute-start(bf16[224,256]{1,0:T(8,128)(2,1)S(1)} %shard_map.62), channel_id=1, source_target_pairs={{0,0},{1,33},{2,34},{3,3},{4,68},{5,101},{6,102},{7,71},{8,136},{9... | collective-permute-start | bytes 344072 | tf_op jit(solution)/shard_map/ppermute | solution.py:348
  70.3 13.9 %all-to-all-start.3 = ((bf16[16,32,256]{2,1,0:T(8,128)(2,1)}), bf16[16,32,256]{2,1,0:T(8,128)(2,1)S(1)}, u32[]{:S(2)}, u32[]{:S(2)}) async-start(bf16[16,32,256]{2,1,0:T(8,128)(2,1)} %shard_map.64), calls=%async_computation.3 | async-start | bytes 524288 | tf_op jit(solution)/shard_map/all_to_all | solution.py:352

commit v9 on v7

--- a/solution.py
+++ b/solution.py
@@ -21,11 +21,11 @@
     return (along_x * 3 + along_y) * 3 + along_z
 
 
-def home(pair, core, chip):
-    return (pair + 4 * core + chip) & 7
-
-
-def pack_kernel(chip_ref, x_ref, u_ref, out_ref, x_own, u_own, turned, sems):
+def home(pair, core, spot_ref):
+    return ((pair + 4 * core + spot_ref[0]) & 7) ^ (spot_ref[0] >> 3)
+
+
+def pack_kernel(spot_ref, x_ref, u_ref, out_ref, x_own, u_own, turned, sems):
     take_u = pltpu.make_async_copy(u_ref, u_own, sems.at[0])
     takes_x = [
         pltpu.make_async_copy(x_ref.at[rows, :], x_own.at[rows, :], sems.at[1 + part])
@@ -50,7 +50,7 @@
     for pair in range(SLABS):
         for core in range(2):
             start = pair * OUTS + core * 16
-            turned[home(pair, core, chip_ref[0]), core * 16 : core * 16 + 16, :] = by_out[
+            turned[home(pair, core, spot_ref), core * 16 : core * 16 + 16, :] = by_out[
                 start : start + 16
             ]
     last = pltpu.make_async_copy(
@@ -79,12 +79,27 @@
 
 
 def main_kernel(
-    core_ref, r_ref, same_ref, opposite_ref, out_ref, own_ref, other_ref, g_ref, w2_ref, z_ref
+    corner_ref,
+    r_ref,
+    mine_ref,
+    got_ref,
+    mine_opposite_ref,
+    got_opposite_ref,
+    out_ref,
+    own_ref,
+    other_ref,
+    g_ref,
+    w2_ref,
+    z_ref,
 ):
-    first = core_ref[0] == 0
+    first = (corner_ref[0] & 1) == 0
+    lower = corner_ref[0] < 2
     for tap in range(TAPS):
         start = tap * OUTS
-        same, opposite = same_ref[tap], opposite_ref[tap]
+        place = tap if tap < 14 else tap - 13
+        leads = lower if tap < 14 else jnp.logical_not(lower)
+        same = jnp.where(leads, mine_ref[place], got_ref[place])
+        opposite = jnp.where(leads, mine_opposite_ref[place], got_opposite_ref[place])
         w2_ref[start : start + 16, :] = jnp.where(first, same, opposite)
         w2_ref[start + 16 : start + 32, :] = jnp.where(first, opposite, same)
     w2_ref[TAPS * OUTS :, :] = jnp.zeros((OUTS, CELLS), BF16)
@@ -194,7 +209,7 @@
         out_ref[place] = total.astype(BF16)
 
 
-def final_kernel(chip_ref, r_ref, act_ref, grad_ref):
+def final_kernel(spot_ref, r_ref, act_ref, grad_ref):
     total = r_ref[0, :CELLS, :].astype(F32)
     for slab in range(1, SLABS):
         total = total + r_ref[slab, :CELLS, :].astype(F32)
@@ -204,7 +219,7 @@
             jnp.concatenate(
                 [
                     r_ref[
-                        home(pair, core, chip_ref[0]),
+                        home(pair, core, spot_ref),
                         CELLS + core * 16 : CELLS + core * 16 + 16,
                         :,
                     ].astype(F32)
@@ -242,8 +257,9 @@
 
 def local(inputs, weights, upstream):
     owner = lax.axis_index("fsdp")
-    core = (owner % 2).astype(jnp.int32).reshape(1)
-    chip = (owner // 2).astype(jnp.int32).reshape(1)
+    rep_here = lax.axis_index("rep")
+    corner = (owner % 2 + 2 * rep_here).astype(jnp.int32).reshape(1)
+    spot = (owner // 2 + 8 * rep_here).astype(jnp.int32).reshape(1)
     chips = lax.axis_size("fsdp") // 2
     reps = lax.axis_size("rep")
     total_cells = 2 * chips * reps * WHOLE
@@ -254,7 +270,7 @@
 
     everyone = ("fsdp", "slab", "rep")
     mirrored = [
-        (place(z, core, y, rep), place((y + 4 * core - z) % SLABS, core, y, rep))
+        (place(z, core, y, rep), place(((y ^ rep) + 4 * core - z) % SLABS, core, y, rep))
         for z in range(chips)
         for core in range(2)
         for y in range(SLABS)
@@ -263,14 +279,23 @@
     cores = [(2 * z + core, 2 * z + 1 - core) for z in range(chips) for core in range(2)]
 
     by_tap = jnp.transpose(weights, (1, 0, 2))
-    same = lax.ppermute(by_tap, everyone, mirrored)
-    opposite = lax.ppermute(same, "fsdp", cores)
+    beside = [
+        (place(z, core, y, rep), place(z, core, y ^ 1, 1 - rep))
+        for z in range(chips)
+        for core in range(2)
+        for y in range(SLABS)
+        for rep in range(reps)
+    ]
+    mine = lax.dynamic_slice_in_dim(by_tap, 13 * rep_here, 14, axis=0)
+    mine = lax.ppermute(mine, everyone, mirrored)
+    got = lax.ppermute(mine, everyone, beside)
+    halves = (mine, got, lax.ppermute(mine, "fsdp", cores), lax.ppermute(got, "fsdp", cores))
 
     cells = inputs.reshape(CELLS, CELLS)
     packed = call(
         pack_kernel,
         [shape(SLABS, CELLS + OUTS, CELLS)],
-        (chip, cells, upstream.reshape(CELLS, CELLS)),
+        (spot, cells, upstream.reshape(CELLS, CELLS)),
         specs=[SMEM, HBM, HBM],
         scratch=[
             pltpu.VMEM((CELLS, CELLS), BF16),
@@ -290,8 +315,8 @@
             shape(TAPS * 16, CELLS, dtype=F32),
             shape(TAPS * 16, CELLS),
         ],
-        (core, gathered, same, opposite),
-        specs=[SMEM, VMEM, VMEM, VMEM],
+        (corner, gathered, *halves),
+        specs=[SMEM] + [VMEM] * 5,
         scratch=[
             pltpu.VMEM((ROWS, WHOLE), BF16),
             pltpu.VMEM((ROWS, CELLS), BF16),
@@ -303,7 +328,7 @@
     activated, input_grad = call(
         final_kernel,
         [shape(CELLS, CELLS), shape(CELLS, CELLS)],
-        (chip, returned),
+        (spot, returned),
         specs=[SMEM, VMEM],
     )
 

time: 83.9 us -> 86.3 us (1.029)
  the two profiles are of different devices: /device:TPU:2 before, /device:TPU:32 now
where the time goes in v9:
time: 86.3 us; the launch traced here: 86 us
  waiting for transfers between devices  30 us (35%)
  starting transfers between devices  29.1 us (34%)
  blocking collectives  15.4 us (18%)
  Pallas kernels  9.91 us (11%)
    all_to_all x1, blocking collectives, local(): lax.all_to_all(sums.reshape(plane, 512 // plane, CELLS), ('slab', 'rep'),...  15.4 us
    pallas_call x6, Pallas kernels, call(): pl.pallas_call(kernel, out_shape=tuple(outs), in_specs=specs or [VMEM] *...  9.91 us
    ppermute x1, waiting for transfers between devices, local(): sums = lax.ppermute(sums, everyone, mirrored)  8.76 us
    all_to_all x1, waiting for transfers between devices, local(): parts = lax.all_to_all(share, ('slab', 'rep'), 0, 0).astype(F32)  7.52 us
    ppermute x1, starting transfers between devices, local(): mine = lax.ppermute(mine, everyone, mirrored)  7.31 us
    all_to_all x1, starting transfers between devices, local(): returned = lax.all_to_all(terms, 'slab', 0, 0)  6.41 us
    all_to_all x1, starting transfers between devices, local(): gathered = lax.all_to_all(packed, 'slab', 0, 0)  5.41 us
    ppermute x1, waiting for transfers between devices, local(): mine = lax.ppermute(mine, everyone, mirrored)  4.18 us
  transfers between devices with their start and end apart: 9, of which 7 were waited for; matrix products, arithmetic and copies ran while one was open for 0% of the time, Pallas kernels for 1%

profile of v9, /device:TPU:32, one launch (start us, length us, event | category | flops | bytes accessed | tf_op | source)
XLA Modules:
  0.0 86.0 jit_solution(10242739896719340802)
XLA Ops:
  0.6 0.0 copy-start
  0.7 2.1 %shard_map.58 = bf16[8,288,256]{2,1,0:T(8,128)(2,1)} custom-call(s32[1]{0:T(128)} %bitcast.spot_ref, bf16[256,256]{1,0:T(8,128)(2,1)} %bitcast.14, bf16[256,256]{1,0:T(8,128)(2,1)} %bitcast.15), custom_call_target="tpu_custom_call" | custom-call | bytes 1441796 | tf_op jit(solution)/shard_map/pallas_call | solution.py:247
  2.7 5.4 %all-to-all-start = ((bf16[8,288,256]{2,1,0:T(8,128)(2,1)}), bf16[8,288,256]{2,1,0:T(8,128)(2,1)S(1)}, u32[]{:S(2)}, u32[]{:S(2)}) async-start(bf16[8,288,256]{2,1,0:T(8,128)(2,1)} %shard_map.58), calls=%async_computation | async-start | bytes 2359296 | tf_op jit(solution)/shard_map/all_to_all | solution.py:309
  8.2 7.3 %collective-permute-start = (bf16[14,16,256]{2,1,0:T(8,128)(2,1)S(1)}, bf16[14,16,256]{2,1,0:T(8,128)(2,1)S(1)}, u32[]{:S(2)}, u32[]{:S(2)}) collective-permute-start(bf16[14,16,256]{2,1,0:T(8,128)(2,1)S(1)} %dynamic-slice_bitcast_fusion), channel_id=1, source_target_pairs={{0,0},{1,33},{2,34},{3,3},{4,68},{5,101},{6,102},{7,71},{8,136},{9... | collective-permute-start | bytes 344072 | tf_op jit(solution)/shard_map/ppermute | solution.py:290
  15.5 4.2 %collective-permute-done.mine_ref = bf16[14,16,256]{2,1,0:T(8,128)(2,1)S(1)} collective-permute-done((bf16[14,16,256]{2,1,0:T(8,128)(2,1)S(1)}, bf16[14,16,256]{2,1,0:T(8,128)(2,1)S(1)}, u32[]{:S(2)}, u32[]{:S(2)}) %collective-permute-start) | collective-permute-done | bytes 114720 | tf_op jit(solution)/shard_map/ppermute | solution.py:290
  19.7 3.2 %collective-permute-start.1 = (bf16[14,16,256]{2,1,0:T(8,128)(2,1)S(1)}, bf16[14,16,256]{2,1,0:T(8,128)(2,1)S(1)}, u32[]{:S(2)}, u32[]{:S(2)}) collective-permute-start(bf16[14,16,256]{2,1,0:T(8,128)(2,1)S(1)} %collective-permute-done.mine_ref), channel_id=1, source_target_pairs={{0,3},{1,2},{2,1},{3,0},{4,7},{5,6},{6,5},{7,4},{8,11},{9,10},{10,... | collective-permute-start | bytes 344072 | tf_op jit(solution)/shard_map/ppermute | solution.py:291
  22.9 0.0 collective-permute-start.2
  22.9 2.8 %collective-permute-done.1.got_ref = bf16[14,16,256]{2,1,0:T(8,128)(2,1)S(1)} collective-permute-done((bf16[14,16,256]{2,1,0:T(8,128)(2,1)S(1)}, bf16[14,16,256]{2,1,0:T(8,128)(2,1)S(1)}, u32[]{:S(2)}, u32[]{:S(2)}) %collective-permute-start.1) | collective-permute-done | bytes 114720 | tf_op jit(solution)/shard_map/ppermute | solution.py:291
  25.7 0.0 collective-permute-start.3
  25.7 0.0 collective-permute-done.2.mine_opposite_ref
  25.7 1.3 %collective-permute-done.3.got_opposite_ref = bf16[14,16,256]{2,1,0:T(8,128)(2,1)S(1)} collective-permute-done((bf16[14,16,256]{2,1,0:T(8,128)(2,1)S(1)}, bf16[14,16,256]{2,1,0:T(8,128)(2,1)S(1)}, u32[]{:S(2)}, u32[]{:S(2)}) %collective-permute-start.3) | collective-permute-done | bytes 114720 | tf_op jit(solution)/shard_map/ppermute | solution.py:292
  27.0 6.1 %shard_map.59 = (bf16[8,288,256]{2,1,0:T(8,128)(2,1)}, f32[432,256]{1,0:T(8,128)S(1)}, bf16[432,256]{1,0:T(8,128)(2,1)S(1)}) custom-call(s32[1]{0:T(128)} %bitcast.1.corner_ref, bf16[8,288,256]{2,1,0:T(8,128)(2,1)S(1)} %all-to-all-done.r_ref, bf16[14,16,256]{2,1,0:T(8,128)(2,1)S(1)} %collective-permute-done.mine_ref, ...), custom_call_target="tpu_custom_call" | custom-call | flops 2818572288 | bytes 3481604 | tf_op jit(solution)/shard_map/pallas_call | solution.py:247
  33.1 6.4 %all-to-all-start.1 = ((bf16[8,288,256]{2,1,0:T(8,128)(2,1)}), bf16[8,288,256]{2,1,0:T(8,128)(2,1)S(1)}, u32[]{:S(2)}, u32[]{:S(2)}) async-start(bf16[8,288,256]{2,1,0:T(8,128)(2,1)} %get-tuple-element.8), calls=%async_computation.1 | async-start | bytes 2359296 | tf_op jit(solution)/shard_map/all_to_all | solution.py:327
  39.6 0.0 collective-permute-start.4
  39.6 1.5 %collective-permute-done.4.got_ref = bf16[432,256]{1,0:T(8,128)(2,1)S(1)} collective-permute-done((bf16[432,256]{1,0:T(8,128)(2,1)S(1)}, bf16[432,256]{1,0:T(8,128)(2,1)S(1)}, u32[]{:S(2)}, u32[]{:S(2)}) %collective-permute-start.4) | collective-permute-done | bytes 221216 | tf_op jit(solution)/shard_map/ppermute | solution.py:336
  41.1 3.3 %collective-permute-start.5 = (bf16[432,256]{1,0:T(8,128)(2,1)S(1)}, bf16[432,256]{1,0:T(8,128)(2,1)S(1)}, u32[]{:S(2)}, u32[]{:S(2)}) collective-permute-start(bf16[432,256]{1,0:T(8,128)(2,1)S(1)} %shard_map.61), channel_id=1, source_target_pairs={{0,0},{1,33},{2,34},{3,3},{4,68},{5,101},{6,102},{7,71},{8,136},{9... | collective-permute-start | bytes 663560 | tf_op jit(solution)/shard_map/ppermute | solution.py:338
  44.4 8.8 %collective-permute-done.5.rows_ref = bf16[432,256]{1,0:T(8,128)(2,1)S(1)} collective-permute-done((bf16[432,256]{1,0:T(8,128)(2,1)S(1)}, bf16[432,256]{1,0:T(8,128)(2,1)S(1)}, u32[]{:S(2)}, u32[]{:S(2)}) %collective-permute-start.5) | collective-permute-done | bytes 221216 | tf_op jit(solution)/shard_map/ppermute | solution.py:338
  53.1 3.9 %all-to-all-done.1.r_ref.after_ref = bf16[8,288,256]{2,1,0:T(8,128)(2,1)S(1)} async-done(((bf16[8,288,256]{2,1,0:T(8,128)(2,1)}), bf16[8,288,256]{2,1,0:T(8,128)(2,1)S(1)}, u32[]{:S(2)}, u32[]{:S(2)}) %all-to-all-start.1) | async-done | bytes 1179680 | tf_op jit(solution)/shard_map/all_to_all | solution.py:327
  57.0 15.4 %all_to_all.20.parts_ref = bf16[16,32,256]{2,1,0:T(8,128)(2,1)S(1)} all-to-all(bf16[16,32,256]{2,1,0:T(8,128)(2,1)S(1)} %bitcast.12), channel_id=1, replica_groups=mesh['fsdp'=16,'slab'=8,'rep'=2] {'slab','rep'}, dimensions={0} | all-to-all | bytes 524288 | tf_op jit(solution)/shard_map/all_to_all | solution.py:346
  72.4 0.8 shard_map.63
  73.2 3.5 %all-to-all-start.3 = ((bf16[16,32,256]{2,1,0:T(8,128)(2,1)}), bf16[16,32,256]{2,1,0:T(8,128)(2,1)S(1)}, u32[]{:S(2)}, u32[]{:S(2)}) async-start(bf16[16,32,256]{2,1,0:T(8,128)(2,1)} %shard_map.63), calls=%async_computation.3 | async-start | bytes 524288 | tf_op jit(solution)/shard_map/all_to_all | solution.py:350
  76.7 0.9 %shard_map.60 = (bf16[256,256]{1,0:T(8,128)(2,1)}, bf16[256,256]{1,0:T(8,128)(2,1)}) custom-call(s32[1]{0:T(128)} %bitcast.spot_ref, bf16[8,288,256]{2,1,0:T(8,128)(2,1)S(1)} %all-to-all-done.1.r_ref.after_ref), custom_call_target="tpu_custom_call" | custom-call | bytes 1441796 | tf_op jit(solution)/shard_map/pallas_call | solution.py:247
  77.6 7.5 %all-to-all-done.3 = bf16[16,32,256]{2,1,0:T(8,128)(2,1)S(1)} async-done(((bf16[16,32,256]{2,1,0:T(8,128)(2,1)}), bf16[16,32,256]{2,1,0:T(8,128)(2,1)S(1)}, u32[]{:S(2)}, u32[]{:S(2)}) %all-to-all-start.3) | async-done | bytes 262176 | tf_op jit(solution)/shard_map/all_to_all | solution.py:350
  85.1 0.8 multiply_bitcast_fusion
  (5 shorter events, 0.1 us)
Async XLA Ops:
  0.6 7.5 %copy-start = (bf16[16,27,256]{2,0,1:T(8,128)(2,1)S(1)}, bf16[16,27,256]{2,0,1:T(8,128)(2,1)}, u32[]{:S(2)}) copy-start(bf16[16,27,256]{2,0,1:T(8,128)(2,1)} %param.4) | copy-start | bytes 663556
  2.7 24.3 %all-to-all-start = ((bf16[8,288,256]{2,1,0:T(8,128)(2,1)}), bf16[8,288,256]{2,1,0:T(8,128)(2,1)S(1)}, u32[]{:S(2)}, u32[]{:S(2)}) async-start(bf16[8,288,256]{2,1,0:T(8,128)(2,1)} %shard_map.58), calls=%async_computation | async-start | bytes 2359296 | tf_op jit(solution)/shard_map/all_to_all | solution.py:309
  8.2 11.5 %collective-permute-start = (bf16[14,16,256]{2,1,0:T(8,128)(2,1)S(1)}, bf16[14,16,256]{2,1,0:T(8,128)(2,1)S(1)}, u32[]{:S(2)}, u32[]{:S(2)}) collective-permute-start(bf16[14,16,256]{2,1,0:T(8,128)(2,1)S(1)} %dynamic-slice_bitcast_fusion), channel_id=1, source_target_pairs={{0,0},{1,33},{2,34},{3,3},{4,68},{5,101},{6,102},{7,71},{8,136},{9... | collective-permute-start | bytes 344072 | tf_op jit(solution)/shard_map/ppermute | solution.py:290
  19.7 6.0 %collective-permute-start.1 = (bf16[14,16,256]{2,1,0:T(8,128)(2,1)S(1)}, bf16[14,16,256]{2,1,0:T(8,128)(2,1)S(1)}, u32[]{:S(2)}, u32[]{:S(2)}) collective-permute-start(bf16[14,16,256]{2,1,0:T(8,128)(2,1)S(1)} %collective-permute-done.mine_ref), channel_id=1, source_target_pairs={{0,3},{1,2},{2,1},{3,0},{4,7},{5,6},{6,5},{7,4},{8,11},{9,10},{10,... | collective-permute-start | bytes 344072 | tf_op jit(solution)/shard_map/ppermute | solution.py:291
  22.9 2.8 %collective-permute-start.2 = (bf16[14,16,256]{2,1,0:T(8,128)(2,1)S(1)}, bf16[14,16,256]{2,1,0:T(8,128)(2,1)S(1)}, u32[]{:S(2)}, u32[]{:S(2)}) collective-permute-start(bf16[14,16,256]{2,1,0:T(8,128)(2,1)S(1)} %collective-permute-done.mine_ref), channel_id=1, source_target_pairs={{0,16},{16,0},{32,48},{48,32},{64,80},{80,64},{96,112},{112,96},{1... | collective-permute-start | bytes 344072 | tf_op jit(solution)/shard_map/ppermute | solution.py:292
  25.7 1.3 %collective-permute-start.3 = (bf16[14,16,256]{2,1,0:T(8,128)(2,1)S(1)}, bf16[14,16,256]{2,1,0:T(8,128)(2,1)S(1)}, u32[]{:S(2)}, u32[]{:S(2)}) collective-permute-start(bf16[14,16,256]{2,1,0:T(8,128)(2,1)S(1)} %collective-permute-done.1.got_ref), channel_id=1, source_target_pairs={{0,16},{16,0},{32,48},{48,32},{64,80},{80,64},{96,112},{112,96},{1... | collective-permute-start | bytes 344072 | tf_op jit(solution)/shard_map/ppermute | solution.py:292
  33.1 23.9 %all-to-all-start.1 = ((bf16[8,288,256]{2,1,0:T(8,128)(2,1)}), bf16[8,288,256]{2,1,0:T(8,128)(2,1)S(1)}, u32[]{:S(2)}, u32[]{:S(2)}) async-start(bf16[8,288,256]{2,1,0:T(8,128)(2,1)} %get-tuple-element.8), calls=%async_computation.1 | async-start | bytes 2359296 | tf_op jit(solution)/shard_map/all_to_all | solution.py:327
  39.6 1.5 %collective-permute-start.4 = (bf16[432,256]{1,0:T(8,128)(2,1)S(1)}, bf16[432,256]{1,0:T(8,128)(2,1)S(1)}, u32[]{:S(2)}, u32[]{:S(2)}) collective-permute-start(bf16[432,256]{1,0:T(8,128)(2,1)S(1)} %get-tuple-element.12), channel_id=1, source_target_pairs={{0,16},{16,0},{32,48},{48,32},{64,80},{80,64},{96,112},{112,96},{1... | collective-permute-start | bytes 663560 | tf_op jit(solution)/shard_map/ppermute | solution.py:336
  41.1 12.0 %collective-permute-start.5 = (bf16[432,256]{1,0:T(8,128)(2,1)S(1)}, bf16[432,256]{1,0:T(8,128)(2,1)S(1)}, u32[]{:S(2)}, u32[]{:S(2)}) collective-permute-start(bf16[432,256]{1,0:T(8,128)(2,1)S(1)} %shard_map.61), channel_id=1, source_target_pairs={{0,0},{1,33},{2,34},{3,3},{4,68},{5,101},{6,102},{7,71},{8,136},{9... | collective-permute-start | bytes 663560 | tf_op jit(solution)/shard_map/ppermute | solution.py:338
  73.2 12.0 %all-to-all-start.3 = ((bf16[16,32,256]{2,1,0:T(8,128)(2,1)}), bf16[16,32,256]{2,1,0:T(8,128)(2,1)S(1)}, u32[]{:S(2)}, u32[]{:S(2)}) async-start(bf16[16,32,256]{2,1,0:T(8,128)(2,1)} %shard_map.63), calls=%async_computation.3 | async-start | bytes 524288 | tf_op jit(solution)/shard_map/all_to_all | solution.py:350

commit v10 on v7

--- a/solution.py
+++ b/solution.py
@@ -182,8 +182,16 @@
 
 
 def lengthen_kernel(rows_ref, after_ref, out_ref):
-    out_ref[: TAPS * 16, :] = rows_ref[...]
-    out_ref[TAPS * 16 :, :] = jnp.zeros((out_ref.shape[0] - TAPS * 16, CELLS), BF16)
+    rows = out_ref.shape[1]
+    reps = out_ref.shape[0] // SLABS
+    for slab in range(SLABS):
+        held = max(0, min(rows, TAPS * 16 - slab * rows))
+        for rep in range(reps):
+            place = slab * reps + rep
+            if held > 0:
+                out_ref[place, :held, :] = rows_ref[slab * rows : slab * rows + held, :]
+            if held < rows:
+                out_ref[place, held:, :] = jnp.zeros((rows - held, CELLS), BF16)
 
 
 def share_kernel(parts_ref, out_ref):
@@ -313,16 +321,11 @@
     sums = lax.ppermute(sums, everyone, mirrored)
     plane = SLABS * reps
     sums = call(
-        lengthen_kernel,
-        [shape(512, CELLS)],
-        (sums, returned),
-        specs=[VMEM, ANY],
+        lengthen_kernel, [shape(plane, 64, CELLS)], (sums, returned), specs=[VMEM, ANY]
     )[0]
-    scattered = lax.all_to_all(
-        sums.reshape(plane, 512 // plane, CELLS), ("slab", "rep"), 0, 0
-    )
-    share = call(share_kernel, [shape(plane, 512 // plane, CELLS)], (scattered,))[0]
-    parts = lax.all_to_all(share, ("slab", "rep"), 0, 0).astype(F32)
+    scattered = lax.all_to_all(sums, ("slab", "rep"), 0, 0)
+    share = call(share_kernel, [shape(SLABS, 64, CELLS)], (scattered,))[0]
+    parts = lax.all_to_all(share, "slab", 0, 0).astype(F32)
     weight_grad = jnp.transpose(parts.reshape(32, 16, CELLS)[:TAPS], (1, 0, 2)) * factor
     return (
         activated.reshape(inputs.shape),

time: 83.9 us -> 84 us (level)
  waiting for transfers between devices: 27.6 us -> 26.6 us
    all_to_all x1, waiting for transfers between devices: 6.19 us -> 5.24 us  [local(): parts = lax.all_to_all(share, 'slab', 0, 0).astype(F32)]
    all_to_all x1, blocking collectives: 15.7 us -> 16.5 us  [local(): scattered = lax.all_to_all(sums, ('slab', 'rep'), 0, 0)]
where the time goes in v10:
time: 84 us; the launch traced here: 83.6 us
  starting transfers between devices  29.1 us (35%)
  waiting for transfers between devices  26.6 us (32%)
  blocking collectives  16.5 us (20%)
  Pallas kernels  9.85 us (12%)
    all_to_all x1, blocking collectives, local(): scattered = lax.all_to_all(sums, ('slab', 'rep'), 0, 0)  16.5 us
    pallas_call x6, Pallas kernels, call(): pl.pallas_call(kernel, out_shape=tuple(outs), in_specs=specs or [VMEM] *...  9.85 us
    all_to_all x1, starting transfers between devices, local(): returned = lax.all_to_all(terms, 'slab', 0, 0)  7.3 us
    all_to_all x1, waiting for transfers between devices, local(): returned = lax.all_to_all(terms, 'slab', 0, 0)  6.87 us
    all_to_all x1, starting transfers between devices, local(): gathered = lax.all_to_all(packed, 'slab', 0, 0)  6.07 us
    all_to_all x1, waiting for transfers between devices, local(): parts = lax.all_to_all(share, 'slab', 0, 0).astype(F32)  5.24 us
    all_to_all x1, starting transfers between devices, local(): parts = lax.all_to_all(share, 'slab', 0, 0).astype(F32)  5.03 us
    ppermute x1, waiting for transfers between devices, local(): sums = lax.ppermute(sums, everyone, mirrored)  4.39 us
  transfers between devices with their start and end apart: 7, of which 7 were waited for; matrix products, arithmetic and copies ran while one was open for 0% of the time, Pallas kernels for 1%

profile of v10, /device:TPU:2, one launch (start us, length us, event | category | flops | bytes accessed | tf_op | source)
XLA Modules:
  0.0 83.6 jit_solution(18129163761918447653)
XLA Ops:
  0.6 2.0 %shard_map.58 = bf16[8,288,256]{2,1,0:T(8,128)(2,1)} custom-call(s32[1]{0:T(128)} %bitcast.chip_ref, bf16[256,256]{1,0:T(8,128)(2,1)} %bitcast.11, bf16[256,256]{1,0:T(8,128)(2,1)} %bitcast.12), custom_call_target="tpu_custom_call" | custom-call | bytes 1441796 | tf_op jit(solution)/shard_map/pallas_call | solution.py:240
  2.7 0.0 copy-start
  2.7 6.1 %all-to-all-start = ((bf16[8,288,256]{2,1,0:T(8,128)(2,1)}), bf16[8,288,256]{2,1,0:T(8,128)(2,1)S(1)}, u32[]{:S(2)}, u32[]{:S(2)}) async-start(bf16[8,288,256]{2,1,0:T(8,128)(2,1)} %shard_map.58), calls=%async_computation | async-start | bytes 2359296 | tf_op jit(solution)/shard_map/all_to_all | solution.py:292
  8.8 0.0 copy-done
  8.8 3.8 %collective-permute-start = (bf16[27,16,256]{2,1,0:T(8,128)(2,1)S(1)}, bf16[27,16,256]{2,1,0:T(8,128)(2,1)S(1)}, u32[]{:S(2)}, u32[]{:S(2)}) collective-permute-start(bf16[27,16,256]{2,1,0:T(8,128)(2,1)S(1)} %bitcast.13), channel_id=1, source_target_pairs={{0,0},{1,1},{2,34},{3,35},{4,68},{5,69},{6,102},{7,103},{8,136},{9... | collective-permute-start | bytes 663560 | tf_op jit(solution)/shard_map/ppermute | solution.py:274
  12.6 4.0 %collective-permute-done.same_ref = bf16[27,16,256]{2,1,0:T(8,128)(2,1)S(1)} collective-permute-done((bf16[27,16,256]{2,1,0:T(8,128)(2,1)S(1)}, bf16[27,16,256]{2,1,0:T(8,128)(2,1)S(1)}, u32[]{:S(2)}, u32[]{:S(2)}) %collective-permute-start) | collective-permute-done | bytes 221216 | tf_op jit(solution)/shard_map/ppermute | solution.py:274
  16.6 3.5 %collective-permute-start.1 = (bf16[27,16,256]{2,1,0:T(8,128)(2,1)S(1)}, bf16[27,16,256]{2,1,0:T(8,128)(2,1)S(1)}, u32[]{:S(2)}, u32[]{:S(2)}) collective-permute-start(bf16[27,16,256]{2,1,0:T(8,128)(2,1)S(1)} %collective-permute-done.same_ref), channel_id=1, source_target_pairs={{0,16},{16,0},{32,48},{48,32},{64,80},{80,64},{96,112},{112,96},{1... | collective-permute-start | bytes 663560 | tf_op jit(solution)/shard_map/ppermute | solution.py:275
  20.1 1.1 %collective-permute-done.1.opposite_ref = bf16[27,16,256]{2,1,0:T(8,128)(2,1)S(1)} collective-permute-done((bf16[27,16,256]{2,1,0:T(8,128)(2,1)S(1)}, bf16[27,16,256]{2,1,0:T(8,128)(2,1)S(1)}, u32[]{:S(2)}, u32[]{:S(2)}) %collective-permute-start.1) | collective-permute-done | bytes 221216 | tf_op jit(solution)/shard_map/ppermute | solution.py:275
  21.2 3.5 %all-to-all-done.r_ref = bf16[8,288,256]{2,1,0:T(8,128)(2,1)S(1)} async-done(((bf16[8,288,256]{2,1,0:T(8,128)(2,1)}), bf16[8,288,256]{2,1,0:T(8,128)(2,1)S(1)}, u32[]{:S(2)}, u32[]{:S(2)}) %all-to-all-start) | async-done | bytes 1179680 | tf_op jit(solution)/shard_map/all_to_all | solution.py:292
  24.7 6.0 %shard_map.59 = (bf16[8,288,256]{2,1,0:T(8,128)(2,1)}, f32[432,256]{1,0:T(8,128)S(1)}, bf16[432,256]{1,0:T(8,128)(2,1)S(1)}) custom-call(s32[1]{0:T(128)} %bitcast.1.core_ref, bf16[8,288,256]{2,1,0:T(8,128)(2,1)S(1)} %all-to-all-done.r_ref, bf16[27,16,256]{2,1,0:T(8,128)(2,1)S(1)} %collective-permute-done.same_ref, ...), custom_call_target="tpu_custom_call" | custom-call | flops 2818572288 | bytes 3465220 | tf_op jit(solution)/shard_map/pallas_call | solution.py:240
  30.8 7.3 %all-to-all-start.1 = ((bf16[8,288,256]{2,1,0:T(8,128)(2,1)}), bf16[8,288,256]{2,1,0:T(8,128)(2,1)S(1)}, u32[]{:S(2)}, u32[]{:S(2)}) async-start(bf16[8,288,256]{2,1,0:T(8,128)(2,1)} %get-tuple-element.8), calls=%async_computation.1 | async-start | bytes 2359296 | tf_op jit(solution)/shard_map/all_to_all | solution.py:310
  38.0 0.0 collective-permute-start.2
  38.0 1.5 %collective-permute-done.2.got_ref = bf16[432,256]{1,0:T(8,128)(2,1)S(1)} collective-permute-done((bf16[432,256]{1,0:T(8,128)(2,1)S(1)}, bf16[432,256]{1,0:T(8,128)(2,1)S(1)}, u32[]{:S(2)}, u32[]{:S(2)}) %collective-permute-start.2) | collective-permute-done | bytes 221216 | tf_op jit(solution)/shard_map/ppermute | solution.py:319
  39.5 0.1 shard_map.61
  39.6 3.4 %collective-permute-start.3 = (bf16[432,256]{1,0:T(8,128)(2,1)S(1)}, bf16[432,256]{1,0:T(8,128)(2,1)S(1)}, u32[]{:S(2)}, u32[]{:S(2)}) collective-permute-start(bf16[432,256]{1,0:T(8,128)(2,1)S(1)} %shard_map.61), channel_id=1, source_target_pairs={{0,0},{1,1},{2,34},{3,35},{4,68},{5,69},{6,102},{7,103},{8,136},{9... | collective-permute-start | bytes 663560 | tf_op jit(solution)/shard_map/ppermute | solution.py:321
  43.0 4.4 %collective-permute-done.3.rows_ref = bf16[432,256]{1,0:T(8,128)(2,1)S(1)} collective-permute-done((bf16[432,256]{1,0:T(8,128)(2,1)S(1)}, bf16[432,256]{1,0:T(8,128)(2,1)S(1)}, u32[]{:S(2)}, u32[]{:S(2)}) %collective-permute-start.3) | collective-permute-done | bytes 221216 | tf_op jit(solution)/shard_map/ppermute | solution.py:321
  47.4 6.9 %all-to-all-done.1.r_ref.after_ref = bf16[8,288,256]{2,1,0:T(8,128)(2,1)S(1)} async-done(((bf16[8,288,256]{2,1,0:T(8,128)(2,1)}), bf16[8,288,256]{2,1,0:T(8,128)(2,1)S(1)}, u32[]{:S(2)}, u32[]{:S(2)}) %all-to-all-start.1) | async-done | bytes 1179680 | tf_op jit(solution)/shard_map/all_to_all | solution.py:310
  54.3 16.5 %all_to_all.20.parts_ref = bf16[16,64,256]{2,1,0:T(8,128)(2,1)S(1)} all-to-all(bf16[16,64,256]{2,1,0:T(8,128)(2,1)S(1)} %shard_map.62), channel_id=1, replica_groups=mesh['fsdp'=16,'slab'=8,'rep'=2] {'slab','rep'}, dimensions={0} | all-to-all | bytes 1048576 | tf_op jit(solution)/shard_map/all_to_all | solution.py:326
  70.9 0.8 shard_map.63
  71.6 5.0 %all-to-all-start.3 = ((bf16[8,64,256]{2,1,0:T(8,128)(2,1)}), bf16[8,64,256]{2,1,0:T(8,128)(2,1)S(1)}, u32[]{:S(2)}, u32[]{:S(2)}) async-start(bf16[8,64,256]{2,1,0:T(8,128)(2,1)} %shard_map.63), calls=%async_computation.3 | async-start | bytes 524288 | tf_op jit(solution)/shard_map/all_to_all | solution.py:328
  76.7 0.9 %shard_map.60 = (bf16[256,256]{1,0:T(8,128)(2,1)}, bf16[256,256]{1,0:T(8,128)(2,1)}) custom-call(s32[1]{0:T(128)} %bitcast.chip_ref, bf16[8,288,256]{2,1,0:T(8,128)(2,1)S(1)} %all-to-all-done.1.r_ref.after_ref), custom_call_target="tpu_custom_call" | custom-call | bytes 1441796 | tf_op jit(solution)/shard_map/pallas_call | solution.py:240
  77.6 5.2 %all-to-all-done.3 = bf16[8,64,256]{2,1,0:T(8,128)(2,1)S(1)} async-done(((bf16[8,64,256]{2,1,0:T(8,128)(2,1)}), bf16[8,64,256]{2,1,0:T(8,128)(2,1)S(1)}, u32[]{:S(2)}, u32[]{:S(2)}) %all-to-all-start.3) | async-done | bytes 262176 | tf_op jit(solution)/shard_map/all_to_all | solution.py:328
  82.8 0.8 multiply_bitcast_fusion
  (1 shorter events, 0.0 us)
Async XLA Ops:
  2.7 6.1 %copy-start = (bf16[16,27,256]{2,0,1:T(8,128)(2,1)S(1)}, bf16[16,27,256]{2,0,1:T(8,128)(2,1)}, u32[]{:S(2)}) copy-start(bf16[16,27,256]{2,0,1:T(8,128)(2,1)} %param.4) | copy-start | bytes 663556
  2.7 22.0 %all-to-all-start = ((bf16[8,288,256]{2,1,0:T(8,128)(2,1)}), bf16[8,288,256]{2,1,0:T(8,128)(2,1)S(1)}, u32[]{:S(2)}, u32[]{:S(2)}) async-start(bf16[8,288,256]{2,1,0:T(8,128)(2,1)} %shard_map.58), calls=%async_computation | async-start | bytes 2359296 | tf_op jit(solution)/shard_map/all_to_all | solution.py:292
  8.8 7.8 %collective-permute-start = (bf16[27,16,256]{2,1,0:T(8,128)(2,1)S(1)}, bf16[27,16,256]{2,1,0:T(8,128)(2,1)S(1)}, u32[]{:S(2)}, u32[]{:S(2)}) collective-permute-start(bf16[27,16,256]{2,1,0:T(8,128)(2,1)S(1)} %bitcast.13), channel_id=1, source_target_pairs={{0,0},{1,1},{2,34},{3,35},{4,68},{5,69},{6,102},{7,103},{8,136},{9... | collective-permute-start | bytes 663560 | tf_op jit(solution)/shard_map/ppermute | solution.py:274
  16.6 4.6 %collective-permute-start.1 = (bf16[27,16,256]{2,1,0:T(8,128)(2,1)S(1)}, bf16[27,16,256]{2,1,0:T(8,128)(2,1)S(1)}, u32[]{:S(2)}, u32[]{:S(2)}) collective-permute-start(bf16[27,16,256]{2,1,0:T(8,128)(2,1)S(1)} %collective-permute-done.same_ref), channel_id=1, source_target_pairs={{0,16},{16,0},{32,48},{48,32},{64,80},{80,64},{96,112},{112,96},{1... | collective-permute-start | bytes 663560 | tf_op jit(solution)/shard_map/ppermute | solution.py:275
  30.8 23.5 %all-to-all-start.1 = ((bf16[8,288,256]{2,1,0:T(8,128)(2,1)}), bf16[8,288,256]{2,1,0:T(8,128)(2,1)S(1)}, u32[]{:S(2)}, u32[]{:S(2)}) async-start(bf16[8,288,256]{2,1,0:T(8,128)(2,1)} %get-tuple-element.8), calls=%async_computation.1 | async-start | bytes 2359296 | tf_op jit(solution)/shard_map/all_to_all | solution.py:310
  38.0 1.5 %collective-permute-start.2 = (bf16[432,256]{1,0:T(8,128)(2,1)S(1)}, bf16[432,256]{1,0:T(8,128)(2,1)S(1)}, u32[]{:S(2)}, u32[]{:S(2)}) collective-permute-start(bf16[432,256]{1,0:T(8,128)(2,1)S(1)} %get-tuple-element.12), channel_id=1, source_target_pairs={{0,16},{16,0},{32,48},{48,32},{64,80},{80,64},{96,112},{112,96},{1... | collective-permute-start | bytes 663560 | tf_op jit(solution)/shard_map/ppermute | solution.py:319
  39.6 7.8 %collective-permute-start.3 = (bf16[432,256]{1,0:T(8,128)(2,1)S(1)}, bf16[432,256]{1,0:T(8,128)(2,1)S(1)}, u32[]{:S(2)}, u32[]{:S(2)}) collective-permute-start(bf16[432,256]{1,0:T(8,128)(2,1)S(1)} %shard_map.61), channel_id=1, source_target_pairs={{0,0},{1,1},{2,34},{3,35},{4,68},{5,69},{6,102},{7,103},{8,136},{9... | collective-permute-start | bytes 663560 | tf_op jit(solution)/shard_map/ppermute | solution.py:321
  71.6 11.2 %all-to-all-start.3 = ((bf16[8,64,256]{2,1,0:T(8,128)(2,1)}), bf16[8,64,256]{2,1,0:T(8,128)(2,1)S(1)}, u32[]{:S(2)}, u32[]{:S(2)}) async-start(bf16[8,64,256]{2,1,0:T(8,128)(2,1)} %shard_map.63), calls=%async_computation.3 | async-start | bytes 524288 | tf_op jit(solution)/shard_map/all_to_all | solution.py:328

commit v11 on v7

--- a/solution.py
+++ b/solution.py
@@ -15,6 +15,7 @@
 ROWS = 28 * OUTS
 WHOLE = SLABS * CELLS
 COLUMNS = WHOLE // LANES
+AHEAD = 2 * 10**10
 
 
 def tap_index(along_x, along_y, along_z):
@@ -308,7 +309,10 @@
     )
 
     sums = call(
-        add_kernel, [shape(TAPS * 16, CELLS)], (own, lax.ppermute(other, "fsdp", cores))
+        add_kernel,
+        [shape(TAPS * 16, CELLS)],
+        (own, lax.ppermute(other, "fsdp", cores)),
+        flops=AHEAD,
     )[0]
     sums = lax.ppermute(sums, everyone, mirrored)
     plane = SLABS * reps

time: 83.9 us -> 82.6 us (0.985)
  blocking collectives: 15.7 us -> 14 us
    all_to_all x1, waiting for transfers between devices: 6.87 us -> 8.58 us  [local(): returned = lax.all_to_all(terms, 'slab', 0, 0)]
    all_to_all x1, blocking collectives: 15.7 us -> 14 us  [local(): lax.all_to_all(sums.reshape(plane, 512 // plane, CELLS), ('slab', 'rep'),...]
    ppermute x1, waiting for transfers between devices: 1.47 us -> 0.01 us  [local(): lax.ppermute(other, 'fsdp', cores)]
  transfers between devices with their start and end apart: 7 -> 7, of which waited for: 7 -> 6; matrix products, arithmetic and copies ran while one was open for 0% -> 0% of each run, Pallas kernels for 1% -> 1%
where the time goes in v11:
time: 82.6 us; the launch traced here: 82.2 us
  starting transfers between devices  29.1 us (35%)
  waiting for transfers between devices  27.8 us (34%)
  blocking collectives  14 us (17%)
  Pallas kernels  9.81 us (12%)
    all_to_all x1, blocking collectives, local(): lax.all_to_all(sums.reshape(plane, 512 // plane, CELLS), ('slab', 'rep'),...  14 us
    pallas_call x6, Pallas kernels, call(): pl.pallas_call(kernel, out_shape=tuple(outs), in_specs=specs or [VMEM] *...  9.81 us
    all_to_all x1, waiting for transfers between devices, local(): returned = lax.all_to_all(terms, 'slab', 0, 0)  8.58 us
    all_to_all x1, starting transfers between devices, local(): returned = lax.all_to_all(terms, 'slab', 0, 0)  7.44 us
    all_to_all x1, waiting for transfers between devices, local(): parts = lax.all_to_all(share, ('slab', 'rep'), 0, 0).astype(F32)  6.19 us
    all_to_all x1, starting transfers between devices, local(): gathered = lax.all_to_all(packed, 'slab', 0, 0)  6.07 us
    all_to_all x1, starting transfers between devices, local(): parts = lax.all_to_all(share, ('slab', 'rep'), 0, 0).astype(F32)  4.88 us
    ppermute x1, waiting for transfers between devices, local(): sums = lax.ppermute(sums, everyone, mirrored)  4.39 us
  transfers between devices with their start and end apart: 7, of which 6 were waited for; matrix products, arithmetic and copies ran while one was open for 0% of the time, Pallas kernels for 1%

profile of v11, /device:TPU:2, one launch (start us, length us, event | category | flops | bytes accessed | tf_op | source)
XLA Modules:
  0.0 82.2 jit_solution(206158825440745865)
XLA Ops:
  0.6 2.0 %shard_map.58 = bf16[8,288,256]{2,1,0:T(8,128)(2,1)} custom-call(s32[1]{0:T(128)} %bitcast.chip_ref, bf16[256,256]{1,0:T(8,128)(2,1)} %bitcast.13, bf16[256,256]{1,0:T(8,128)(2,1)} %bitcast.14), custom_call_target="tpu_custom_call" | custom-call | bytes 1441796 | tf_op jit(solution)/shard_map/pallas_call | solution.py:233
  2.7 0.0 copy-start
  2.7 6.1 %all-to-all-start = ((bf16[8,288,256]{2,1,0:T(8,128)(2,1)}), bf16[8,288,256]{2,1,0:T(8,128)(2,1)S(1)}, u32[]{:S(2)}, u32[]{:S(2)}) async-start(bf16[8,288,256]{2,1,0:T(8,128)(2,1)} %shard_map.58), calls=%async_computation | async-start | bytes 2359296 | tf_op jit(solution)/shard_map/all_to_all | solution.py:285
  8.8 0.0 copy-done
  8.8 3.8 %collective-permute-start = (bf16[27,16,256]{2,1,0:T(8,128)(2,1)S(1)}, bf16[27,16,256]{2,1,0:T(8,128)(2,1)S(1)}, u32[]{:S(2)}, u32[]{:S(2)}) collective-permute-start(bf16[27,16,256]{2,1,0:T(8,128)(2,1)S(1)} %bitcast.15), channel_id=1, source_target_pairs={{0,0},{1,1},{2,34},{3,35},{4,68},{5,69},{6,102},{7,103},{8,136},{9... | collective-permute-start | bytes 663560 | tf_op jit(solution)/shard_map/ppermute | solution.py:267
  12.6 4.0 %collective-permute-done.same_ref = bf16[27,16,256]{2,1,0:T(8,128)(2,1)S(1)} collective-permute-done((bf16[27,16,256]{2,1,0:T(8,128)(2,1)S(1)}, bf16[27,16,256]{2,1,0:T(8,128)(2,1)S(1)}, u32[]{:S(2)}, u32[]{:S(2)}) %collective-permute-start) | collective-permute-done | bytes 221216 | tf_op jit(solution)/shard_map/ppermute | solution.py:267
  16.6 3.5 %collective-permute-start.1 = (bf16[27,16,256]{2,1,0:T(8,128)(2,1)S(1)}, bf16[27,16,256]{2,1,0:T(8,128)(2,1)S(1)}, u32[]{:S(2)}, u32[]{:S(2)}) collective-permute-start(bf16[27,16,256]{2,1,0:T(8,128)(2,1)S(1)} %collective-permute-done.same_ref), channel_id=1, source_target_pairs={{0,16},{16,0},{32,48},{48,32},{64,80},{80,64},{96,112},{112,96},{1... | collective-permute-start | bytes 663560 | tf_op jit(solution)/shard_map/ppermute | solution.py:268
  20.1 1.1 %collective-permute-done.1.opposite_ref = bf16[27,16,256]{2,1,0:T(8,128)(2,1)S(1)} collective-permute-done((bf16[27,16,256]{2,1,0:T(8,128)(2,1)S(1)}, bf16[27,16,256]{2,1,0:T(8,128)(2,1)S(1)}, u32[]{:S(2)}, u32[]{:S(2)}) %collective-permute-start.1) | collective-permute-done | bytes 221216 | tf_op jit(solution)/shard_map/ppermute | solution.py:268
  21.2 3.5 %all-to-all-done.r_ref = bf16[8,288,256]{2,1,0:T(8,128)(2,1)S(1)} async-done(((bf16[8,288,256]{2,1,0:T(8,128)(2,1)}), bf16[8,288,256]{2,1,0:T(8,128)(2,1)S(1)}, u32[]{:S(2)}, u32[]{:S(2)}) %all-to-all-start) | async-done | bytes 1179680 | tf_op jit(solution)/shard_map/all_to_all | solution.py:285
  24.7 6.0 %shard_map.59 = (bf16[8,288,256]{2,1,0:T(8,128)(2,1)}, f32[432,256]{1,0:T(8,128)S(1)}, bf16[432,256]{1,0:T(8,128)(2,1)S(1)}) custom-call(s32[1]{0:T(128)} %bitcast.1.core_ref, bf16[8,288,256]{2,1,0:T(8,128)(2,1)S(1)} %all-to-all-done.r_ref, bf16[27,16,256]{2,1,0:T(8,128)(2,1)S(1)} %collective-permute-done.same_ref, ...), custom_call_target="tpu_custom_call" | custom-call | flops 2818572288 | bytes 3465220 | tf_op jit(solution)/shard_map/pallas_call | solution.py:233
  30.8 0.0 collective-permute-start.2
  30.8 7.4 %all-to-all-start.1 = ((bf16[8,288,256]{2,1,0:T(8,128)(2,1)}), bf16[8,288,256]{2,1,0:T(8,128)(2,1)S(1)}, u32[]{:S(2)}, u32[]{:S(2)}) async-start(bf16[8,288,256]{2,1,0:T(8,128)(2,1)} %get-tuple-element.8), calls=%async_computation.1 | async-start | bytes 2359296 | tf_op jit(solution)/shard_map/all_to_all | solution.py:303
  38.2 0.0 collective-permute-done.2.got_ref
  38.2 0.1 shard_map.61
  38.3 3.4 %collective-permute-start.3 = (bf16[432,256]{1,0:T(8,128)(2,1)S(1)}, bf16[432,256]{1,0:T(8,128)(2,1)S(1)}, u32[]{:S(2)}, u32[]{:S(2)}) collective-permute-start(bf16[432,256]{1,0:T(8,128)(2,1)S(1)} %shard_map.61), channel_id=1, source_target_pairs={{0,0},{1,1},{2,34},{3,35},{4,68},{5,69},{6,102},{7,103},{8,136},{9... | collective-permute-start | bytes 663560 | tf_op jit(solution)/shard_map/ppermute | solution.py:317
  41.7 4.4 %collective-permute-done.3.rows_ref = bf16[432,256]{1,0:T(8,128)(2,1)S(1)} collective-permute-done((bf16[432,256]{1,0:T(8,128)(2,1)S(1)}, bf16[432,256]{1,0:T(8,128)(2,1)S(1)}, u32[]{:S(2)}, u32[]{:S(2)}) %collective-permute-start.3) | collective-permute-done | bytes 221216 | tf_op jit(solution)/shard_map/ppermute | solution.py:317
  46.1 8.6 %all-to-all-done.1.r_ref.after_ref = bf16[8,288,256]{2,1,0:T(8,128)(2,1)S(1)} async-done(((bf16[8,288,256]{2,1,0:T(8,128)(2,1)}), bf16[8,288,256]{2,1,0:T(8,128)(2,1)S(1)}, u32[]{:S(2)}, u32[]{:S(2)}) %all-to-all-start.1) | async-done | bytes 1179680 | tf_op jit(solution)/shard_map/all_to_all | solution.py:303
  54.7 14.0 %all_to_all.20.parts_ref = bf16[16,32,256]{2,1,0:T(8,128)(2,1)S(1)} all-to-all(bf16[16,32,256]{2,1,0:T(8,128)(2,1)S(1)} %bitcast.11), channel_id=1, replica_groups=mesh['fsdp'=16,'slab'=8,'rep'=2] {'slab','rep'}, dimensions={0} | all-to-all | bytes 524288 | tf_op jit(solution)/shard_map/all_to_all | solution.py:325
  68.6 0.8 shard_map.63
  69.4 4.9 %all-to-all-start.3 = ((bf16[16,32,256]{2,1,0:T(8,128)(2,1)}), bf16[16,32,256]{2,1,0:T(8,128)(2,1)S(1)}, u32[]{:S(2)}, u32[]{:S(2)}) async-start(bf16[16,32,256]{2,1,0:T(8,128)(2,1)} %shard_map.63), calls=%async_computation.3 | async-start | bytes 524288 | tf_op jit(solution)/shard_map/all_to_all | solution.py:329
  74.3 0.9 %shard_map.60 = (bf16[256,256]{1,0:T(8,128)(2,1)}, bf16[256,256]{1,0:T(8,128)(2,1)}) custom-call(s32[1]{0:T(128)} %bitcast.chip_ref, bf16[8,288,256]{2,1,0:T(8,128)(2,1)S(1)} %all-to-all-done.1.r_ref.after_ref), custom_call_target="tpu_custom_call" | custom-call | bytes 1441796 | tf_op jit(solution)/shard_map/pallas_call | solution.py:233
  75.2 6.2 %all-to-all-done.3 = bf16[16,32,256]{2,1,0:T(8,128)(2,1)S(1)} async-done(((bf16[16,32,256]{2,1,0:T(8,128)(2,1)}), bf16[16,32,256]{2,1,0:T(8,128)(2,1)S(1)}, u32[]{:S(2)}, u32[]{:S(2)}) %all-to-all-start.3) | async-done | bytes 262176 | tf_op jit(solution)/shard_map/all_to_all | solution.py:329
  81.4 0.8 multiply_bitcast_fusion
  (1 shorter events, 0.0 us)
Async XLA Ops:
  2.7 6.1 %copy-start = (bf16[16,27,256]{2,0,1:T(8,128)(2,1)S(1)}, bf16[16,27,256]{2,0,1:T(8,128)(2,1)}, u32[]{:S(2)}) copy-start(bf16[16,27,256]{2,0,1:T(8,128)(2,1)} %param.4) | copy-start | bytes 663556
  2.7 22.0 %all-to-all-start = ((bf16[8,288,256]{2,1,0:T(8,128)(2,1)}), bf16[8,288,256]{2,1,0:T(8,128)(2,1)S(1)}, u32[]{:S(2)}, u32[]{:S(2)}) async-start(bf16[8,288,256]{2,1,0:T(8,128)(2,1)} %shard_map.58), calls=%async_computation | async-start | bytes 2359296 | tf_op jit(solution)/shard_map/all_to_all | solution.py:285
  8.8 7.8 %collective-permute-start = (bf16[27,16,256]{2,1,0:T(8,128)(2,1)S(1)}, bf16[27,16,256]{2,1,0:T(8,128)(2,1)S(1)}, u32[]{:S(2)}, u32[]{:S(2)}) collective-permute-start(bf16[27,16,256]{2,1,0:T(8,128)(2,1)S(1)} %bitcast.15), channel_id=1, source_target_pairs={{0,0},{1,1},{2,34},{3,35},{4,68},{5,69},{6,102},{7,103},{8,136},{9... | collective-permute-start | bytes 663560 | tf_op jit(solution)/shard_map/ppermute | solution.py:267
  16.6 4.6 %collective-permute-start.1 = (bf16[27,16,256]{2,1,0:T(8,128)(2,1)S(1)}, bf16[27,16,256]{2,1,0:T(8,128)(2,1)S(1)}, u32[]{:S(2)}, u32[]{:S(2)}) collective-permute-start(bf16[27,16,256]{2,1,0:T(8,128)(2,1)S(1)} %collective-permute-done.same_ref), channel_id=1, source_target_pairs={{0,16},{16,0},{32,48},{48,32},{64,80},{80,64},{96,112},{112,96},{1... | collective-permute-start | bytes 663560 | tf_op jit(solution)/shard_map/ppermute | solution.py:268
  30.8 7.4 %collective-permute-start.2 = (bf16[432,256]{1,0:T(8,128)(2,1)S(1)}, bf16[432,256]{1,0:T(8,128)(2,1)S(1)}, u32[]{:S(2)}, u32[]{:S(2)}) collective-permute-start(bf16[432,256]{1,0:T(8,128)(2,1)S(1)} %get-tuple-element.12), channel_id=1, source_target_pairs={{0,16},{16,0},{32,48},{48,32},{64,80},{80,64},{96,112},{112,96},{1... | collective-permute-start | bytes 663560 | tf_op jit(solution)/shard_map/ppermute | solution.py:314
  30.8 23.9 %all-to-all-start.1 = ((bf16[8,288,256]{2,1,0:T(8,128)(2,1)}), bf16[8,288,256]{2,1,0:T(8,128)(2,1)S(1)}, u32[]{:S(2)}, u32[]{:S(2)}) async-start(bf16[8,288,256]{2,1,0:T(8,128)(2,1)} %get-tuple-element.8), calls=%async_computation.1 | async-start | bytes 2359296 | tf_op jit(solution)/shard_map/all_to_all | solution.py:303
  38.3 7.8 %collective-permute-start.3 = (bf16[432,256]{1,0:T(8,128)(2,1)S(1)}, bf16[432,256]{1,0:T(8,128)(2,1)S(1)}, u32[]{:S(2)}, u32[]{:S(2)}) collective-permute-start(bf16[432,256]{1,0:T(8,128)(2,1)S(1)} %shard_map.61), channel_id=1, source_target_pairs={{0,0},{1,1},{2,34},{3,35},{4,68},{5,69},{6,102},{7,103},{8,136},{9... | collective-permute-start | bytes 663560 | tf_op jit(solution)/shard_map/ppermute | solution.py:317
  69.4 12.0 %all-to-all-start.3 = ((bf16[16,32,256]{2,1,0:T(8,128)(2,1)}), bf16[16,32,256]{2,1,0:T(8,128)(2,1)S(1)}, u32[]{:S(2)}, u32[]{:S(2)}) async-start(bf16[16,32,256]{2,1,0:T(8,128)(2,1)} %shard_map.63), calls=%async_computation.3 | async-start | bytes 524288 | tf_op jit(solution)/shard_map/all_to_all | solution.py:329
